TPU v7x, 128 devices: a whole 4x4x4 slice. The times are simulated.
128 devices in a mesh: feat: 16 (over z, y), grp: 8 (over x, core).
Axes of the slice: x: 4, y: 4, z: 4, core: 2. Of those that a mesh axis runs over, the one named last changes fastest.
Arguments:
- node_table: bfloat16 [8, 32768, 1024], P('grp', None, 'feat'), may hold values from -6 to 6
- node_ids: int32 [8, 32768], P('grp'), may hold values from 0 to 32767, as said below
- block_lists: int32 [8, 128, 3], P('grp'), may hold values from 0 to 255
- block_counts: int32 [8, 128], P('grp'), may hold values from 1 to 3
- tiles: bfloat16 [8, 128, 3, 128, 128], P('grp'), may hold values from 0.049804688 to 1
- batch_sizes: int32 [8], P('grp'), may hold values from 8192 to 16384, as said below
- w_self: bfloat16 [1024, 256], replicated, may hold values from -0.1875 to 0.1875
- w_neigh: bfloat16 [1024, 256], replicated, may hold values from -0.75 to 0.75
- bias: float32 [256], replicated, may hold values from -3 to 3
- cotangent: bfloat16 [8, 16384, 256], P('grp', 'feat'), may hold values from -0.06591797 to 0.06591797
Outputs:
- hidden: bfloat16 [8, 16384, 256], P('grp', 'feat')
- grad_self: float32 [1024, 256], P('feat')
- grad_neigh: float32 [1024, 256], P('feat')
Inputs may be any that keep to these rules, and one draw needn't show every extreme that they name: `batch_sizes`: each group's entry is at least half of 16384; some group has exactly 16384. `node_ids`: each group's entries are a permutation of 0 to 32767 in which every aligned run of 128 entries (starting at a multiple of 128) holds exactly the rows of one aligned 128-row block of the table, in some order.
All inputs are finite; a program needn't handle non-finite values.
Results may differ from a plain program's by a relative error of at most 0.0052.
Values may be sent and summed in bfloat16 or wider, within the bound.
No kernel may reach another device: no remote copies, remote signals or barrier semaphores. Data moves between devices by JAX's collectives and lax.ppermute only.
A program may use at most 128 MiB of HBM per device.

v0:
```python
import jax
import jax.numpy as jnp
from jax import lax
from jax.sharding import PartitionSpec as P


def aggregate(source_rows, lists, counts, tiles):
    block = tiles.shape[-1]
    width = source_rows.shape[1]
    blocks = source_rows.reshape(-1, block, width)
    picked = blocks[lists]
    keeping = jnp.arange(lists.shape[1], dtype=jnp.int32)[None, :] < counts[:, None]
    weights = jnp.where(keeping[:, :, None, None], tiles, jnp.zeros((), tiles.dtype))
    summed = jnp.einsum("bsij,bsjc->bic", weights, picked, preferred_element_type=jnp.float32)
    degree = jnp.sum(weights, axis=(1, 3), dtype=jnp.float32)
    return (summed / degree[:, :, None]).reshape(-1, width).astype(jnp.bfloat16)


def sample_rows(table, ids, block):
    width = table.shape[1]
    id_blocks = ids.reshape(-1, block)
    which = id_blocks[:, 0] // block
    within = id_blocks - which[:, None] * block
    table_blocks = table.reshape(-1, block, width)
    chosen = jnp.take(table_blocks, which, axis=0)
    columns = jnp.arange(block, dtype=jnp.int32)
    selector = (within[:, :, None] == columns[None, None, :]).astype(table.dtype)
    placed = jnp.einsum("bij,bjc->bic", selector, chosen, preferred_element_type=jnp.float32)
    return placed.astype(jnp.bfloat16).reshape(-1, width)


def outer(left, right):
    return lax.dot_general(
        left, right, (((0,), (0,)), ((), ())), preferred_element_type=jnp.float32
    )


def activate(pre, upstream, valid):
    active, back = jax.vjp(jax.nn.gelu, pre)
    hidden = (active * valid).astype(jnp.bfloat16)
    slope = (back(upstream)[0] * valid).astype(jnp.bfloat16)
    return (hidden, slope)


def on_device(
    node_table,
    node_ids,
    block_lists,
    block_counts,
    tiles,
    batch_sizes,
    w_self,
    w_neigh,
    bias,
    cotangent,
):
    table = node_table[0]
    width = table.shape[1]
    gathered = sample_rows(table, node_ids[0], tiles.shape[-1])
    agg_cols = aggregate(gathered, block_lists[0], block_counts[0], tiles[0])
    dst_total = agg_cols.shape[0]
    self_cols = gathered[:dst_total]
    rank = lax.axis_index("feat")
    owned = dst_total // lax.axis_size("feat")
    hidden_units = w_self.shape[1]
    positions = rank * owned + jnp.arange(owned, dtype=jnp.int32)
    valid = (positions < batch_sizes[0]).astype(jnp.float32)[:, None]
    upstream = cotangent[0].astype(jnp.float32)
    self_rows, agg_rows = (
        lax.all_to_all(self_cols, "feat", split_axis=0, concat_axis=1, tiled=True),
        lax.all_to_all(agg_cols, "feat", split_axis=0, concat_axis=1, tiled=True),
    )
    pre = (
        jnp.dot(self_rows, w_self, preferred_element_type=jnp.float32)
        + jnp.dot(agg_rows, w_neigh, preferred_element_type=jnp.float32)
        + bias
    )
    hidden, slope = activate(pre, upstream, valid)
    both = jnp.concatenate([outer(self_rows, slope), outer(agg_rows, slope)], axis=1)
    summed = lax.psum(both, ("feat", "grp"))
    mine = lax.dynamic_slice_in_dim(summed, rank * width, width, 0)
    return (hidden[None], mine[:, :hidden_units], mine[:, hidden_units:])


def solution(mesh):
    in_specs = (
        P("grp", None, "feat"),
        P("grp", None),
        P("grp", None, None),
        P("grp", None),
        P("grp", None, None, None, None),
        P("grp"),
        P(),
        P(),
        P(),
        P("grp", "feat", None),
    )
    out_specs = (P("grp", "feat", None), P("feat", None), P("feat", None))
    return jax.shard_map(
        on_device, mesh=mesh, in_specs=in_specs, out_specs=out_specs, check_vma=False
    )
```

profile of v0, /device:TPU:1, one launch (start us, length us, event | category | flops | bytes accessed | tf_op | source)
XLA Modules:
  0.0 288.8 jit_solution(18229090564325638348)
XLA Ops:
  7.2 1.0 copy.42
  8.3 3.3 %copy.43 = bf16[8,8,256,128]{3,2,1,0:T(8,128)(2,1)S(1)} copy(bf16[8,8,256,128]{3,1,2,0:T(8,128)(2,1)} %bitcast.57) | data formatting | bytes 8388608
  11.6 4.6 %copy.33 = bf16[256,128,64]{1,2,0:T(8,128)(2,1)} copy(bf16[256,128,64]{1,0,2:T(8,128)(2,1)S(1)} %bitcast.54) | data formatting | bytes 8388608 | tf_op jit(solution)/shard_map/reshape;squeeze | solution.py:24
  16.4 5.3 %gather_fusion = bf16[256,128,64]{1,2,0:T(8,128)(2,1)} fusion(bf16[256,128,64]{1,2,0:T(8,128)(2,1)} %copy.33, s32[1024]{0:T(1024)S(1)} %pad_clamp_fusion.1), kind=kCustom, calls=%fused_computation | custom fusion | bytes 8389632 | tf_op jit(solution)/shard_map/jit(_take)/gather | solution.py:25
  21.6 8.9 %fusion.7 = bf16[256,128,64]{1,2,0:T(8,128)(2,1)S(1)} fusion(bf16[256,128,64]{1,2,0:T(8,128)(2,1)} %gather_fusion, pred[256]{0:T(512)(128)(4,1)S(1)} %get-tuple-element.17, s32[256,128]{1,0:T(8,128)S(1)} %broadcast_subtract_fusion), kind=kOutput, calls=%fused_computation.13 | convolution fusion | flops 545259520 | bytes 8519936 | tf_op jit(solution)/shard_map/bij,bjc->bic/dot_general | solution.py:28
  30.6 2.0 copy-done.1
  32.8 1.4 copy.34
  34.2 2.3 all_to_all.26
  36.5 4.1 %copy.35 = bf16[16,1024,64]{1,2,0:T(8,128)(2,1)} copy(bf16[16,1024,64]{1,0,2:T(8,128)(2,1)} %all_to_all.26) | data formatting | bytes 4194304 | tf_op jit(solution)/shard_map/all_to_all | solution.py:70
  40.5 8.6 %all-to-all-start = ((bf16[16,1024,64]{1,2,0:T(8,128)(2,1)}), bf16[16,1024,64]{1,2,0:T(8,128)(2,1)S(1)}, u32[]{:S(2)}, u32[]{:S(2)}) async-start(bf16[16,1024,64]{1,2,0:T(8,128)(2,1)} %copy.35), calls=%async_computation | async-start | bytes 4194304 | tf_op jit(solution)/shard_map/all_to_all | solution.py:70
  49.3 8.0 %convert_reduce_fusion = f32[128,128]{1,0:T(8,128)S(1)} fusion(bf16[1,128,3,128,128]{4,3,2,1,0:T(8,128)(2,1)} %param.14, pred[128,3]{1,0:T(8,128)(4,1)S(1)} %iota_compare_fusion.4), kind=kLoop, calls=%fused_computation.2 | loop fusion | flops 18857984 | bytes 12648832 | tf_op jit(solution)/shard_map/reduce_sum | solution.py:15
  57.7 6.2 %gather_fusion.1 = bf16[384,128,64]{1,2,0:T(8,128)(2,1)} fusion(bf16[256,128,64]{1,2,0:T(8,128)(2,1)} %copy-done.1, s32[1024]{0:T(1024)S(1)} %pad_clamp_fusion), kind=kCustom, calls=%fused_computation.1 | custom fusion | bytes 12584448 | tf_op jit(solution)/shard_map/gather | solution.py:11
  63.9 9.6 %fusion.4 = bf16[128,128,64]{1,2,0:T(8,128)(2,1)S(1)} fusion(bf16[128,3,128,64]{2,3,1,0:T(8,128)(2,1)} %bitcast.53, bf16[1,128,3,128,128]{4,3,2,1,0:T(8,128)(2,1)} %param.14, pred[128,3]{1,0:T(8,128)(4,1)S(1)} %iota_compare_fusion.4, f32[128,128]{1,0:T(8,128)S(1)} %convert_reduce_fusion), kind=kOutput, calls=%fused_computation.10 | convolution fusion | flops 813694976 | bytes 21037440 | tf_op jit(solution)/shard_map/bsij,bsjc->bic/dot_general | solution.py:14
  73.5 2.7 copy.37
  76.2 4.2 %convert_element_type.36 = bf16[16,1024,64]{1,0,2:T(8,128)(2,1)} reshape(bf16[128,128,64]{1,0,2:T(8,128)(2,1)} %copy.37) | data formatting | bytes 4194304 | tf_op jit(solution)/shard_map/convert_element_type | solution.py:16
  80.3 4.1 %copy.38 = bf16[16,1024,64]{1,2,0:T(8,128)(2,1)} copy(bf16[16,1024,64]{1,0,2:T(8,128)(2,1)} %convert_element_type.36) | data formatting | bytes 4194304 | tf_op jit(solution)/shard_map/convert_element_type | solution.py:16
  84.5 6.8 %all-to-all-start.1 = ((bf16[16,1024,64]{1,2,0:T(8,128)(2,1)}), bf16[16,1024,64]{1,2,0:T(8,128)(2,1)}, u32[]{:S(2)}, u32[]{:S(2)}) async-start(bf16[16,1024,64]{1,2,0:T(8,128)(2,1)} %copy.38), calls=%async_computation.1 | async-start | bytes 4194304 | tf_op jit(solution)/shard_map/all_to_all | solution.py:71
  92.2 1.7 fusion.28
  94.0 26.1 %all-to-all-done.1 = bf16[16,1024,64]{1,2,0:T(8,128)(2,1)} async-done(((bf16[16,1024,64]{1,2,0:T(8,128)(2,1)}), bf16[16,1024,64]{1,2,0:T(8,128)(2,1)}, u32[]{:S(2)}, u32[]{:S(2)}) %all-to-all-start.1) | async-done | bytes 2097184 | tf_op jit(solution)/shard_map/all_to_all | solution.py:71
  120.1 4.3 %fusion.15 = (bf16[1024,256]{1,0:T(8,128)(2,1)S(1)}, bf16[1,1024,256]{2,1,0:T(8,128)(2,1)}) fusion(bf16[1,1024,256]{2,1,0:T(8,128)(2,1)} %param.19, f32[1024]{0:T(1024)S(1)} %fusion.24, f32[256]{0:T(256)S(1)} %copy-done.6, f32[1024,256]{1,0:T(8,128)} %fusion.28, bf16[1024,1024]{0,1:T(8,128)(2,1)} %bitcast.12, bf16[1024,256]{1,0:T(8,128)(2,1)S(1)} %copy-done), kind=kOutput, calls=%fused_computation.25 | convolution fusion | flops 543948800 | bytes 5248000 | tf_op jit(solution)/shard_map/dot_general | solution.py:75
  124.4 2.3 fusion.30
  127.6 1.5 pad_maximum_fusion
  129.0 150.4 %all-reduce.2.cloned.1.call-done = f32[1024,512]{0,1:T(8,128)} async-done(((f32[1024,512]{0,1:T(8,128)}), f32[1024,512]{0,1:T(8,128)}) %all-reduce.2.cloned.1.call-update) | async-done | bytes 2097168 | tf_op jit(solution)/shard_map/psum | solution.py:80
  279.4 1.1 fusion.27
  (30 shorter events, 3.2 us)
Async XLA Ops:
  7.2 113.0 %copy-start = (bf16[1024,256]{1,0:T(8,128)(2,1)S(1)}, bf16[1024,256]{1,0:T(8,128)(2,1)}, u32[]{:S(2)}) copy-start(bf16[1024,256]{1,0:T(8,128)(2,1)} %param.17) | copy-start | bytes 1572868
  11.6 4.7 %copy-start.2 = (s32[1,32768]{1,0:T(1,128)S(1)}, s32[1,32768]{1,0:T(1,128)}, u32[]{:S(2)}) copy-start(s32[1,32768]{1,0:T(1,128)} %param.11) | copy-start | bytes 393220
  30.6 2.0 copy-start.1
  36.4 12.7 %copy-start.4 = (s32[1,128]{1,0:T(1,128)S(1)}, s32[1,128]{1,0:T(1,128)}, u32[]{:S(2)}) copy-start(s32[1,128]{1,0:T(1,128)} %param.13) | copy-start | bytes 1540
  40.5 43.9 %all-to-all-start = ((bf16[16,1024,64]{1,2,0:T(8,128)(2,1)}), bf16[16,1024,64]{1,2,0:T(8,128)(2,1)S(1)}, u32[]{:S(2)}, u32[]{:S(2)}) async-start(bf16[16,1024,64]{1,2,0:T(8,128)(2,1)} %copy.35), calls=%async_computation | async-start | bytes 4194304 | tf_op jit(solution)/shard_map/all_to_all | solution.py:70
  49.3 8.0 %copy-start.3 = (s32[1,128,3]{1,0,2:T(1,128)S(1)}, s32[1,128,3]{1,0,2:T(1,128)}, u32[]{:S(2)}) copy-start(s32[1,128,3]{1,0,2:T(1,128)} %param.12) | copy-start | bytes 4612
  80.3 11.9 %copy-start.5 = (bf16[1024,256]{1,0:T(8,128)(2,1)S(1)}, bf16[1024,256]{1,0:T(8,128)(2,1)}, u32[]{:S(2)}) copy-start(bf16[1024,256]{1,0:T(8,128)(2,1)} %param.16) | copy-start | bytes 1572868
  84.5 35.7 %copy-start.6 = (f32[256]{0:T(256)S(1)}, f32[256]{0:T(256)}, u32[]{:S(2)}) copy-start(f32[256]{0:T(256)} %param.18) | copy-start | bytes 3076
  84.5 35.6 %all-to-all-start.1 = ((bf16[16,1024,64]{1,2,0:T(8,128)(2,1)}), bf16[16,1024,64]{1,2,0:T(8,128)(2,1)}, u32[]{:S(2)}, u32[]{:S(2)}) async-start(bf16[16,1024,64]{1,2,0:T(8,128)(2,1)} %copy.38), calls=%async_computation.1 | async-start | bytes 4194304 | tf_op jit(solution)/shard_map/all_to_all | solution.py:71
  91.3 188.1 %all-reduce.2.cloned.1.call-start = ((), (), s32[]{:S(2)}) async-start(), calls=%async_computation.2 | async-start | bytes 4194304 | tf_op jit(solution)/shard_map/psum | solution.py:80
Sparse Core Ops, SparseCore 0:
  129.2 150.2 all-reduce.1
where the time goes:
time: 290 us; the launch traced here: 289 us
  waiting for transfers between devices  177 us (61%)
  local copies, waits for them, and re-layouts  44.3 us (15%)
  matrix products  27.7 us (10%)
  starting transfers between devices  15.7 us (5%)
  between operations  14.9 us (5%)
  other arithmetic  9.72 us (3%)
    psum x1, waiting for transfers between devices, on_device(): summed = lax.psum(both, ('feat', 'grp'))  150 us
    all_to_all x1, waiting for transfers between devices, on_device(): lax.all_to_all(agg_cols, 'feat', split_axis=0, concat_axis=1, tiled=True)  26.1 us
    convert_element_type x3, local copies, waits for them, and re-layouts, aggregate(): return (summed / degree[:, :, None]).reshape(-1, width).astype(jnp.bfloat16)  11 us
    dot_general x1, matrix products, aggregate(): jnp.einsum('bsij,bsjc->bic', weights, picked, preferred_element_type=jnp....  9.58 us
    dot_general x1, matrix products, sample_rows(): jnp.einsum('bij,bjc->bic', selector, chosen, preferred_element_type=jnp.f...  8.94 us
    all_to_all x1, starting transfers between devices, on_device(): lax.all_to_all(self_cols, 'feat', split_axis=0, concat_axis=1, tiled=True)  8.61 us
    reduce_sum x1, other arithmetic, aggregate(): degree = jnp.sum(weights, axis=(1, 3), dtype=jnp.float32)  8.02 us
    unnamed x18, local copies, waits for them, and re-layouts  7.86 us
  transfers between devices with their start and end apart: 3, of which 2 were waited for; matrix products, arithmetic and copies ran while one was open for 13% of the time, Pallas kernels for 0%

commit v1 on v0

v1 whole, which is shorter than its diff:
```python
import jax
import jax.numpy as jnp
from jax import lax
from jax.experimental import pallas as pl
from jax.experimental.pallas import tpu as pltpu
from jax.sharding import Mesh, PartitionSpec as P

BLOCK = 128
MIB = 1 << 20
FEAT = ("z", "y")
GRP = ("x", "core")
NT = (((1,), (1,)), ((), ()))
NN = (((1,), (0,)), ((), ()))


def dot(left, right, dims=NN):
    return lax.dot_general(left, right, dims, preferred_element_type=jnp.float32)


def selector(within):
    rows = lax.broadcasted_iota(jnp.int32, (BLOCK, BLOCK), 0)
    return jnp.where(rows == within, 1.0, 0.0).astype(jnp.bfloat16)


def pick_kernel(which_ref, table_ref, out_ref, sem):
    owners, _, owned = out_ref.shape
    per = owned // BLOCK

    def start(b, carry):
        w = which_ref[b]
        pltpu.make_async_copy(
            table_ref.at[:, pl.ds(pl.multiple_of(w * BLOCK, BLOCK), BLOCK)],
            out_ref.at[b // per, :, pl.ds(pl.multiple_of((b % per) * BLOCK, BLOCK), BLOCK)],
            sem,
        ).start()
        return carry

    lax.fori_loop(0, owners * per, start, 0)
    pltpu.make_async_copy(out_ref, out_ref, sem).wait()


def pick(which, table, owners):
    width, rows = table.shape
    owned = rows // 2 // owners
    return pl.pallas_call(
        pick_kernel,
        out_shape=jax.ShapeDtypeStruct((owners, width, owned), table.dtype),
        in_specs=[pl.BlockSpec(memory_space=pltpu.SMEM), pl.BlockSpec(memory_space=pl.ANY)],
        out_specs=pl.BlockSpec(memory_space=pl.ANY),
        scratch_shapes=[pltpu.SemaphoreType.DMA],
        cost_estimate=pl.CostEstimate(flops=0, bytes_accessed=4 * MIB, transcendentals=0),
        name="pick_own_blocks",
    )(which, table)


def aggregate_kernel(which_ref, lists_ref, counts_ref, ids_ref, table_ref, tiles_ref, out_ref, source):
    step = pl.program_id(0)
    blocks = ids_ref.shape[0]
    width = table_ref.shape[0]
    per, slots = tiles_ref.shape[0], tiles_ref.shape[1]

    @pl.when(step == 0)
    def _():
        source[blocks] = jnp.zeros(source.shape[1:], source.dtype)

        def place(n, carry):
            w = which_ref[n]
            chosen = table_ref[:, pl.ds(pl.multiple_of(w * BLOCK, BLOCK), BLOCK)]
            within = ids_ref[pl.ds(n, 1), :] - w * BLOCK
            source[n, :width] = dot(chosen, selector(within)).astype(jnp.bfloat16)
            source[n, width:] = jnp.ones((source.shape[1] - width, BLOCK), jnp.bfloat16)
            return carry

        lax.fori_loop(0, blocks, place, 0, unroll=4)

    for b in range(per):
        d = step * per + b
        count = counts_ref[d]
        left = jnp.concatenate(
            [source[jnp.where(s < count, lists_ref[d * slots + s], blocks)] for s in range(slots)], axis=1
        )
        right = jnp.concatenate([tiles_ref[b, s] for s in range(slots)], axis=1)
        total = dot(left, right, NT)
        out_ref[0, :, b * BLOCK : (b + 1) * BLOCK] = (total[:width] / total[width : width + 1]).astype(jnp.bfloat16)


def aggregate(which, lists, counts, ids, table, tiles, owners):
    width, rows = table.shape
    blocks = rows // BLOCK
    dst_blocks, slots = tiles.shape[0], tiles.shape[1]
    per = dst_blocks // owners
    return pl.pallas_call(
        aggregate_kernel,
        grid_spec=pltpu.PrefetchScalarGridSpec(
            num_scalar_prefetch=3,
            grid=(owners,),
            in_specs=[
                pl.BlockSpec(memory_space=pltpu.VMEM),
                pl.BlockSpec(memory_space=pltpu.VMEM),
                pl.BlockSpec((per, slots, BLOCK, BLOCK), lambda r, *_: (r, 0, 0, 0)),
            ],
            out_specs=pl.BlockSpec((1, width, per * BLOCK), lambda r, *_: (r, 0, 0)),
            scratch_shapes=[pltpu.VMEM((blocks + 1, width + 16, BLOCK), jnp.bfloat16)],
        ),
        out_shape=jax.ShapeDtypeStruct((owners, width, per * BLOCK), jnp.bfloat16),
        compiler_params=pltpu.CompilerParams(vmem_limit_bytes=32 * MIB),
        cost_estimate=pl.CostEstimate(flops=4_000_000_000, bytes_accessed=20 * MIB, transcendentals=0),
        name="aggregate",
    )(which, lists, counts, ids, table, tiles)


def own_kernel(first_ref, ids_ref, moved_ref, weight_ref, bias_ref, own_ref, pre_ref):
    step = pl.program_id(0)
    per = own_ref.shape[1] // BLOCK
    for b in range(per):
        row = first_ref[0] + step * per + b
        within = jnp.bitwise_and(ids_ref[pl.ds(row, 1), :], BLOCK - 1)
        columns = slice(b * BLOCK, (b + 1) * BLOCK)
        own_ref[:, columns] = dot(moved_ref[:, columns], selector(within)).astype(jnp.bfloat16)
    pre_ref[...] = dot(weight_ref[...], own_ref[...]) + bias_ref[...]


def own_part(first, ids, moved, weight, bias):
    features, owned = moved.shape
    hidden = weight.shape[0]
    wide = 2 * BLOCK
    return pl.pallas_call(
        own_kernel,
        grid=(owned // wide,),
        in_specs=[
            pl.BlockSpec(memory_space=pltpu.SMEM),
            pl.BlockSpec(memory_space=pltpu.VMEM),
            pl.BlockSpec((features, wide), lambda i: (0, i)),
            pl.BlockSpec(memory_space=pltpu.VMEM),
            pl.BlockSpec(memory_space=pltpu.VMEM),
        ],
        out_specs=[
            pl.BlockSpec((features, wide), lambda i: (0, i)),
            pl.BlockSpec((hidden, wide), lambda i: (0, i)),
        ],
        out_shape=[
            jax.ShapeDtypeStruct((features, owned), jnp.bfloat16),
            jax.ShapeDtypeStruct((hidden, owned), jnp.float32),
        ],
        compiler_params=pltpu.CompilerParams(vmem_limit_bytes=24 * MIB),
        cost_estimate=pl.CostEstimate(flops=2_000_000_000, bytes_accessed=6 * MIB, transcendentals=0),
        name="own_part",
    )(first, ids, moved, weight, bias)


def gelu_and_slope(pre):
    c, k = 0.7978845608028654, 0.044715
    square = pre * pre
    t = jnp.tanh(c * pre * (1.0 + k * square))
    half = 0.5 * (1.0 + t)
    slope = half + 0.5 * pre * (1.0 - t * t) * (c * (1.0 + 3.0 * k * square))
    return pre * half, slope


def finish_kernel(
    place_ref, pre_ref, agg_ref, own_ref, weight_ref, upstream_ref, hidden_ref, keep_ref, send_ref, slope
):
    owned = pre_ref.shape[1]
    wide = 2 * BLOCK
    limit, core = place_ref[0], place_ref[1]
    for j in range(owned // wide):
        columns = slice(j * wide, (j + 1) * wide)
        pre = pre_ref[:, columns] + dot(weight_ref[...], agg_ref[:, columns])
        active, back = gelu_and_slope(pre)
        positions = j * wide + lax.broadcasted_iota(jnp.int32, (1, wide), 1)
        valid = jnp.where(positions < limit, 1.0, 0.0)
        hidden_ref[:, columns] = (active * valid).astype(jnp.bfloat16)
        slope[:, columns] = (upstream_ref[:, columns].astype(jnp.float32) * back * valid).astype(jnp.bfloat16)

    owners, share, _ = keep_ref.shape

    def grads(left_ref, out_ref):
        group = 4

        def part(i, carry):
            left = left_ref[pl.ds(pl.multiple_of(i * group * share, group * share), group * share), :]
            out_ref[pl.ds(i * group, group)] = dot(left, slope[...], NT).reshape(group, share, -1)
            return carry

        lax.fori_loop(0, owners // group, part, 0)

    @pl.when(core == 0)
    def _():
        grads(own_ref, keep_ref)
        grads(agg_ref, send_ref)

    @pl.when(core != 0)
    def _():
        grads(own_ref, send_ref)
        grads(agg_ref, keep_ref)


def finish(place, pre, agg, own, weight, upstream, owners):
    hidden, owned = pre.shape
    features = agg.shape[0]
    part = jax.ShapeDtypeStruct((owners, features // owners, hidden), jnp.float32)
    vmem = pl.BlockSpec(memory_space=pltpu.VMEM)
    return pl.pallas_call(
        finish_kernel,
        in_specs=[pl.BlockSpec(memory_space=pltpu.SMEM)] + [vmem] * 5,
        out_specs=[vmem] * 3,
        out_shape=[jax.ShapeDtypeStruct((hidden, owned), jnp.bfloat16), part, part],
        scratch_shapes=[pltpu.VMEM((hidden, owned), jnp.bfloat16)],
        compiler_params=pltpu.CompilerParams(vmem_limit_bytes=32 * MIB),
        cost_estimate=pl.CostEstimate(flops=2_000_000_000, bytes_accessed=9 * MIB, transcendentals=262144),
        name="finish",
    )(place, pre, agg, own, weight, upstream)


def on_device(
    node_table, node_ids, block_lists, block_counts, tiles, batch_sizes, w_self, w_neigh, bias, cotangent
):
    owners = lax.axis_size(FEAT)
    rank, core = lax.axis_index(FEAT), lax.axis_index("core")
    table = jnp.swapaxes(node_table[0], 0, 1)
    width = table.shape[0]
    ids = node_ids[0].reshape(-1, BLOCK)
    which = lax.shift_right_logical(ids[:, 0], 7)
    owned = cotangent.shape[1]

    mine = pick(which, table, owners)
    moved = lax.all_to_all(mine, FEAT, split_axis=0, concat_axis=0, tiled=True)
    aggregated = aggregate(which, block_lists[0].reshape(-1), block_counts[0], ids, table, tiles[0], owners)
    agg = lax.all_to_all(aggregated, FEAT, split_axis=0, concat_axis=0, tiled=True).reshape(-1, owned)

    first = (rank * (owned // BLOCK)).reshape(1)
    own, pre = own_part(first, ids, moved.reshape(-1, owned), w_self.T, bias[:, None])
    place = jnp.stack([batch_sizes[0] - rank * owned, core])
    hidden, keep, send = finish(place, pre, agg, own, w_neigh.T, cotangent[0].T, owners)

    got = lax.ppermute(send, "core", [(0, 1), (1, 0)])
    parts = lax.all_to_all(keep + got, FEAT, split_axis=0, concat_axis=0, tiled=True)
    total = jnp.sum(parts, axis=0)
    others = [lax.ppermute(total, "x", [(i, i ^ k) for i in range(4)]) for k in (1, 2, 3)]
    total = (total + others[0]) + (others[1] + others[2])
    other = lax.ppermute(total, "core", [(0, 1), (1, 0)])
    first_core = core == 0
    return (
        hidden.T[None],
        jnp.where(first_core, total, other),
        jnp.where(first_core, other, total),
    )


def solution(mesh):
    axes = Mesh(mesh.devices.reshape(4, 4, 4, 2), ("z", "y", "x", "core"))
    in_specs = (
        P(GRP, None, FEAT),
        P(GRP, None),
        P(GRP, None, None),
        P(GRP, None),
        P(GRP, None, None, None, None),
        P(GRP),
        P(),
        P(),
        P(),
        P(GRP, FEAT, None),
    )
    out_specs = (P(GRP, FEAT, None), P(FEAT, None), P(FEAT, None))
    return jax.shard_map(on_device, mesh=axes, in_specs=in_specs, out_specs=out_specs, check_vma=False)
```

time: 290 us -> 189 us (0.65)
  waiting for transfers between devices: 177 us -> 27.4 us
  Pallas kernels: 0 us -> 96 us
  matrix products: 27.7 us -> 0 us
  local copies, waits for them, and re-layouts: 44.3 us -> 17.9 us
  blocking collectives: 0 us -> 19 us
  between operations: 14.9 us -> 1.48 us
  starting transfers between devices: 15.7 us -> 23.8 us
  other arithmetic: 9.72 us -> 2.55 us
    psum x1 -> x0, waiting for transfers between devices: 150 us -> none  [on_device(): summed = lax.psum(both, ('feat', 'grp'))]
    pallas_call x0 -> x4, Pallas kernels: none -> 96 us  [the longest x1 65.3 us: pick(): pl.pallas_call(pick_kernel, out_shape=jax.ShapeDtypeStruct((owners, width...]
    dot_general x6 -> x0, matrix products: 27.7 us -> none  [the longest x1 9.58 us: aggregate(): jnp.einsum('bsij,bsjc->bic', weights, picked, preferred_element_type=jnp....]
    all_to_all x0 -> x1, blocking collectives: none -> 19 us  [on_device(): lax.all_to_all(keep + got, FEAT, split_axis=0, concat_axis=0, tiled=True)]
    gather x2 -> x0, local copies, waits for them, and re-layouts: 11.5 us -> none  [the longest x1 6.22 us: aggregate(): picked = blocks[lists]]
    convert_element_type x3 -> x0, local copies, waits for them, and re-layouts: 11 us -> none  [aggregate(): return (summed / degree[:, :, None]).reshape(-1, width).astype(jnp.bfloat16)]
    ppermute x0 -> x5, starting transfers between devices: none -> 10.1 us  [the longest x3 3.94 us: on_device(): lax.ppermute(total, 'x', [(i, i ^ k) for i in range(4)])]
    unnamed x18 -> x31, local copies, waits for them, and re-layouts: 7.86 us -> 17.6 us
  transfers between devices with their start and end apart: 3 -> 7, of which waited for: 2 -> 5; matrix products, arithmetic and copies ran while one was open for 13% -> 3% of each run, Pallas kernels for 0% -> 13%
where the time goes in v1:
time: 189 us; the launch traced here: 188 us
  Pallas kernels  96 us (51%)
  waiting for transfers between devices  27.4 us (14%)
  starting transfers between devices  23.8 us (13%)
  blocking collectives  19 us (10%)
  local copies, waits for them, and re-layouts  17.9 us (9%)
  other arithmetic  2.55 us (1%)
    pallas_call x1, Pallas kernels, pick(): pl.pallas_call(pick_kernel, out_shape=jax.ShapeDtypeStruct((owners, width...  65.3 us
    pallas_call x1, Pallas kernels, aggregate(): pl.pallas_call(aggregate_kernel, grid_spec=pltpu.PrefetchScalarGridSpec(n...  21.4 us
    all_to_all x1, blocking collectives, on_device(): lax.all_to_all(keep + got, FEAT, split_axis=0, concat_axis=0, tiled=True)  19 us
    all_to_all x1, waiting for transfers between devices, on_device(): lax.all_to_all(aggregated, FEAT, split_axis=0, concat_axis=0, tiled=True)  18.3 us
    unnamed x31, local copies, waits for them, and re-layouts  17.6 us
    all_to_all x1, starting transfers between devices, on_device(): moved = lax.all_to_all(mine, FEAT, split_axis=0, concat_axis=0, tiled=True)  8.74 us
    pallas_call x1, Pallas kernels, finish(): pl.pallas_call(finish_kernel, in_specs=[pl.BlockSpec(memory_space=pltpu.S...  5.73 us
    all_to_all x1, starting transfers between devices, on_device(): lax.all_to_all(aggregated, FEAT, split_axis=0, concat_axis=0, tiled=True)  4.92 us
  transfers between devices with their start and end apart: 7, of which 5 were waited for; matrix products, arithmetic and copies ran while one was open for 3% of the time, Pallas kernels for 13%

profile of v1, /device:TPU:1, one launch (start us, length us, event | category | flops | bytes accessed | tf_op | source)
XLA Modules:
  0.0 188.0 jit_solution(11342788518128124429)
XLA Ops:
  0.6 1.6 fusion.which_ref
  2.2 65.3 %pick_own_blocks.1 = bf16[16,64,1024]{2,1,0:T(8,128)(2,1)} custom-call(s32[256]{0:T(256)} %fusion.which_ref, bf16[64,32768]{1,0:T(8,128)(2,1)} %bitcast.22), custom_call_target="tpu_custom_call" | custom-call | bytes 4194304 | tf_op jit(solution)/shard_map/pick_own_blocks/pallas_call | solution.py:45
  67.6 8.7 %all-to-all-start = ((bf16[16,64,1024]{2,1,0:T(8,128)(2,1)}), bf16[16,64,1024]{2,1,0:T(8,128)(2,1)S(1)}, u32[]{:S(2)}, u32[]{:S(2)}) async-start(bf16[16,64,1024]{2,1,0:T(8,128)(2,1)} %pick_own_blocks.1), calls=%async_computation | async-start | bytes 4194304 | tf_op jit(solution)/shard_map/all_to_all | solution.py:227
  76.7 2.2 %copy-done = bf16[1,32768,64]{1,2,0:T(8,128)(2,1)S(1)} copy-done((bf16[1,32768,64]{1,2,0:T(8,128)(2,1)S(1)}, bf16[1,32768,64]{1,2,0:T(8,128)(2,1)}, u32[]{:S(2)}) %copy-start) | copy-done | bytes 4194328
  78.9 4.6 %copy-done.1 = bf16[1,128,3,128,128]{4,3,2,1,0:T(8,128)(2,1)S(1)} copy-done((bf16[1,128,3,128,128]{4,3,2,1,0:T(8,128)(2,1)S(1)}, bf16[1,128,3,128,128]{4,3,2,1,0:T(8,128)(2,1)}, u32[]{:S(2)}) %copy-start.1) | copy-done | bytes 12582936
  83.5 21.4 %aggregate.1 = bf16[16,64,1024]{2,1,0:T(8,128)(2,1)} custom-call(s32[256]{0:T(256)S(1)} %copy-done.4, s32[384]{0:T(512)S(1)} %reshape_squeeze.7.lists_ref, s32[128]{0:T(128)S(1)} %bitcast.33, s32[256,128]{1,0:T(8,128)S(1)} %bitcast.27, bf16[64,32768]{1,0:T(8,128)(2,1)S(1)} %bitcast.23, bf16[128,3,128,128]{3,2,1,0:T(8,128)(2,1)S(1)} %bitcast.24), custom_call_target="tpu_custom_call" | custom-call | flops 4000000000 | bytes 20971520 | tf_op jit(solution)/shard_map/aggregate/pallas_call | solution.py:92
  104.9 1.9 %all-to-all-done = bf16[16,64,1024]{2,1,0:T(8,128)(2,1)S(1)} async-done(((bf16[16,64,1024]{2,1,0:T(8,128)(2,1)}), bf16[16,64,1024]{2,1,0:T(8,128)(2,1)S(1)}, u32[]{:S(2)}, u32[]{:S(2)}) %all-to-all-start) | async-done | bytes 2097184 | tf_op jit(solution)/shard_map/all_to_all | solution.py:227
  106.8 4.9 %all-to-all-start.1 = ((bf16[16,64,1024]{2,1,0:T(8,128)(2,1)}), bf16[16,64,1024]{2,1,0:T(8,128)(2,1)}, u32[]{:S(2)}, u32[]{:S(2)}) async-start(bf16[16,64,1024]{2,1,0:T(8,128)(2,1)} %aggregate.1), calls=%async_computation.1 | async-start | bytes 4194304 | tf_op jit(solution)/shard_map/all_to_all | solution.py:229
  112.8 1.2 copy.20
  114.1 2.0 %copy.21 = bf16[1,1024,256]{1,2,0:T(8,128)(2,1)} copy(bf16[1,1024,256]{2,1,0:T(8,128)(2,1)} %param.19) | data formatting | bytes 1048576 | tf_op args[9]
  116.2 3.5 %own_part.1 = (bf16[1024,1024]{1,0:T(8,128)(2,1)S(1)}, f32[256,1024]{1,0:T(8,128)S(1)}) custom-call(s32[1]{0:T(128)} %bitcast.3.first_ref, s32[256,128]{1,0:T(8,128)S(1)} %bitcast.28, bf16[1024,1024]{1,0:T(8,128)(2,1)S(1)} %bitcast.25, bf16[256,1024]{1,0:T(8,128)(2,1)S(1)} %bitcast.30, f32[256,1]{1,0:T(8,128)S(1)} %copy.18.bias_ref), custom_call_target="tpu_custom_call" | custom-call | flops 2000000000 | bytes 6291456 | tf_op jit(solution)/shard_map/own_part/pallas_call | solution.py:127
  119.7 1.3 copy-done.6
  122.0 18.3 %all-to-all-done.1 = bf16[16,64,1024]{2,1,0:T(8,128)(2,1)} async-done(((bf16[16,64,1024]{2,1,0:T(8,128)(2,1)}), bf16[16,64,1024]{2,1,0:T(8,128)(2,1)}, u32[]{:S(2)}, u32[]{:S(2)}) %all-to-all-start.1) | async-done | bytes 2097184 | tf_op jit(solution)/shard_map/all_to_all | solution.py:229
  141.4 1.6 copy-done.7
  143.0 1.2 copy-done.9
  144.2 5.7 %finish.1 = (bf16[256,1024]{1,0:T(8,128)(2,1)S(1)}, f32[16,64,256]{2,1,0:T(8,128)S(1)}, f32[16,64,256]{2,1,0:T(8,128)S(1)}) custom-call(s32[2]{0:T(128)S(1)} %pad_add_fusion.place_ref, f32[256,1024]{1,0:T(8,128)S(1)} %copy-done.9, bf16[1024,1024]{1,0:T(8,128)(2,1)} %bitcast.13.agg_ref, bf16[1024,1024]{1,0:T(8,128)(2,1)S(1)} %copy-done.7, ...), custom_call_target="tpu_custom_call" | custom-call | flops 2000000000 | bytes 9437184 | tf_op jit(solution)/shard_map/finish/pallas_call | solution.py:203
  149.9 3.4 %collective-permute-start = (f32[16,64,256]{2,1,0:T(8,128)S(1)}, f32[16,64,256]{2,1,0:T(8,128)S(1)}, u32[]{:S(2)}, u32[]{:S(2)}) collective-permute-start(f32[16,64,256]{2,1,0:T(8,128)S(1)} %get-tuple-element.12), channel_id=1, source_target_pairs={{0,1},{1,0},{2,3},{3,2},{4,5},{5,4},{6,7},{7,6},{8,9},{9,8},{10,11... | collective-permute-start | bytes 3145736 | tf_op jit(solution)/shard_map/ppermute | solution.py:236
  153.3 2.3 %collective-permute-done = f32[16,64,256]{2,1,0:T(8,128)S(1)} collective-permute-done((f32[16,64,256]{2,1,0:T(8,128)S(1)}, f32[16,64,256]{2,1,0:T(8,128)S(1)}, u32[]{:S(2)}, u32[]{:S(2)}) %collective-permute-start) | collective-permute-done | bytes 1048608 | tf_op jit(solution)/shard_map/ppermute | solution.py:236
  155.7 19.0 %all_to_all.15 = f32[16,64,256]{2,1,0:T(8,128)S(1)} all-to-all(f32[16,64,256]{2,1,0:T(8,128)S(1)} %add.16), channel_id=1, replica_groups=mesh['z'=4,'y'=4,'x'=4,'core'=2] {'z','y'}, dimensions={0} | all-to-all | bytes 2097152 | tf_op jit(solution)/shard_map/all_to_all | solution.py:237
  174.7 1.3 collective-permute-start.1
  176.0 2.5 %collective-permute-start.2 = (f32[64,256]{1,0:T(8,128)S(1)}, f32[64,256]{1,0:T(8,128)S(1)}, u32[]{:S(2)}, u32[]{:S(2)}) collective-permute-start(f32[64,256]{1,0:T(8,128)S(1)} %reduce_sum.9), channel_id=1, source_target_pairs={{0,4},{2,6},{4,0},{6,2},{1,5},{3,7},{5,1},{7,3},{8,12},{10,14},{12... | collective-permute-start | bytes 196616 | tf_op jit(solution)/shard_map/ppermute | solution.py:239
  178.7 2.2 %collective-permute-done.2 = f32[64,256]{1,0:T(8,128)S(1)} collective-permute-done((f32[64,256]{1,0:T(8,128)S(1)}, f32[64,256]{1,0:T(8,128)S(1)}, u32[]{:S(2)}, u32[]{:S(2)}) %collective-permute-start.2) | collective-permute-done | bytes 65568 | tf_op jit(solution)/shard_map/ppermute | solution.py:239
  180.8 2.7 %collective-permute-done.3 = f32[64,256]{1,0:T(8,128)S(1)} collective-permute-done((f32[64,256]{1,0:T(8,128)S(1)}, f32[64,256]{1,0:T(8,128)S(1)}, u32[]{:S(2)}, u32[]{:S(2)}) %collective-permute-start.3) | collective-permute-done | bytes 65568 | tf_op jit(solution)/shard_map/ppermute | solution.py:239
  183.5 2.9 %collective-permute-start.4 = (f32[64,256]{1,0:T(8,128)S(1)}, f32[64,256]{1,0:T(8,128)S(1)}, u32[]{:S(2)}, u32[]{:S(2)}) collective-permute-start(f32[64,256]{1,0:T(8,128)S(1)} %add_add_fusion), channel_id=1, source_target_pairs={{0,1},{1,0},{2,3},{3,2},{4,5},{5,4},{6,7},{7,6},{8,9},{9,8},{10,11... | collective-permute-start | bytes 196616 | tf_op jit(solution)/shard_map/ppermute | solution.py:241
  (34 shorter events, 4.9 us)
Async XLA Ops:
  67.6 8.8 %copy-start.11 = (s32[1,128,3]{1,0,2:T(1,128)S(1)}, s32[1,128,3]{1,0,2:T(1,128)}, u32[]{:S(2)}) copy-start(s32[1,128,3]{1,0,2:T(1,128)} %param.12) | copy-start | bytes 4612
  67.6 9.1 %copy-start.2 = (s32[1,32768]{1,0:T(1,128)S(1)}, s32[1,32768]{1,0:T(1,128)}, u32[]{:S(2)}) copy-start(s32[1,32768]{1,0:T(1,128)} %param.11) | copy-start | bytes 393220
  67.6 9.1 %copy-start.4 = (s32[256]{0:T(256)S(1)}, s32[256]{0:T(256)}, u32[]{:S(2)}) copy-start(s32[256]{0:T(256)} %fusion.which_ref) | copy-start | bytes 3076
  67.6 9.1 %copy-start.5 = (s32[1,128]{1,0:T(1,128)S(1)}, s32[1,128]{1,0:T(1,128)}, u32[]{:S(2)}) copy-start(s32[1,128]{1,0:T(1,128)} %param.13) | copy-start | bytes 1540
  67.6 39.2 %all-to-all-start = ((bf16[16,64,1024]{2,1,0:T(8,128)(2,1)}), bf16[16,64,1024]{2,1,0:T(8,128)(2,1)S(1)}, u32[]{:S(2)}, u32[]{:S(2)}) async-start(bf16[16,64,1024]{2,1,0:T(8,128)(2,1)} %pick_own_blocks.1), calls=%async_computation | async-start | bytes 4194304 | tf_op jit(solution)/shard_map/all_to_all | solution.py:227
  76.7 2.2 %copy-start = (bf16[1,32768,64]{1,2,0:T(8,128)(2,1)S(1)}, bf16[1,32768,64]{1,2,0:T(8,128)(2,1)}, u32[]{:S(2)}) copy-start(bf16[1,32768,64]{1,2,0:T(8,128)(2,1)} %param.10) | copy-start | bytes 12582916
  78.9 4.6 %copy-start.1 = (bf16[1,128,3,128,128]{4,3,2,1,0:T(8,128)(2,1)S(1)}, bf16[1,128,3,128,128]{4,3,2,1,0:T(8,128)(2,1)}, u32[]{:S(2)}) copy-start(bf16[1,128,3,128,128]{4,3,2,1,0:T(8,128)(2,1)} %param.14) | copy-start | bytes 37748740
  104.9 6.9 %copy-start.10 = (bf16[1024,256]{1,0:T(8,128)(2,1)S(1)}, bf16[1024,256]{1,0:T(8,128)(2,1)}, u32[]{:S(2)}) copy-start(bf16[1024,256]{1,0:T(8,128)(2,1)} %param.16) | copy-start | bytes 1572868
  104.9 7.1 %copy-start.12 = (f32[256]{0:T(256)S(1)}, f32[256]{0:T(256)}, u32[]{:S(2)}) copy-start(f32[256]{0:T(256)} %param.18) | copy-start | bytes 3076
  106.8 33.5 %all-to-all-start.1 = ((bf16[16,64,1024]{2,1,0:T(8,128)(2,1)}), bf16[16,64,1024]{2,1,0:T(8,128)(2,1)}, u32[]{:S(2)}, u32[]{:S(2)}) async-start(bf16[16,64,1024]{2,1,0:T(8,128)(2,1)} %aggregate.1), calls=%async_computation.1 | async-start | bytes 4194304 | tf_op jit(solution)/shard_map/all_to_all | solution.py:229
  119.7 1.4 copy-start.6
  121.0 1.0 copy-start.8
  140.3 1.0 copy-start.3
  141.4 1.6 copy-start.7
  142.9 1.2 copy-start.9
  149.9 5.6 %collective-permute-start = (f32[16,64,256]{2,1,0:T(8,128)S(1)}, f32[16,64,256]{2,1,0:T(8,128)S(1)}, u32[]{:S(2)}, u32[]{:S(2)}) collective-permute-start(f32[16,64,256]{2,1,0:T(8,128)S(1)} %get-tuple-element.12), channel_id=1, source_target_pairs={{0,1},{1,0},{2,3},{3,2},{4,5},{5,4},{6,7},{7,6},{8,9},{9,8},{10,11... | collective-permute-start | bytes 3145736 | tf_op jit(solution)/shard_map/ppermute | solution.py:236
  174.7 3.9 %collective-permute-start.1 = (f32[64,256]{1,0:T(8,128)S(1)}, f32[64,256]{1,0:T(8,128)S(1)}, u32[]{:S(2)}, u32[]{:S(2)}) collective-permute-start(f32[64,256]{1,0:T(8,128)S(1)} %reduce_sum.9), channel_id=1, source_target_pairs={{0,2},{2,0},{4,6},{6,4},{1,3},{3,1},{5,7},{7,5},{8,10},{10,8},{12,... | collective-permute-start | bytes 196616 | tf_op jit(solution)/shard_map/ppermute | solution.py:239
  176.0 4.8 %collective-permute-start.2 = (f32[64,256]{1,0:T(8,128)S(1)}, f32[64,256]{1,0:T(8,128)S(1)}, u32[]{:S(2)}, u32[]{:S(2)}) collective-permute-start(f32[64,256]{1,0:T(8,128)S(1)} %reduce_sum.9), channel_id=1, source_target_pairs={{0,4},{2,6},{4,0},{6,2},{1,5},{3,7},{5,1},{7,3},{8,12},{10,14},{12... | collective-permute-start | bytes 196616 | tf_op jit(solution)/shard_map/ppermute | solution.py:239
  178.5 5.0 %collective-permute-start.3 = (f32[64,256]{1,0:T(8,128)S(1)}, f32[64,256]{1,0:T(8,128)S(1)}, u32[]{:S(2)}, u32[]{:S(2)}) collective-permute-start(f32[64,256]{1,0:T(8,128)S(1)} %reduce_sum.9), channel_id=1, source_target_pairs={{0,6},{2,4},{4,2},{6,0},{1,7},{3,5},{5,3},{7,1},{8,14},{10,12},{12... | collective-permute-start | bytes 196616 | tf_op jit(solution)/shard_map/ppermute | solution.py:239
  183.5 3.9 %collective-permute-start.4 = (f32[64,256]{1,0:T(8,128)S(1)}, f32[64,256]{1,0:T(8,128)S(1)}, u32[]{:S(2)}, u32[]{:S(2)}) collective-permute-start(f32[64,256]{1,0:T(8,128)S(1)} %add_add_fusion), channel_id=1, source_target_pairs={{0,1},{1,0},{2,3},{3,2},{4,5},{5,4},{6,7},{7,6},{8,9},{9,8},{10,11... | collective-permute-start | bytes 196616 | tf_op jit(solution)/shard_map/ppermute | solution.py:241

commit v2 on v1

--- a/solution.py
+++ b/solution.py
@@ -7,6 +7,7 @@
 
 BLOCK = 128
 MIB = 1 << 20
+WHOLE = 60 * MIB
 FEAT = ("z", "y")
 GRP = ("x", "core")
 NT = (((1,), (1,)), ((), ()))
@@ -35,7 +36,7 @@
         ).start()
         return carry
 
-    lax.fori_loop(0, owners * per, start, 0)
+    lax.fori_loop(0, owners * per, start, 0, unroll=8)
     pltpu.make_async_copy(out_ref, out_ref, sem).wait()
 
 
@@ -46,64 +47,79 @@
         pick_kernel,
         out_shape=jax.ShapeDtypeStruct((owners, width, owned), table.dtype),
         in_specs=[pl.BlockSpec(memory_space=pltpu.SMEM), pl.BlockSpec(memory_space=pl.ANY)],
-        out_specs=pl.BlockSpec(memory_space=pl.ANY),
+        out_specs=pl.BlockSpec(memory_space=pltpu.VMEM),
         scratch_shapes=[pltpu.SemaphoreType.DMA],
+        compiler_params=pltpu.CompilerParams(vmem_limit_bytes=WHOLE),
         cost_estimate=pl.CostEstimate(flops=0, bytes_accessed=4 * MIB, transcendentals=0),
         name="pick_own_blocks",
     )(which, table)
 
 
-def aggregate_kernel(which_ref, lists_ref, counts_ref, ids_ref, table_ref, tiles_ref, out_ref, source):
-    step = pl.program_id(0)
+def aggregate_kernel(
+    which_ref, lists_ref, counts_ref, ids_ref, table_hbm, tiles_hbm, out_ref, source, table, tiles, sems
+):
     blocks = ids_ref.shape[0]
-    width = table_ref.shape[0]
-    per, slots = tiles_ref.shape[0], tiles_ref.shape[1]
-
-    @pl.when(step == 0)
-    def _():
-        source[blocks] = jnp.zeros(source.shape[1:], source.dtype)
-
-        def place(n, carry):
-            w = which_ref[n]
-            chosen = table_ref[:, pl.ds(pl.multiple_of(w * BLOCK, BLOCK), BLOCK)]
-            within = ids_ref[pl.ds(n, 1), :] - w * BLOCK
-            source[n, :width] = dot(chosen, selector(within)).astype(jnp.bfloat16)
-            source[n, width:] = jnp.ones((source.shape[1] - width, BLOCK), jnp.bfloat16)
-            return carry
-
-        lax.fori_loop(0, blocks, place, 0, unroll=4)
-
-    for b in range(per):
-        d = step * per + b
-        count = counts_ref[d]
-        left = jnp.concatenate(
-            [source[jnp.where(s < count, lists_ref[d * slots + s], blocks)] for s in range(slots)], axis=1
-        )
-        right = jnp.concatenate([tiles_ref[b, s] for s in range(slots)], axis=1)
-        total = dot(left, right, NT)
-        out_ref[0, :, b * BLOCK : (b + 1) * BLOCK] = (total[:width] / total[width : width + 1]).astype(jnp.bfloat16)
+    width = table.shape[0]
+    owners = out_ref.shape[0]
+    dst_blocks, slots = tiles.shape[0], tiles.shape[1]
+    per = dst_blocks // owners
+
+    def load_tiles(r):
+        part = pl.ds(r * per, per)
+        return pltpu.make_async_copy(tiles_hbm.at[part], tiles.at[part], sems.at[r])
+
+    load_table = pltpu.make_async_copy(table_hbm, table, sems.at[owners])
+    load_table.start()
+    for r in range(owners):
+        load_tiles(r).start()
+    source[blocks] = jnp.zeros(source.shape[1:], source.dtype)
+    load_table.wait()
+
+    def place(n, carry):
+        w = which_ref[n]
+        chosen = table[:, pl.ds(pl.multiple_of(w * BLOCK, BLOCK), BLOCK)].astype(jnp.float32)
+        within = jnp.broadcast_to(ids_ref[pl.ds(n, 1), :] - w * BLOCK, (8, BLOCK))
+        rows = [jnp.take_along_axis(chosen[i : i + 8], within, axis=1) for i in range(0, width, 8)]
+        source[n, :width] = jnp.concatenate(rows, axis=0).astype(jnp.bfloat16)
+        source[n, width:] = jnp.ones((source.shape[1] - width, BLOCK), jnp.bfloat16)
+        return carry
+
+    lax.fori_loop(0, blocks, place, 0, unroll=16)
+
+    def owner(r, carry):
+        load_tiles(r).wait()
+        for b in range(per):
+            d = r * per + b
+            count = counts_ref[d]
+            used = [jnp.where(s < count, lists_ref[s * dst_blocks + d], blocks) for s in range(slots)]
+            left = jnp.concatenate([source[u] for u in used], axis=1)
+            right = jnp.concatenate([tiles[d, s] for s in range(slots)], axis=1)
+            total = dot(left, right, NT)
+            out_ref[r, :, b * BLOCK : (b + 1) * BLOCK] = (total[:width] / total[width : width + 1]).astype(
+                jnp.bfloat16
+            )
+        return carry
+
+    lax.fori_loop(0, owners, owner, 0)
 
 
 def aggregate(which, lists, counts, ids, table, tiles, owners):
     width, rows = table.shape
     blocks = rows // BLOCK
-    dst_blocks, slots = tiles.shape[0], tiles.shape[1]
-    per = dst_blocks // owners
+    smem, vmem = pl.BlockSpec(memory_space=pltpu.SMEM), pl.BlockSpec(memory_space=pltpu.VMEM)
+    anywhere = pl.BlockSpec(memory_space=pl.ANY)
     return pl.pallas_call(
         aggregate_kernel,
-        grid_spec=pltpu.PrefetchScalarGridSpec(
-            num_scalar_prefetch=3,
-            grid=(owners,),
-            in_specs=[
-                pl.BlockSpec(memory_space=pltpu.VMEM),
-                pl.BlockSpec(memory_space=pltpu.VMEM),
-                pl.BlockSpec((per, slots, BLOCK, BLOCK), lambda r, *_: (r, 0, 0, 0)),
-            ],
-            out_specs=pl.BlockSpec((1, width, per * BLOCK), lambda r, *_: (r, 0, 0)),
-            scratch_shapes=[pltpu.VMEM((blocks + 1, width + 16, BLOCK), jnp.bfloat16)],
-        ),
-        out_shape=jax.ShapeDtypeStruct((owners, width, per * BLOCK), jnp.bfloat16),
-        compiler_params=pltpu.CompilerParams(vmem_limit_bytes=32 * MIB),
+        in_specs=[smem, smem, smem, vmem, anywhere, anywhere],
+        out_specs=vmem,
+        out_shape=jax.ShapeDtypeStruct((owners, width, tiles.shape[0] // owners * BLOCK), jnp.bfloat16),
+        scratch_shapes=[
+            pltpu.VMEM((blocks + 1, width + 16, BLOCK), jnp.bfloat16),
+            pltpu.VMEM(table.shape, jnp.bfloat16),
+            pltpu.VMEM(tiles.shape, jnp.bfloat16),
+            pltpu.SemaphoreType.DMA((owners + 1,)),
+        ],
+        compiler_params=pltpu.CompilerParams(vmem_limit_bytes=WHOLE),
         cost_estimate=pl.CostEstimate(flops=4_000_000_000, bytes_accessed=20 * MIB, transcendentals=0),
         name="aggregate",
     )(which, lists, counts, ids, table, tiles)
@@ -158,19 +174,36 @@
 
 
 def finish_kernel(
-    place_ref, pre_ref, agg_ref, own_ref, weight_ref, upstream_ref, hidden_ref, keep_ref, send_ref, slope
+    place_ref, pre_hbm, agg_hbm, own_hbm, weight_hbm, upstream_hbm, hidden_ref, keep_ref, send_ref,
+    pre_ref, agg_ref, own_ref, weight_ref, upstream_ref, slope, sems,
 ):
     owned = pre_ref.shape[1]
     wide = 2 * BLOCK
+    chunks = [slice(j, j + wide) for j in range(0, owned, wide)]
     limit, core = place_ref[0], place_ref[1]
-    for j in range(owned // wide):
-        columns = slice(j * wide, (j + 1) * wide)
-        pre = pre_ref[:, columns] + dot(weight_ref[...], agg_ref[:, columns])
-        active, back = gelu_and_slope(pre)
+
+    loads = [pltpu.make_async_copy(weight_hbm, weight_ref, sems.at[0])]
+    for j, columns in enumerate(chunks):
+        loads.append(pltpu.make_async_copy(agg_hbm.at[:, columns], agg_ref.at[:, columns], sems.at[j + 1]))
+    loads.append(pltpu.make_async_copy(pre_hbm, pre_ref, sems.at[len(chunks) + 1]))
+    loads.append(pltpu.make_async_copy(upstream_hbm, upstream_ref, sems.at[len(chunks) + 2]))
+    loads.append(pltpu.make_async_copy(own_hbm, own_ref, sems.at[len(chunks) + 3]))
+    for load in loads:
+        load.start()
+    loads[0].wait()
+
+    for j, columns in enumerate(chunks):
+        loads[j + 1].wait()
+        pre = dot(weight_ref[...], agg_ref[:, columns])
+        if j == 0:
+            loads[-3].wait()
+            loads[-2].wait()
+        active, back = gelu_and_slope(pre + pre_ref[:, columns])
         positions = j * wide + lax.broadcasted_iota(jnp.int32, (1, wide), 1)
         valid = jnp.where(positions < limit, 1.0, 0.0)
         hidden_ref[:, columns] = (active * valid).astype(jnp.bfloat16)
         slope[:, columns] = (upstream_ref[:, columns].astype(jnp.float32) * back * valid).astype(jnp.bfloat16)
+    loads[-1].wait()
 
     owners, share, _ = keep_ref.shape
 
@@ -179,7 +212,8 @@
 
         def part(i, carry):
             left = left_ref[pl.ds(pl.multiple_of(i * group * share, group * share), group * share), :]
-            out_ref[pl.ds(i * group, group)] = dot(left, slope[...], NT).reshape(group, share, -1)
+            total = dot(left, slope[...], NT).reshape(group, share, -1)
+            out_ref[pl.ds(i * group, group)] = total.astype(out_ref.dtype)
             return carry
 
         lax.fori_loop(0, owners // group, part, 0)
@@ -198,15 +232,20 @@
 def finish(place, pre, agg, own, weight, upstream, owners):
     hidden, owned = pre.shape
     features = agg.shape[0]
-    part = jax.ShapeDtypeStruct((owners, features // owners, hidden), jnp.float32)
-    vmem = pl.BlockSpec(memory_space=pltpu.VMEM)
+    part = (owners, features // owners, hidden)
+    vmem, anywhere = pl.BlockSpec(memory_space=pltpu.VMEM), pl.BlockSpec(memory_space=pl.ANY)
     return pl.pallas_call(
         finish_kernel,
-        in_specs=[pl.BlockSpec(memory_space=pltpu.SMEM)] + [vmem] * 5,
+        in_specs=[pl.BlockSpec(memory_space=pltpu.SMEM)] + [anywhere] * 5,
         out_specs=[vmem] * 3,
-        out_shape=[jax.ShapeDtypeStruct((hidden, owned), jnp.bfloat16), part, part],
-        scratch_shapes=[pltpu.VMEM((hidden, owned), jnp.bfloat16)],
-        compiler_params=pltpu.CompilerParams(vmem_limit_bytes=32 * MIB),
+        out_shape=[
+            jax.ShapeDtypeStruct((hidden, owned), jnp.bfloat16),
+            jax.ShapeDtypeStruct(part, jnp.float32),
+            jax.ShapeDtypeStruct(part, jnp.bfloat16),
+        ],
+        scratch_shapes=[pltpu.VMEM(a.shape, a.dtype) for a in (pre, agg, own, weight, upstream)]
+        + [pltpu.VMEM((hidden, owned), jnp.bfloat16), pltpu.SemaphoreType.DMA((owned // (2 * BLOCK) + 4,))],
+        compiler_params=pltpu.CompilerParams(vmem_limit_bytes=WHOLE),
         cost_estimate=pl.CostEstimate(flops=2_000_000_000, bytes_accessed=9 * MIB, transcendentals=262144),
         name="finish",
     )(place, pre, agg, own, weight, upstream)
@@ -225,7 +264,7 @@
 
     mine = pick(which, table, owners)
     moved = lax.all_to_all(mine, FEAT, split_axis=0, concat_axis=0, tiled=True)
-    aggregated = aggregate(which, block_lists[0].reshape(-1), block_counts[0], ids, table, tiles[0], owners)
+    aggregated = aggregate(which, block_lists[0].T.reshape(-1), block_counts[0], ids, table, tiles[0], owners)
     agg = lax.all_to_all(aggregated, FEAT, split_axis=0, concat_axis=0, tiled=True).reshape(-1, owned)
 
     first = (rank * (owned // BLOCK)).reshape(1)
@@ -234,8 +273,8 @@
     hidden, keep, send = finish(place, pre, agg, own, w_neigh.T, cotangent[0].T, owners)
 
     got = lax.ppermute(send, "core", [(0, 1), (1, 0)])
-    parts = lax.all_to_all(keep + got, FEAT, split_axis=0, concat_axis=0, tiled=True)
-    total = jnp.sum(parts, axis=0)
+    parts = lax.all_to_all((keep + got).astype(jnp.bfloat16), FEAT, split_axis=0, concat_axis=0, tiled=True)
+    total = jnp.sum(parts, axis=0, dtype=jnp.float32)
     others = [lax.ppermute(total, "x", [(i, i ^ k) for i in range(4)]) for k in (1, 2, 3)]
     total = (total + others[0]) + (others[1] + others[2])
     other = lax.ppermute(total, "core", [(0, 1), (1, 0)])

time: 189 us -> 121 us (0.64)
  Pallas kernels: 96 us -> 32.4 us
  local copies, waits for them, and re-layouts: 17.9 us -> 8.35 us
  waiting for transfers between devices: 27.4 us -> 35.9 us
  blocking collectives: 19 us -> 13.5 us
    pallas_call x1, Pallas kernels: 65.3 us -> 4.1 us  [pick(): pl.pallas_call(pick_kernel, out_shape=jax.ShapeDtypeStruct((owners, width...]
    all_to_all x1, waiting for transfers between devices: 1.93 us -> 14.2 us  [on_device(): moved = lax.all_to_all(mine, FEAT, split_axis=0, concat_axis=0, tiled=True)]
    unnamed x31 -> x19, local copies, waits for them, and re-layouts: 17.6 us -> 8.22 us
    pallas_call x1, Pallas kernels: 21.4 us -> 15.7 us  [aggregate(): pl.pallas_call(aggregate_kernel, in_specs=[smem, smem, smem, vmem, anywhe...]
    all_to_all x1, blocking collectives: 19 us -> 13.5 us  [on_device(): lax.all_to_all((keep + got).astype(jnp.bfloat16), FEAT, split_axis=0, con...]
    pallas_call x1, Pallas kernels: 5.73 us -> 9.19 us  [finish(): pl.pallas_call(finish_kernel, in_specs=[pl.BlockSpec(memory_space=pltpu.S...]
    all_to_all x1, waiting for transfers between devices: 18.3 us -> 15.2 us  [on_device(): lax.all_to_all(aggregated, FEAT, split_axis=0, concat_axis=0, tiled=True)]
  transfers between devices with their start and end apart: 7 -> 7, of which waited for: 5 -> 5; matrix products, arithmetic and copies ran while one was open for 3% -> 5% of each run, Pallas kernels for 13% -> 16%
where the time goes in v2:
time: 121 us
  waiting for transfers between devices  35.9 us (30%)
  Pallas kernels  32.4 us (27%)
  starting transfers between devices  24.6 us (20%)
  blocking collectives  13.5 us (11%)
  local copies, waits for them, and re-layouts  8.35 us (7%)
  other arithmetic  4.29 us (4%)
  between operations  1.45 us (1%)
    pallas_call x1, Pallas kernels, aggregate(): pl.pallas_call(aggregate_kernel, in_specs=[smem, smem, smem, vmem, anywhe...  15.7 us
    all_to_all x1, waiting for transfers between devices, on_device(): lax.all_to_all(aggregated, FEAT, split_axis=0, concat_axis=0, tiled=True)  15.2 us
    all_to_all x1, waiting for transfers between devices, on_device(): moved = lax.all_to_all(mine, FEAT, split_axis=0, concat_axis=0, tiled=True)  14.2 us
    all_to_all x1, blocking collectives, on_device(): lax.all_to_all((keep + got).astype(jnp.bfloat16), FEAT, split_axis=0, con...  13.5 us
    pallas_call x1, Pallas kernels, finish(): pl.pallas_call(finish_kernel, in_specs=[pl.BlockSpec(memory_space=pltpu.S...  9.19 us
    all_to_all x1, starting transfers between devices, on_device(): moved = lax.all_to_all(mine, FEAT, split_axis=0, concat_axis=0, tiled=True)  8.61 us
    unnamed x19, local copies, waits for them, and re-layouts  8.22 us
    ppermute x1, starting transfers between devices, on_device(): got = lax.ppermute(send, 'core', [(0, 1), (1, 0)])  4.86 us
  transfers between devices with their start and end apart: 7, of which 5 were waited for; matrix products, arithmetic and copies ran while one was open for 5% of the time, Pallas kernels for 16%

profile of v2, /device:TPU:1, one launch (start us, length us, event | category | flops | bytes accessed | tf_op | source)
XLA Modules:
  0.0 120.5 jit_solution(6090559148085027703)
XLA Ops:
  0.6 1.6 %fusion.which_ref = s32[256]{0:T(256)} fusion(s32[256,128]{1,0:T(8,128)} %bitcast.30), kind=kLoop, calls=%fused_computation.3 | loop fusion | flops 256 | bytes 2048 | tf_op jit(solution)/shard_map/shift_right_logical | solution.py:262
  2.2 4.1 %pick_own_blocks.1 = bf16[16,64,1024]{2,1,0:T(8,128)(2,1)} custom-call(s32[256]{0:T(256)} %fusion.which_ref, bf16[64,32768]{1,0:T(8,128)(2,1)} %bitcast.34), custom_call_target="tpu_custom_call" | custom-call | bytes 4194304 | tf_op jit(solution)/shard_map/pick_own_blocks/pallas_call | solution.py:46
  6.3 8.6 %all-to-all-start = ((bf16[16,64,1024]{2,1,0:T(8,128)(2,1)}), bf16[16,64,1024]{2,1,0:T(8,128)(2,1)S(1)}, u32[]{:S(2)}, u32[]{:S(2)}) async-start(bf16[16,64,1024]{2,1,0:T(8,128)(2,1)} %pick_own_blocks.1), calls=%async_computation | async-start | bytes 4194304 | tf_op jit(solution)/shard_map/all_to_all | solution.py:266
  15.5 15.7 %aggregate.1 = bf16[16,64,1024]{2,1,0:T(8,128)(2,1)} custom-call(s32[256]{0:T(256)} %fusion.which_ref, s32[384]{0:T(512)} %bitcast.40, s32[128]{0:T(128)} %bitcast.42, s32[256,128]{1,0:T(8,128)} %bitcast.31, bf16[64,32768]{1,0:T(8,128)(2,1)} %bitcast.35, bf16[128,3,128,128]{3,2,1,0:T(8,128)(2,1)} %bitcast.36), custom_call_target="tpu_custom_call" | custom-call | flops 4000000000 | bytes 20971520 | tf_op jit(solution)/shard_map/aggregate/pallas_call | solution.py:111
  31.2 14.2 %all-to-all-done = bf16[16,64,1024]{2,1,0:T(8,128)(2,1)S(1)} async-done(((bf16[16,64,1024]{2,1,0:T(8,128)(2,1)}), bf16[16,64,1024]{2,1,0:T(8,128)(2,1)S(1)}, u32[]{:S(2)}, u32[]{:S(2)}) %all-to-all-start) | async-done | bytes 2097184 | tf_op jit(solution)/shard_map/all_to_all | solution.py:266
  45.4 4.4 %all-to-all-start.1 = ((bf16[16,64,1024]{2,1,0:T(8,128)(2,1)}), bf16[16,64,1024]{2,1,0:T(8,128)(2,1)}, u32[]{:S(2)}, u32[]{:S(2)}) async-start(bf16[16,64,1024]{2,1,0:T(8,128)(2,1)} %aggregate.1), calls=%async_computation.1 | async-start | bytes 4194304 | tf_op jit(solution)/shard_map/all_to_all | solution.py:268
  50.9 2.0 %copy.19 = bf16[1024,256]{0,1:T(8,128)(2,1)} copy(bf16[1024,256]{1,0:T(8,128)(2,1)} %param.17) | data formatting | bytes 1048576 | tf_op args[7]
  53.0 2.0 %copy.20 = bf16[1,1024,256]{1,2,0:T(8,128)(2,1)} copy(bf16[1,1024,256]{2,1,0:T(8,128)(2,1)} %param.19) | data formatting | bytes 1048576 | tf_op args[9]
  55.6 3.5 %own_part.1 = (bf16[1024,1024]{1,0:T(8,128)(2,1)S(1)}, f32[256,1024]{1,0:T(8,128)S(1)}) custom-call(s32[1]{0:T(128)} %bitcast.3.first_ref, s32[256,128]{1,0:T(8,128)S(1)} %bitcast.32, bf16[1024,1024]{1,0:T(8,128)(2,1)S(1)} %bitcast.29, bf16[256,1024]{1,0:T(8,128)(2,1)S(1)} %bitcast.33, f32[256,1]{1,0:T(8,128)S(1)} %copy.18.bias_ref), custom_call_target="tpu_custom_call" | custom-call | flops 2000000000 | bytes 6291456 | tf_op jit(solution)/shard_map/own_part/pallas_call | solution.py:143
  59.1 1.3 %copy-done.1 = bf16[1024,1024]{1,0:T(8,128)(2,1)} copy-done((bf16[1024,1024]{1,0:T(8,128)(2,1)}, bf16[1024,1024]{1,0:T(8,128)(2,1)S(1)}, u32[]{:S(2)}) %copy-start.1) | copy-done | bytes 2097176
  60.4 1.0 copy-done.2
  61.4 15.2 %all-to-all-done.1 = bf16[16,64,1024]{2,1,0:T(8,128)(2,1)} async-done(((bf16[16,64,1024]{2,1,0:T(8,128)(2,1)}), bf16[16,64,1024]{2,1,0:T(8,128)(2,1)}, u32[]{:S(2)}, u32[]{:S(2)}) %all-to-all-start.1) | async-done | bytes 2097184 | tf_op jit(solution)/shard_map/all_to_all | solution.py:268
  76.6 9.2 %finish.1 = (bf16[256,1024]{1,0:T(8,128)(2,1)}, f32[16,64,256]{2,1,0:T(8,128)}, bf16[16,64,256]{2,1,0:T(8,128)(2,1)}) custom-call(s32[2]{0:T(128)} %pad_add_fusion.place_ref, f32[256,1024]{1,0:T(8,128)} %copy-done.2, bf16[1024,1024]{1,0:T(8,128)(2,1)} %bitcast.15.agg_hbm, bf16[1024,1024]{1,0:T(8,128)(2,1)} %copy-done.1, bf16[256,1024]{1,0:T(8,128)(2,1)} %bitcast.38, ...), custom_call_target="tpu_custom_call" | custom-call | flops 2000000000 | bytes 9437184 | tf_op jit(solution)/shard_map/finish/pallas_call | solution.py:237
  85.8 4.9 %collective-permute-start = (bf16[16,64,256]{2,1,0:T(8,128)(2,1)}, bf16[16,64,256]{2,1,0:T(8,128)(2,1)S(1)}, u32[]{:S(2)}, u32[]{:S(2)}) collective-permute-start(bf16[16,64,256]{2,1,0:T(8,128)(2,1)} %get-tuple-element.12), channel_id=1, source_target_pairs={{0,1},{1,0},{2,3},{3,2},{4,5},{5,4},{6,7},{7,6},{8,9},{9,8},{10,11... | collective-permute-start | bytes 1572872 | tf_op jit(solution)/shard_map/ppermute | solution.py:275
  90.7 1.7 %collective-permute-done = bf16[16,64,256]{2,1,0:T(8,128)(2,1)S(1)} collective-permute-done((bf16[16,64,256]{2,1,0:T(8,128)(2,1)}, bf16[16,64,256]{2,1,0:T(8,128)(2,1)S(1)}, u32[]{:S(2)}, u32[]{:S(2)}) %collective-permute-start) | collective-permute-done | bytes 524320 | tf_op jit(solution)/shard_map/ppermute | solution.py:275
  92.4 1.4 %add_convert_fusion = bf16[16,64,256]{2,1,0:T(8,128)(2,1)S(1)} fusion(f32[16,64,256]{2,1,0:T(8,128)} %get-tuple-element.11, bf16[16,64,256]{2,1,0:T(8,128)(2,1)S(1)} %collective-permute-done), kind=kLoop, calls=%fused_computation.1 | loop fusion | flops 786432 | bytes 2097152 | tf_op jit(solution)/shard_map/convert_element_type | solution.py:276
  93.8 13.5 %all_to_all.15 = bf16[16,64,256]{2,1,0:T(8,128)(2,1)S(1)} all-to-all(bf16[16,64,256]{2,1,0:T(8,128)(2,1)S(1)} %add_convert_fusion), channel_id=1, replica_groups=mesh['z'=4,'y'=4,'x'=4,'core'=2] {'z','y'}, dimensions={0} | all-to-all | bytes 1048576 | tf_op jit(solution)/shard_map/all_to_all | solution.py:276
  107.3 1.3 %collective-permute-start.1 = (f32[64,256]{1,0:T(8,128)S(1)}, f32[64,256]{1,0:T(8,128)S(1)}, u32[]{:S(2)}, u32[]{:S(2)}) collective-permute-start(f32[64,256]{1,0:T(8,128)S(1)} %convert_reduce_fusion), channel_id=1, source_target_pairs={{0,2},{2,0},{4,6},{6,4},{1,3},{3,1},{5,7},{7,5},{8,10},{10,8},{12,... | collective-permute-start | bytes 196616 | tf_op jit(solution)/shard_map/ppermute | solution.py:278
  108.6 2.4 %collective-permute-start.2 = (f32[64,256]{1,0:T(8,128)S(1)}, f32[64,256]{1,0:T(8,128)S(1)}, u32[]{:S(2)}, u32[]{:S(2)}) collective-permute-start(f32[64,256]{1,0:T(8,128)S(1)} %convert_reduce_fusion), channel_id=1, source_target_pairs={{0,4},{2,6},{4,0},{6,2},{1,5},{3,7},{5,1},{7,3},{8,12},{10,14},{12... | collective-permute-start | bytes 196616 | tf_op jit(solution)/shard_map/ppermute | solution.py:278
  111.3 2.1 %collective-permute-done.2 = f32[64,256]{1,0:T(8,128)S(1)} collective-permute-done((f32[64,256]{1,0:T(8,128)S(1)}, f32[64,256]{1,0:T(8,128)S(1)}, u32[]{:S(2)}, u32[]{:S(2)}) %collective-permute-start.2) | collective-permute-done | bytes 65568 | tf_op jit(solution)/shard_map/ppermute | solution.py:278
  113.4 2.7 %collective-permute-done.3 = f32[64,256]{1,0:T(8,128)S(1)} collective-permute-done((f32[64,256]{1,0:T(8,128)S(1)}, f32[64,256]{1,0:T(8,128)S(1)}, u32[]{:S(2)}, u32[]{:S(2)}) %collective-permute-start.3) | collective-permute-done | bytes 65568 | tf_op jit(solution)/shard_map/ppermute | solution.py:278
  116.1 2.7 %collective-permute-start.4 = (f32[64,256]{1,0:T(8,128)S(1)}, f32[64,256]{1,0:T(8,128)S(1)}, u32[]{:S(2)}, u32[]{:S(2)}) collective-permute-start(f32[64,256]{1,0:T(8,128)S(1)} %add_add_fusion), channel_id=1, source_target_pairs={{0,1},{1,0},{2,3},{3,2},{4,5},{5,4},{6,7},{7,6},{8,9},{9,8},{10,11... | collective-permute-start | bytes 196616 | tf_op jit(solution)/shard_map/ppermute | solution.py:280
  118.8 1.0 copy.21
  119.8 0.7 broadcast_select_fusion
  (21 shorter events, 1.8 us)
Async XLA Ops:
  6.3 8.6 %copy-start.5 = (s32[1,128,3]{1,0,2:T(1,128)S(1)}, s32[1,128,3]{1,0,2:T(1,128)}, u32[]{:S(2)}) copy-start(s32[1,128,3]{1,0,2:T(1,128)} %param.12) | copy-start | bytes 4612
  6.3 39.1 %all-to-all-start = ((bf16[16,64,1024]{2,1,0:T(8,128)(2,1)}), bf16[16,64,1024]{2,1,0:T(8,128)(2,1)S(1)}, u32[]{:S(2)}, u32[]{:S(2)}) async-start(bf16[16,64,1024]{2,1,0:T(8,128)(2,1)} %pick_own_blocks.1), calls=%async_computation | async-start | bytes 4194304 | tf_op jit(solution)/shard_map/all_to_all | solution.py:266
  31.2 18.7 %copy-start.3 = (bf16[1024,256]{1,0:T(8,128)(2,1)S(1)}, bf16[1024,256]{1,0:T(8,128)(2,1)}, u32[]{:S(2)}) copy-start(bf16[1024,256]{1,0:T(8,128)(2,1)} %param.16) | copy-start | bytes 1572868
  31.2 18.9 %copy-start.6 = (f32[256]{0:T(256)S(1)}, f32[256]{0:T(256)}, u32[]{:S(2)}) copy-start(f32[256]{0:T(256)} %param.18) | copy-start | bytes 3076
  45.4 31.2 %all-to-all-start.1 = ((bf16[16,64,1024]{2,1,0:T(8,128)(2,1)}), bf16[16,64,1024]{2,1,0:T(8,128)(2,1)}, u32[]{:S(2)}, u32[]{:S(2)}) async-start(bf16[16,64,1024]{2,1,0:T(8,128)(2,1)} %aggregate.1), calls=%async_computation.1 | async-start | bytes 4194304 | tf_op jit(solution)/shard_map/all_to_all | solution.py:268
  49.9 5.7 %copy-start = (s32[1,32768]{1,0:T(1,128)S(1)}, s32[1,32768]{1,0:T(1,128)}, u32[]{:S(2)}) copy-start(s32[1,32768]{1,0:T(1,128)} %param.11) | copy-start | bytes 393220
  59.1 1.3 %copy-start.1 = (bf16[1024,1024]{1,0:T(8,128)(2,1)}, bf16[1024,1024]{1,0:T(8,128)(2,1)S(1)}, u32[]{:S(2)}) copy-start(bf16[1024,1024]{1,0:T(8,128)(2,1)S(1)} %get-tuple-element.9.own_hbm) | copy-start | bytes 6291460
  60.4 1.0 copy-start.2
  85.8 33.0 %copy-start.4 = (bf16[256,1024]{1,0:T(8,128)(2,1)S(1)}, bf16[256,1024]{1,0:T(8,128)(2,1)}, u32[]{:S(2)}) copy-start(bf16[256,1024]{1,0:T(8,128)(2,1)} %get-tuple-element.10) | copy-start | bytes 1572868
  85.8 6.6 %collective-permute-start = (bf16[16,64,256]{2,1,0:T(8,128)(2,1)}, bf16[16,64,256]{2,1,0:T(8,128)(2,1)S(1)}, u32[]{:S(2)}, u32[]{:S(2)}) collective-permute-start(bf16[16,64,256]{2,1,0:T(8,128)(2,1)} %get-tuple-element.12), channel_id=1, source_target_pairs={{0,1},{1,0},{2,3},{3,2},{4,5},{5,4},{6,7},{7,6},{8,9},{9,8},{10,11... | collective-permute-start | bytes 1572872 | tf_op jit(solution)/shard_map/ppermute | solution.py:275
  107.3 3.9 %collective-permute-start.1 = (f32[64,256]{1,0:T(8,128)S(1)}, f32[64,256]{1,0:T(8,128)S(1)}, u32[]{:S(2)}, u32[]{:S(2)}) collective-permute-start(f32[64,256]{1,0:T(8,128)S(1)} %convert_reduce_fusion), channel_id=1, source_target_pairs={{0,2},{2,0},{4,6},{6,4},{1,3},{3,1},{5,7},{7,5},{8,10},{10,8},{12,... | collective-permute-start | bytes 196616 | tf_op jit(solution)/shard_map/ppermute | solution.py:278
  108.6 4.8 %collective-permute-start.2 = (f32[64,256]{1,0:T(8,128)S(1)}, f32[64,256]{1,0:T(8,128)S(1)}, u32[]{:S(2)}, u32[]{:S(2)}) collective-permute-start(f32[64,256]{1,0:T(8,128)S(1)} %convert_reduce_fusion), channel_id=1, source_target_pairs={{0,4},{2,6},{4,0},{6,2},{1,5},{3,7},{5,1},{7,3},{8,12},{10,14},{12... | collective-permute-start | bytes 196616 | tf_op jit(solution)/shard_map/ppermute | solution.py:278
  111.1 5.0 %collective-permute-start.3 = (f32[64,256]{1,0:T(8,128)S(1)}, f32[64,256]{1,0:T(8,128)S(1)}, u32[]{:S(2)}, u32[]{:S(2)}) collective-permute-start(f32[64,256]{1,0:T(8,128)S(1)} %convert_reduce_fusion), channel_id=1, source_target_pairs={{0,6},{2,4},{4,2},{6,0},{1,7},{3,5},{5,3},{7,1},{8,14},{10,12},{12... | collective-permute-start | bytes 196616 | tf_op jit(solution)/shard_map/ppermute | solution.py:278
  116.1 3.7 %collective-permute-start.4 = (f32[64,256]{1,0:T(8,128)S(1)}, f32[64,256]{1,0:T(8,128)S(1)}, u32[]{:S(2)}, u32[]{:S(2)}) collective-permute-start(f32[64,256]{1,0:T(8,128)S(1)} %add_add_fusion), channel_id=1, source_target_pairs={{0,1},{1,0},{2,3},{3,2},{4,5},{5,4},{6,7},{7,6},{8,9},{9,8},{10,11... | collective-permute-start | bytes 196616 | tf_op jit(solution)/shard_map/ppermute | solution.py:280

commit v3 on v2

--- a/solution.py
+++ b/solution.py
@@ -23,68 +23,112 @@
     return jnp.where(rows == within, 1.0, 0.0).astype(jnp.bfloat16)
 
 
-def pick_kernel(which_ref, table_ref, out_ref, sem):
+def place_blocks(which_ref, ids_ref, table, source):
+    width = table.shape[0]
+
+    def place(n, carry):
+        w = which_ref[n]
+        chosen = table[:, pl.ds(pl.multiple_of(w * BLOCK, BLOCK), BLOCK)].astype(jnp.float32)
+        within = jnp.broadcast_to(ids_ref[pl.ds(n, 1), :] - w * BLOCK, (8, BLOCK))
+        rows = [jnp.take_along_axis(chosen[i : i + 8], within, axis=1) for i in range(0, width, 8)]
+        source[n, :width] = jnp.concatenate(rows, axis=0).astype(jnp.bfloat16)
+        return carry
+
+    lax.fori_loop(0, ids_ref.shape[0], place, 0, unroll=16)
+
+
+def pick_kernel(core_ref, which_ref, ids_ref, table_hbm, out_ref, placed_hbm, table, placed, sems):
     owners, _, owned = out_ref.shape
     per = owned // BLOCK
 
     def start(b, carry):
         w = which_ref[b]
         pltpu.make_async_copy(
-            table_ref.at[:, pl.ds(pl.multiple_of(w * BLOCK, BLOCK), BLOCK)],
+            table_hbm.at[:, pl.ds(pl.multiple_of(w * BLOCK, BLOCK), BLOCK)],
             out_ref.at[b // per, :, pl.ds(pl.multiple_of((b % per) * BLOCK, BLOCK), BLOCK)],
-            sem,
+            sems.at[0],
         ).start()
         return carry
 
     lax.fori_loop(0, owners * per, start, 0, unroll=8)
-    pltpu.make_async_copy(out_ref, out_ref, sem).wait()
-
-
-def pick(which, table, owners):
+
+    @pl.when(core_ref[0] == 1)
+    def _():
+        load = pltpu.make_async_copy(table_hbm, table, sems.at[1])
+        load.start()
+        load.wait()
+        place_blocks(which_ref, ids_ref, table, placed)
+        store = pltpu.make_async_copy(placed, placed_hbm, sems.at[2])
+        store.start()
+        store.wait()
+
+    pltpu.make_async_copy(out_ref, out_ref, sems.at[0]).wait()
+
+
+def pick(core, which, ids, table, owners):
     width, rows = table.shape
     owned = rows // 2 // owners
+    placed = (rows // BLOCK, width, BLOCK)
+    smem, vmem = pl.BlockSpec(memory_space=pltpu.SMEM), pl.BlockSpec(memory_space=pltpu.VMEM)
+    anywhere = pl.BlockSpec(memory_space=pl.ANY)
     return pl.pallas_call(
         pick_kernel,
-        out_shape=jax.ShapeDtypeStruct((owners, width, owned), table.dtype),
-        in_specs=[pl.BlockSpec(memory_space=pltpu.SMEM), pl.BlockSpec(memory_space=pl.ANY)],
-        out_specs=pl.BlockSpec(memory_space=pltpu.VMEM),
-        scratch_shapes=[pltpu.SemaphoreType.DMA],
+        out_shape=[
+            jax.ShapeDtypeStruct((owners, width, owned), table.dtype),
+            jax.ShapeDtypeStruct(placed, table.dtype),
+        ],
+        in_specs=[smem, smem, vmem, anywhere],
+        out_specs=[vmem, anywhere],
+        scratch_shapes=[
+            pltpu.VMEM(table.shape, table.dtype),
+            pltpu.VMEM(placed, table.dtype),
+            pltpu.SemaphoreType.DMA((3,)),
+        ],
         compiler_params=pltpu.CompilerParams(vmem_limit_bytes=WHOLE),
         cost_estimate=pl.CostEstimate(flops=0, bytes_accessed=4 * MIB, transcendentals=0),
         name="pick_own_blocks",
-    )(which, table)
+    )(core, which, ids, table)
 
 
 def aggregate_kernel(
-    which_ref, lists_ref, counts_ref, ids_ref, table_hbm, tiles_hbm, out_ref, source, table, tiles, sems
+    core_ref, which_ref, lists_ref, counts_ref, ids_ref, table_hbm, placed_hbm, tiles_hbm, out_ref,
+    source, table, tiles, sems,
 ):
     blocks = ids_ref.shape[0]
     width = table.shape[0]
     owners = out_ref.shape[0]
     dst_blocks, slots = tiles.shape[0], tiles.shape[1]
     per = dst_blocks // owners
+    core = core_ref[0]
 
     def load_tiles(r):
         part = pl.ds(r * per, per)
         return pltpu.make_async_copy(tiles_hbm.at[part], tiles.at[part], sems.at[r])
 
     load_table = pltpu.make_async_copy(table_hbm, table, sems.at[owners])
-    load_table.start()
+    load_placed = pltpu.make_async_copy(placed_hbm, source.at[pl.ds(0, blocks), pl.ds(0, width)], sems.at[owners])
+
+    @pl.when(core == 0)
+    def _():
+        load_table.start()
+
+    @pl.when(core == 1)
+    def _():
+        load_placed.start()
+
     for r in range(owners):
         load_tiles(r).start()
+    source[:blocks, width:] = jnp.ones((blocks, source.shape[1] - width, BLOCK), source.dtype)
     source[blocks] = jnp.zeros(source.shape[1:], source.dtype)
-    load_table.wait()
-
-    def place(n, carry):
-        w = which_ref[n]
-        chosen = table[:, pl.ds(pl.multiple_of(w * BLOCK, BLOCK), BLOCK)].astype(jnp.float32)
-        within = jnp.broadcast_to(ids_ref[pl.ds(n, 1), :] - w * BLOCK, (8, BLOCK))
-        rows = [jnp.take_along_axis(chosen[i : i + 8], within, axis=1) for i in range(0, width, 8)]
-        source[n, :width] = jnp.concatenate(rows, axis=0).astype(jnp.bfloat16)
-        source[n, width:] = jnp.ones((source.shape[1] - width, BLOCK), jnp.bfloat16)
-        return carry
-
-    lax.fori_loop(0, blocks, place, 0, unroll=16)
+
+    @pl.when(core == 0)
+    def _():
+        load_table.wait()
+        place_blocks(which_ref, ids_ref, table, source)
+
+    @pl.when(core == 1)
+    def _():
+        load_placed.wait()
 
     def owner(r, carry):
         load_tiles(r).wait()
@@ -103,14 +147,14 @@
     lax.fori_loop(0, owners, owner, 0)
 
 
-def aggregate(which, lists, counts, ids, table, tiles, owners):
+def aggregate(core, which, lists, counts, ids, table, placed, tiles, owners):
     width, rows = table.shape
     blocks = rows // BLOCK
     smem, vmem = pl.BlockSpec(memory_space=pltpu.SMEM), pl.BlockSpec(memory_space=pltpu.VMEM)
     anywhere = pl.BlockSpec(memory_space=pl.ANY)
     return pl.pallas_call(
         aggregate_kernel,
-        in_specs=[smem, smem, smem, vmem, anywhere, anywhere],
+        in_specs=[smem, smem, smem, smem, vmem, anywhere, anywhere, anywhere],
         out_specs=vmem,
         out_shape=jax.ShapeDtypeStruct((owners, width, tiles.shape[0] // owners * BLOCK), jnp.bfloat16),
         scratch_shapes=[
@@ -122,7 +166,7 @@
         compiler_params=pltpu.CompilerParams(vmem_limit_bytes=WHOLE),
         cost_estimate=pl.CostEstimate(flops=4_000_000_000, bytes_accessed=20 * MIB, transcendentals=0),
         name="aggregate",
-    )(which, lists, counts, ids, table, tiles)
+    )(core, which, lists, counts, ids, table, placed, tiles)
 
 
 def own_kernel(first_ref, ids_ref, moved_ref, weight_ref, bias_ref, own_ref, pre_ref):
@@ -262,9 +306,12 @@
     which = lax.shift_right_logical(ids[:, 0], 7)
     owned = cotangent.shape[1]
 
-    mine = pick(which, table, owners)
+    mine, placed = pick(core.reshape(1), which, ids, table, owners)
     moved = lax.all_to_all(mine, FEAT, split_axis=0, concat_axis=0, tiled=True)
-    aggregated = aggregate(which, block_lists[0].T.reshape(-1), block_counts[0], ids, table, tiles[0], owners)
+    lists = block_lists[0].T.reshape(-1)
+    aggregated = aggregate(
+        core.reshape(1), which, lists, block_counts[0], ids, table, placed, tiles[0], owners
+    )
     agg = lax.all_to_all(aggregated, FEAT, split_axis=0, concat_axis=0, tiled=True).reshape(-1, owned)
 
     first = (rank * (owned // BLOCK)).reshape(1)

time: 121 us -> 120 us (level)
  starting transfers between devices: 24.6 us -> 19.9 us
  Pallas kernels: 32.4 us -> 36.4 us
    ppermute x1, starting transfers between devices: 4.86 us -> 0.08 us  [on_device(): got = lax.ppermute(send, 'core', [(0, 1), (1, 0)])]
    pallas_call x2, Pallas kernels: 19.8 us -> 23.7 us  [the longest x1 12.9 us: aggregate(): pl.pallas_call(aggregate_kernel, in_specs=[smem, smem, smem, smem, vmem,...]
    all_to_all x1, waiting for transfers between devices: 14.2 us -> 12.5 us  [on_device(): moved = lax.all_to_all(mine, FEAT, split_axis=0, concat_axis=0, tiled=True)]
  transfers between devices with their start and end apart: 7 -> 7, of which waited for: 5 -> 5; matrix products, arithmetic and copies ran while one was open for 5% -> 6% of each run, Pallas kernels for 16% -> 14%
where the time goes in v3:
time: 120 us
  Pallas kernels  36.4 us (30%)
  waiting for transfers between devices  35.7 us (30%)
  starting transfers between devices  19.9 us (17%)
  blocking collectives  13.5 us (11%)
  local copies, waits for them, and re-layouts  8.36 us (7%)
  other arithmetic  4.28 us (4%)
  between operations  1.47 us (1%)
    all_to_all x1, waiting for transfers between devices, on_device(): lax.all_to_all(aggregated, FEAT, split_axis=0, concat_axis=0, tiled=True)  16.3 us
    all_to_all x1, blocking collectives, on_device(): lax.all_to_all((keep + got).astype(jnp.bfloat16), FEAT, split_axis=0, con...  13.5 us
    pallas_call x1, Pallas kernels, aggregate(): pl.pallas_call(aggregate_kernel, in_specs=[smem, smem, smem, smem, vmem,...  12.9 us
    all_to_all x1, waiting for transfers between devices, on_device(): moved = lax.all_to_all(mine, FEAT, split_axis=0, concat_axis=0, tiled=True)  12.5 us
    pallas_call x1, Pallas kernels, pick(): pl.pallas_call(pick_kernel, out_shape=[jax.ShapeDtypeStruct((owners, widt...  10.8 us
    pallas_call x1, Pallas kernels, finish(): pl.pallas_call(finish_kernel, in_specs=[pl.BlockSpec(memory_space=pltpu.S...  9.22 us
    all_to_all x1, starting transfers between devices, on_device(): moved = lax.all_to_all(mine, FEAT, split_axis=0, concat_axis=0, tiled=True)  8.61 us
    unnamed x19, local copies, waits for them, and re-layouts  8.23 us
  transfers between devices with their start and end apart: 7, of which 5 were waited for; matrix products, arithmetic and copies ran while one was open for 6% of the time, Pallas kernels for 14%

profile of v3, /device:TPU:1, one launch (start us, length us, event | category | flops | bytes accessed | tf_op | source)
XLA Modules:
  0.0 119.7 jit_solution(6053810702576383404)
XLA Ops:
  0.6 1.6 %fusion.which_ref = s32[256]{0:T(256)} fusion(s32[256,128]{1,0:T(8,128)} %bitcast.30), kind=kLoop, calls=%fused_computation.3 | loop fusion | flops 256 | bytes 2048 | tf_op jit(solution)/shard_map/shift_right_logical | solution.py:306
  2.2 10.8 %pick_own_blocks.1 = (bf16[16,64,1024]{2,1,0:T(8,128)(2,1)}, bf16[256,64,128]{2,1,0:T(8,128)(2,1)}) custom-call(s32[1]{0:T(128)} %bitcast.2.core_ref, s32[256]{0:T(256)} %fusion.which_ref, s32[256,128]{1,0:T(8,128)} %bitcast.31, bf16[64,32768]{1,0:T(8,128)(2,1)} %bitcast.35), custom_call_target="tpu_custom_call" | custom-call | bytes 4194304 | tf_op jit(solution)/shard_map/pick_own_blocks/pallas_call | solution.py:74
  13.1 8.6 %all-to-all-start = ((bf16[16,64,1024]{2,1,0:T(8,128)(2,1)}), bf16[16,64,1024]{2,1,0:T(8,128)(2,1)S(1)}, u32[]{:S(2)}, u32[]{:S(2)}) async-start(bf16[16,64,1024]{2,1,0:T(8,128)(2,1)} %get-tuple-element.10), calls=%async_computation | async-start | bytes 4194304 | tf_op jit(solution)/shard_map/all_to_all | solution.py:310
  22.3 12.9 %aggregate.1 = bf16[16,64,1024]{2,1,0:T(8,128)(2,1)} custom-call(s32[1]{0:T(128)} %bitcast.2.core_ref, s32[256]{0:T(256)} %fusion.which_ref, s32[384]{0:T(512)} %bitcast.41, s32[128]{0:T(128)} %bitcast.43, s32[256,128]{1,0:T(8,128)} %bitcast.32, bf16[64,32768]{1,0:T(8,128)(2,1)} %bitcast.36, bf16[256,64,128]{2,1,0:T(8,128)(2,1)} %get-tuple-element.12.placed_hbm, ...), custom_call_target="tpu_custom_call" | custom-call | flops 4000000000 | bytes 20971520 | tf_op jit(solution)/shard_map/aggregate/pallas_call | solution.py:155
  35.2 12.5 %all-to-all-done = bf16[16,64,1024]{2,1,0:T(8,128)(2,1)S(1)} async-done(((bf16[16,64,1024]{2,1,0:T(8,128)(2,1)}), bf16[16,64,1024]{2,1,0:T(8,128)(2,1)S(1)}, u32[]{:S(2)}, u32[]{:S(2)}) %all-to-all-start) | async-done | bytes 2097184 | tf_op jit(solution)/shard_map/all_to_all | solution.py:310
  47.7 4.4 %all-to-all-start.1 = ((bf16[16,64,1024]{2,1,0:T(8,128)(2,1)}), bf16[16,64,1024]{2,1,0:T(8,128)(2,1)}, u32[]{:S(2)}, u32[]{:S(2)}) async-start(bf16[16,64,1024]{2,1,0:T(8,128)(2,1)} %aggregate.1), calls=%async_computation.1 | async-start | bytes 4194304 | tf_op jit(solution)/shard_map/all_to_all | solution.py:315
  53.2 2.0 %copy.19 = bf16[1024,256]{0,1:T(8,128)(2,1)} copy(bf16[1024,256]{1,0:T(8,128)(2,1)} %param.17) | data formatting | bytes 1048576 | tf_op args[7]
  55.2 2.0 %copy.20 = bf16[1,1024,256]{1,2,0:T(8,128)(2,1)} copy(bf16[1,1024,256]{2,1,0:T(8,128)(2,1)} %param.19) | data formatting | bytes 1048576 | tf_op args[9]
  57.3 0.6 pad_add_fusion.place_ref
  57.9 3.5 %own_part.1 = (bf16[1024,1024]{1,0:T(8,128)(2,1)S(1)}, f32[256,1024]{1,0:T(8,128)S(1)}) custom-call(s32[1]{0:T(128)} %bitcast.3.first_ref, s32[256,128]{1,0:T(8,128)S(1)} %bitcast.33, bf16[1024,1024]{1,0:T(8,128)(2,1)S(1)} %bitcast.29, bf16[256,1024]{1,0:T(8,128)(2,1)S(1)} %bitcast.34, f32[256,1]{1,0:T(8,128)S(1)} %copy.18.bias_ref), custom_call_target="tpu_custom_call" | custom-call | flops 2000000000 | bytes 6291456 | tf_op jit(solution)/shard_map/own_part/pallas_call | solution.py:187
  61.4 1.3 %copy-done.1 = bf16[1024,1024]{1,0:T(8,128)(2,1)} copy-done((bf16[1024,1024]{1,0:T(8,128)(2,1)}, bf16[1024,1024]{1,0:T(8,128)(2,1)S(1)}, u32[]{:S(2)}) %copy-start.1) | copy-done | bytes 2097176
  62.7 1.0 copy-done.2
  63.7 16.3 %all-to-all-done.1 = bf16[16,64,1024]{2,1,0:T(8,128)(2,1)} async-done(((bf16[16,64,1024]{2,1,0:T(8,128)(2,1)}), bf16[16,64,1024]{2,1,0:T(8,128)(2,1)}, u32[]{:S(2)}, u32[]{:S(2)}) %all-to-all-start.1) | async-done | bytes 2097184 | tf_op jit(solution)/shard_map/all_to_all | solution.py:315
  80.0 9.2 %finish.1 = (bf16[256,1024]{1,0:T(8,128)(2,1)}, f32[16,64,256]{2,1,0:T(8,128)}, bf16[16,64,256]{2,1,0:T(8,128)(2,1)}) custom-call(s32[2]{0:T(128)} %pad_add_fusion.place_ref, f32[256,1024]{1,0:T(8,128)} %copy-done.2, bf16[1024,1024]{1,0:T(8,128)(2,1)} %bitcast.15.agg_hbm, bf16[1024,1024]{1,0:T(8,128)(2,1)} %copy-done.1, bf16[256,1024]{1,0:T(8,128)(2,1)} %bitcast.39, ...), custom_call_target="tpu_custom_call" | custom-call | flops 2000000000 | bytes 9437184 | tf_op jit(solution)/shard_map/finish/pallas_call | solution.py:281
  89.3 2.1 %collective-permute-done = bf16[16,64,256]{2,1,0:T(8,128)(2,1)S(1)} collective-permute-done((bf16[16,64,256]{2,1,0:T(8,128)(2,1)}, bf16[16,64,256]{2,1,0:T(8,128)(2,1)S(1)}, u32[]{:S(2)}, u32[]{:S(2)}) %collective-permute-start) | collective-permute-done | bytes 524320 | tf_op jit(solution)/shard_map/ppermute | solution.py:322
  91.4 1.4 %add_convert_fusion = bf16[16,64,256]{2,1,0:T(8,128)(2,1)S(1)} fusion(f32[16,64,256]{2,1,0:T(8,128)} %get-tuple-element.15, bf16[16,64,256]{2,1,0:T(8,128)(2,1)S(1)} %collective-permute-done), kind=kLoop, calls=%fused_computation.1 | loop fusion | flops 786432 | bytes 2097152 | tf_op jit(solution)/shard_map/convert_element_type | solution.py:323
  92.8 13.5 %all_to_all.15 = bf16[16,64,256]{2,1,0:T(8,128)(2,1)S(1)} all-to-all(bf16[16,64,256]{2,1,0:T(8,128)(2,1)S(1)} %add_convert_fusion), channel_id=1, replica_groups=mesh['z'=4,'y'=4,'x'=4,'core'=2] {'z','y'}, dimensions={0} | all-to-all | bytes 1048576 | tf_op jit(solution)/shard_map/all_to_all | solution.py:323
  106.4 1.3 %collective-permute-start.1 = (f32[64,256]{1,0:T(8,128)S(1)}, f32[64,256]{1,0:T(8,128)S(1)}, u32[]{:S(2)}, u32[]{:S(2)}) collective-permute-start(f32[64,256]{1,0:T(8,128)S(1)} %convert_reduce_fusion), channel_id=1, source_target_pairs={{0,2},{2,0},{4,6},{6,4},{1,3},{3,1},{5,7},{7,5},{8,10},{10,8},{12,... | collective-permute-start | bytes 196616 | tf_op jit(solution)/shard_map/ppermute | solution.py:325
  107.7 2.5 %collective-permute-start.2 = (f32[64,256]{1,0:T(8,128)S(1)}, f32[64,256]{1,0:T(8,128)S(1)}, u32[]{:S(2)}, u32[]{:S(2)}) collective-permute-start(f32[64,256]{1,0:T(8,128)S(1)} %convert_reduce_fusion), channel_id=1, source_target_pairs={{0,4},{2,6},{4,0},{6,2},{1,5},{3,7},{5,1},{7,3},{8,12},{10,14},{12... | collective-permute-start | bytes 196616 | tf_op jit(solution)/shard_map/ppermute | solution.py:325
  110.3 2.1 %collective-permute-done.2 = f32[64,256]{1,0:T(8,128)S(1)} collective-permute-done((f32[64,256]{1,0:T(8,128)S(1)}, f32[64,256]{1,0:T(8,128)S(1)}, u32[]{:S(2)}, u32[]{:S(2)}) %collective-permute-start.2) | collective-permute-done | bytes 65568 | tf_op jit(solution)/shard_map/ppermute | solution.py:325
  112.5 2.7 %collective-permute-done.3 = f32[64,256]{1,0:T(8,128)S(1)} collective-permute-done((f32[64,256]{1,0:T(8,128)S(1)}, f32[64,256]{1,0:T(8,128)S(1)}, u32[]{:S(2)}, u32[]{:S(2)}) %collective-permute-start.3) | collective-permute-done | bytes 65568 | tf_op jit(solution)/shard_map/ppermute | solution.py:325
  115.2 2.9 %collective-permute-start.4 = (f32[64,256]{1,0:T(8,128)S(1)}, f32[64,256]{1,0:T(8,128)S(1)}, u32[]{:S(2)}, u32[]{:S(2)}) collective-permute-start(f32[64,256]{1,0:T(8,128)S(1)} %add_add_fusion), channel_id=1, source_target_pairs={{0,1},{1,0},{2,3},{3,2},{4,5},{5,4},{6,7},{7,6},{8,9},{9,8},{10,11... | collective-permute-start | bytes 196616 | tf_op jit(solution)/shard_map/ppermute | solution.py:327
  118.0 1.0 copy.21
  119.0 0.7 broadcast_select_fusion
  (21 shorter events, 1.3 us)
Async XLA Ops:
  13.1 8.6 %copy-start.5 = (s32[1,128,3]{1,0,2:T(1,128)S(1)}, s32[1,128,3]{1,0,2:T(1,128)}, u32[]{:S(2)}) copy-start(s32[1,128,3]{1,0,2:T(1,128)} %param.12) | copy-start | bytes 4612
  13.1 34.6 %all-to-all-start = ((bf16[16,64,1024]{2,1,0:T(8,128)(2,1)}), bf16[16,64,1024]{2,1,0:T(8,128)(2,1)S(1)}, u32[]{:S(2)}, u32[]{:S(2)}) async-start(bf16[16,64,1024]{2,1,0:T(8,128)(2,1)} %get-tuple-element.10), calls=%async_computation | async-start | bytes 4194304 | tf_op jit(solution)/shard_map/all_to_all | solution.py:310
  35.2 17.0 %copy-start.3 = (bf16[1024,256]{1,0:T(8,128)(2,1)S(1)}, bf16[1024,256]{1,0:T(8,128)(2,1)}, u32[]{:S(2)}) copy-start(bf16[1024,256]{1,0:T(8,128)(2,1)} %param.16) | copy-start | bytes 1572868
  35.2 17.2 %copy-start.6 = (f32[256]{0:T(256)S(1)}, f32[256]{0:T(256)}, u32[]{:S(2)}) copy-start(f32[256]{0:T(256)} %param.18) | copy-start | bytes 3076
  47.7 32.3 %all-to-all-start.1 = ((bf16[16,64,1024]{2,1,0:T(8,128)(2,1)}), bf16[16,64,1024]{2,1,0:T(8,128)(2,1)}, u32[]{:S(2)}, u32[]{:S(2)}) async-start(bf16[16,64,1024]{2,1,0:T(8,128)(2,1)} %aggregate.1), calls=%async_computation.1 | async-start | bytes 4194304 | tf_op jit(solution)/shard_map/all_to_all | solution.py:315
  52.1 5.7 %copy-start = (s32[1,32768]{1,0:T(1,128)S(1)}, s32[1,32768]{1,0:T(1,128)}, u32[]{:S(2)}) copy-start(s32[1,32768]{1,0:T(1,128)} %param.11) | copy-start | bytes 393220
  61.4 1.3 %copy-start.1 = (bf16[1024,1024]{1,0:T(8,128)(2,1)}, bf16[1024,1024]{1,0:T(8,128)(2,1)S(1)}, u32[]{:S(2)}) copy-start(bf16[1024,1024]{1,0:T(8,128)(2,1)S(1)} %get-tuple-element.13.own_hbm) | copy-start | bytes 6291460
  62.7 1.0 copy-start.2
  89.2 28.8 %copy-start.4 = (bf16[256,1024]{1,0:T(8,128)(2,1)S(1)}, bf16[256,1024]{1,0:T(8,128)(2,1)}, u32[]{:S(2)}) copy-start(bf16[256,1024]{1,0:T(8,128)(2,1)} %get-tuple-element.14) | copy-start | bytes 1572868
  89.2 2.2 %collective-permute-start = (bf16[16,64,256]{2,1,0:T(8,128)(2,1)}, bf16[16,64,256]{2,1,0:T(8,128)(2,1)S(1)}, u32[]{:S(2)}, u32[]{:S(2)}) collective-permute-start(bf16[16,64,256]{2,1,0:T(8,128)(2,1)} %get-tuple-element.16), channel_id=1, source_target_pairs={{0,1},{1,0},{2,3},{3,2},{4,5},{5,4},{6,7},{7,6},{8,9},{9,8},{10,11... | collective-permute-start | bytes 1572872 | tf_op jit(solution)/shard_map/ppermute | solution.py:322
  106.4 3.9 %collective-permute-start.1 = (f32[64,256]{1,0:T(8,128)S(1)}, f32[64,256]{1,0:T(8,128)S(1)}, u32[]{:S(2)}, u32[]{:S(2)}) collective-permute-start(f32[64,256]{1,0:T(8,128)S(1)} %convert_reduce_fusion), channel_id=1, source_target_pairs={{0,2},{2,0},{4,6},{6,4},{1,3},{3,1},{5,7},{7,5},{8,10},{10,8},{12,... | collective-permute-start | bytes 196616 | tf_op jit(solution)/shard_map/ppermute | solution.py:325
  107.7 4.8 %collective-permute-start.2 = (f32[64,256]{1,0:T(8,128)S(1)}, f32[64,256]{1,0:T(8,128)S(1)}, u32[]{:S(2)}, u32[]{:S(2)}) collective-permute-start(f32[64,256]{1,0:T(8,128)S(1)} %convert_reduce_fusion), channel_id=1, source_target_pairs={{0,4},{2,6},{4,0},{6,2},{1,5},{3,7},{5,1},{7,3},{8,12},{10,14},{12... | collective-permute-start | bytes 196616 | tf_op jit(solution)/shard_map/ppermute | solution.py:325
  110.1 5.0 %collective-permute-start.3 = (f32[64,256]{1,0:T(8,128)S(1)}, f32[64,256]{1,0:T(8,128)S(1)}, u32[]{:S(2)}, u32[]{:S(2)}) collective-permute-start(f32[64,256]{1,0:T(8,128)S(1)} %convert_reduce_fusion), channel_id=1, source_target_pairs={{0,6},{2,4},{4,2},{6,0},{1,7},{3,5},{5,3},{7,1},{8,14},{10,12},{12... | collective-permute-start | bytes 196616 | tf_op jit(solution)/shard_map/ppermute | solution.py:325
  115.2 3.9 %collective-permute-start.4 = (f32[64,256]{1,0:T(8,128)S(1)}, f32[64,256]{1,0:T(8,128)S(1)}, u32[]{:S(2)}, u32[]{:S(2)}) collective-permute-start(f32[64,256]{1,0:T(8,128)S(1)} %add_add_fusion), channel_id=1, source_target_pairs={{0,1},{1,0},{2,3},{3,2},{4,5},{5,4},{6,7},{7,6},{8,9},{9,8},{10,11... | collective-permute-start | bytes 196616 | tf_op jit(solution)/shard_map/ppermute | solution.py:327

commit v4 on v2

v4 whole, which is shorter than its diff:
```python
import jax
import jax.numpy as jnp
from jax import lax
from jax.experimental import pallas as pl
from jax.experimental.pallas import tpu as pltpu
from jax.sharding import Mesh, PartitionSpec as P

BLOCK = 128
MIB = 1 << 20
WHOLE = 60 * MIB
FEAT = ("z", "y")
GRP = ("x", "core")
NT = (((1,), (1,)), ((), ()))
NN = (((1,), (0,)), ((), ()))


def dot(left, right, dims=NN):
    return lax.dot_general(left, right, dims, preferred_element_type=jnp.float32)


def selector(within):
    rows = lax.broadcasted_iota(jnp.int32, (BLOCK, BLOCK), 0)
    return jnp.where(rows == within, 1.0, 0.0).astype(jnp.bfloat16)


def place_blocks(which_ref, ids_ref, table, count, store):
    width = table.shape[0]

    def place(n, carry):
        w = which_ref[n]
        chosen = table[:, pl.ds(pl.multiple_of(w * BLOCK, BLOCK), BLOCK)].astype(jnp.float32)
        within = jnp.broadcast_to(ids_ref[pl.ds(n, 1), :] - w * BLOCK, (8, BLOCK))
        rows = [jnp.take_along_axis(chosen[i : i + 8], within, axis=1) for i in range(0, width, 8)]
        store(n, jnp.concatenate(rows, axis=0).astype(jnp.bfloat16))
        return carry

    lax.fori_loop(0, count, place, 0, unroll=16)


def pick_blocks(which_ref, table_hbm, out_ref, sem):
    owners, _, owned = out_ref.shape
    per = owned // BLOCK

    def start(b, carry):
        w = which_ref[b]
        pltpu.make_async_copy(
            table_hbm.at[:, pl.ds(pl.multiple_of(w * BLOCK, BLOCK), BLOCK)],
            out_ref.at[b // per, :, pl.ds(pl.multiple_of((b % per) * BLOCK, BLOCK), BLOCK)],
            sem,
        ).start()
        return carry

    lax.fori_loop(0, owners * per, start, 0, unroll=8)
    pltpu.make_async_copy(out_ref, out_ref, sem).wait()


def aggregate_blocks(
    which_ref, lists_ref, counts_ref, ids_ref, table_hbm, tiles_hbm, out_ref, source, table, tiles, sems
):
    blocks = ids_ref.shape[0]
    width = table.shape[0]
    owners = out_ref.shape[0]
    dst_blocks, slots = tiles.shape[0], tiles.shape[1]
    per = dst_blocks // owners

    def load_tiles(r):
        part = pl.ds(r * per, per)
        return pltpu.make_async_copy(tiles_hbm.at[part], tiles.at[part], sems.at[r])

    load_table = pltpu.make_async_copy(table_hbm, table, sems.at[owners])
    load_table.start()
    for r in range(owners):
        load_tiles(r).start()
    source[:blocks, width:] = jnp.ones((blocks, source.shape[1] - width, BLOCK), source.dtype)
    source[blocks] = jnp.zeros(source.shape[1:], source.dtype)
    load_table.wait()

    def store(n, rows):
        source[n, :width] = rows

    place_blocks(which_ref, ids_ref, table, blocks, store)

    def owner(r, carry):
        load_tiles(r).wait()
        for b in range(per):
            d = r * per + b
            count = counts_ref[d]
            used = [jnp.where(s < count, lists_ref[s * dst_blocks + d], blocks) for s in range(slots)]
            left = jnp.concatenate([source[u] for u in used], axis=1)
            right = jnp.concatenate([tiles[d, s] for s in range(slots)], axis=1)
            total = dot(left, right, NT)
            out_ref[r, :, b * BLOCK : (b + 1) * BLOCK] = (total[:width] / total[width : width + 1]).astype(
                jnp.bfloat16
            )
        return carry

    lax.fori_loop(0, owners, owner, 0)


def first_kernel(
    core_ref, which_ref, lists_ref, counts_ref, ids_ref, table_hbm, tiles_hbm, out_ref, source, table, tiles, sems
):
    @pl.when(core_ref[0] == 0)
    def _():
        pick_blocks(which_ref, table_hbm, out_ref, sems.at[0])

    @pl.when(core_ref[0] == 1)
    def _():
        aggregate_blocks(
            which_ref, lists_ref, counts_ref, ids_ref, table_hbm, tiles_hbm, out_ref, source, table, tiles, sems
        )


def second_kernel(
    core_ref, which_ref, lists_ref, counts_ref, ids_ref, table_hbm, tiles_hbm, out_ref, source, table, tiles, sems
):
    owners, _, owned = out_ref.shape
    per = owned // BLOCK

    @pl.when(core_ref[0] == 1)
    def _():
        load = pltpu.make_async_copy(table_hbm, table, sems.at[0])
        load.start()
        load.wait()

        def store(n, rows):
            out_ref[n // per, :, pl.ds(pl.multiple_of((n % per) * BLOCK, BLOCK), BLOCK)] = rows

        place_blocks(which_ref, ids_ref, table, owners * per, store)

    @pl.when(core_ref[0] == 0)
    def _():
        aggregate_blocks(
            which_ref, lists_ref, counts_ref, ids_ref, table_hbm, tiles_hbm, out_ref, source, table, tiles, sems
        )


def outgoing(kernel, core, which, lists, counts, ids, table, tiles, owners, name):
    width, rows = table.shape
    blocks = rows // BLOCK
    smem, vmem = pl.BlockSpec(memory_space=pltpu.SMEM), pl.BlockSpec(memory_space=pltpu.VMEM)
    anywhere = pl.BlockSpec(memory_space=pl.ANY)
    return pl.pallas_call(
        kernel,
        in_specs=[smem, smem, smem, smem, vmem, anywhere, anywhere],
        out_specs=vmem,
        out_shape=jax.ShapeDtypeStruct((owners, width, tiles.shape[0] // owners * BLOCK), jnp.bfloat16),
        scratch_shapes=[
            pltpu.VMEM((blocks + 1, width + 16, BLOCK), jnp.bfloat16),
            pltpu.VMEM(table.shape, jnp.bfloat16),
            pltpu.VMEM(tiles.shape, jnp.bfloat16),
            pltpu.SemaphoreType.DMA((owners + 1,)),
        ],
        compiler_params=pltpu.CompilerParams(vmem_limit_bytes=WHOLE),
        cost_estimate=pl.CostEstimate(flops=4_000_000_000, bytes_accessed=20 * MIB, transcendentals=0),
        name=name,
    )(core, which, lists, counts, ids, table, tiles)


def arrived_kernel(place_ref, ids_ref, moved_ref, weight_ref, bias_ref, rows_ref, pre_ref):
    step = pl.program_id(0)
    per = rows_ref.shape[1] // BLOCK
    in_order = lax.broadcasted_iota(jnp.int32, (1, BLOCK), 1)
    for b in range(per):
        row = place_ref[1] + step * per + b
        within = jnp.bitwise_and(ids_ref[pl.ds(row, 1), :], BLOCK - 1)
        within = jnp.where(place_ref[0] == 0, within, in_order)
        columns = slice(b * BLOCK, (b + 1) * BLOCK)
        rows_ref[:, columns] = dot(moved_ref[:, columns], selector(within)).astype(jnp.bfloat16)
    pre_ref[...] = dot(weight_ref[0], rows_ref[...]) + bias_ref[...]


def arrived(place, ids, moved, weights, bias):
    features, owned = moved.shape
    hidden = weights.shape[1]
    wide = 2 * BLOCK
    return pl.pallas_call(
        arrived_kernel,
        grid_spec=pltpu.PrefetchScalarGridSpec(
            num_scalar_prefetch=1,
            grid=(owned // wide,),
            in_specs=[
                pl.BlockSpec(memory_space=pltpu.VMEM),
                pl.BlockSpec((features, wide), lambda i, place: (0, i)),
                pl.BlockSpec((1, hidden, features), lambda i, place: (place[0], 0, 0)),
                pl.BlockSpec(memory_space=pltpu.VMEM),
            ],
            out_specs=[
                pl.BlockSpec((features, wide), lambda i, place: (0, i)),
                pl.BlockSpec((hidden, wide), lambda i, place: (0, i)),
            ],
        ),
        out_shape=[
            jax.ShapeDtypeStruct((features, owned), jnp.bfloat16),
            jax.ShapeDtypeStruct((hidden, owned), jnp.float32),
        ],
        compiler_params=pltpu.CompilerParams(vmem_limit_bytes=24 * MIB),
        cost_estimate=pl.CostEstimate(flops=2_000_000_000, bytes_accessed=6 * MIB, transcendentals=0),
        name="first_arrived",
    )(place, ids, moved, weights, bias)


def gelu_and_slope(pre):
    c, k = 0.7978845608028654, 0.044715
    square = pre * pre
    t = jnp.tanh(c * pre * (1.0 + k * square))
    half = 0.5 * (1.0 + t)
    slope = half + 0.5 * pre * (1.0 - t * t) * (c * (1.0 + 3.0 * k * square))
    return pre * half, slope


def finish_kernel(
    place_ref, pre_hbm, second_hbm, first_hbm, weights_hbm, upstream_hbm, hidden_ref, keep_ref, send_ref,
    pre_ref, second_ref, first_ref, weight_ref, upstream_ref, slope, sems,
):
    owned = pre_ref.shape[1]
    wide = 2 * BLOCK
    chunks = [slice(j, j + wide) for j in range(0, owned, wide)]
    core, limit = place_ref[0], place_ref[2]

    loads = [pltpu.make_async_copy(weights_hbm.at[1 - core], weight_ref, sems.at[0])]
    for j, columns in enumerate(chunks):
        loads.append(pltpu.make_async_copy(second_hbm.at[:, columns], second_ref.at[:, columns], sems.at[j + 1]))
    loads.append(pltpu.make_async_copy(pre_hbm, pre_ref, sems.at[len(chunks) + 1]))
    loads.append(pltpu.make_async_copy(upstream_hbm, upstream_ref, sems.at[len(chunks) + 2]))
    loads.append(pltpu.make_async_copy(first_hbm, first_ref, sems.at[len(chunks) + 3]))
    for load in loads:
        load.start()
    loads[0].wait()

    for j, columns in enumerate(chunks):
        loads[j + 1].wait()
        pre = dot(weight_ref[...], second_ref[:, columns])
        if j == 0:
            loads[-3].wait()
            loads[-2].wait()
        active, back = gelu_and_slope(pre + pre_ref[:, columns])
        positions = j * wide + lax.broadcasted_iota(jnp.int32, (1, wide), 1)
        valid = jnp.where(positions < limit, 1.0, 0.0)
        hidden_ref[:, columns] = (active * valid).astype(jnp.bfloat16)
        slope[:, columns] = (upstream_ref[:, columns].astype(jnp.float32) * back * valid).astype(jnp.bfloat16)
    loads[-1].wait()

    owners, share, _ = keep_ref.shape

    def grads(left_ref, out_ref):
        group = 4

        def part(i, carry):
            left = left_ref[pl.ds(pl.multiple_of(i * group * share, group * share), group * share), :]
            total = dot(left, slope[...], NT).reshape(group, share, -1)
            out_ref[pl.ds(i * group, group)] = total.astype(out_ref.dtype)
            return carry

        lax.fori_loop(0, owners // group, part, 0)

    grads(first_ref, keep_ref)
    grads(second_ref, send_ref)


def finish(place, pre, second, first, weights, upstream, owners):
    hidden, owned = pre.shape
    features = second.shape[0]
    part = (owners, features // owners, hidden)
    vmem, anywhere = pl.BlockSpec(memory_space=pltpu.VMEM), pl.BlockSpec(memory_space=pl.ANY)
    return pl.pallas_call(
        finish_kernel,
        in_specs=[pl.BlockSpec(memory_space=pltpu.SMEM)] + [anywhere] * 5,
        out_specs=[vmem] * 3,
        out_shape=[
            jax.ShapeDtypeStruct((hidden, owned), jnp.bfloat16),
            jax.ShapeDtypeStruct(part, jnp.float32),
            jax.ShapeDtypeStruct(part, jnp.bfloat16),
        ],
        scratch_shapes=[pltpu.VMEM(a.shape, a.dtype) for a in (pre, second, first, weights[0], upstream)]
        + [pltpu.VMEM((hidden, owned), jnp.bfloat16), pltpu.SemaphoreType.DMA((owned // (2 * BLOCK) + 4,))],
        compiler_params=pltpu.CompilerParams(vmem_limit_bytes=WHOLE),
        cost_estimate=pl.CostEstimate(flops=2_000_000_000, bytes_accessed=9 * MIB, transcendentals=262144),
        name="finish",
    )(place, pre, second, first, weights, upstream)


def on_device(
    node_table, node_ids, block_lists, block_counts, tiles, batch_sizes, w_self, w_neigh, bias, cotangent
):
    owners = lax.axis_size(FEAT)
    rank, core = lax.axis_index(FEAT), lax.axis_index("core")
    table = jnp.swapaxes(node_table[0], 0, 1)
    width = table.shape[0]
    ids = node_ids[0].reshape(-1, BLOCK)
    which = lax.shift_right_logical(ids[:, 0], 7)
    owned = cotangent.shape[1]

    lists = block_lists[0].T.reshape(-1)
    place = jnp.stack([core, rank * (owned // BLOCK), batch_sizes[0] - rank * owned])
    operands = (core.reshape(1), which, lists, block_counts[0], ids, table, tiles[0], owners)
    weights = jnp.stack([w_self.T, w_neigh.T])

    first = outgoing(first_kernel, *operands, "first_outgoing")
    moved = lax.all_to_all(first, FEAT, split_axis=0, concat_axis=0, tiled=True)
    second = outgoing(second_kernel, *operands, "second_outgoing")
    second = lax.all_to_all(second, FEAT, split_axis=0, concat_axis=0, tiled=True)
    first, pre = arrived(place, ids, moved.reshape(-1, owned), weights, bias[:, None])
    second = second.reshape(-1, owned)
    hidden, keep, send = finish(place, pre, second, first, weights, cotangent[0].T, owners)

    got = lax.ppermute(send, "core", [(0, 1), (1, 0)])
    parts = lax.all_to_all((keep + got).astype(jnp.bfloat16), FEAT, split_axis=0, concat_axis=0, tiled=True)
    total = jnp.sum(parts, axis=0, dtype=jnp.float32)
    others = [lax.ppermute(total, "x", [(i, i ^ k) for i in range(4)]) for k in (1, 2, 3)]
    total = (total + others[0]) + (others[1] + others[2])
    other = lax.ppermute(total, "core", [(0, 1), (1, 0)])
    first_core = core == 0
    return (
        hidden.T[None],
        jnp.where(first_core, total, other),
        jnp.where(first_core, other, total),
    )


def solution(mesh):
    axes = Mesh(mesh.devices.reshape(4, 4, 4, 2), ("z", "y", "x", "core"))
    in_specs = (
        P(GRP, None, FEAT),
        P(GRP, None),
        P(GRP, None, None),
        P(GRP, None),
        P(GRP, None, None, None, None),
        P(GRP),
        P(),
        P(),
        P(),
        P(GRP, FEAT, None),
    )
    out_specs = (P(GRP, FEAT, None), P(FEAT, None), P(FEAT, None))
    return jax.shard_map(on_device, mesh=axes, in_specs=in_specs, out_specs=out_specs, check_vma=False)
```

time: 121 us -> 118 us (0.975)
  starting transfers between devices: 24.6 us -> 20 us
  waiting for transfers between devices: 35.9 us -> 33.2 us
  Pallas kernels: 32.4 us -> 34.9 us
    ppermute x1, starting transfers between devices: 4.86 us -> 0.08 us  [on_device(): got = lax.ppermute(send, 'core', [(0, 1), (1, 0)])]
    all_to_all x2, waiting for transfers between devices: 29.4 us -> 26.2 us  [the longest x1 15.1 us: on_device(): moved = lax.all_to_all(first, FEAT, split_axis=0, concat_axis=0, tiled=True)]
    pallas_call x3, Pallas kernels: 23.2 us -> 26 us  [the longest x2 21.9 us: outgoing(): pl.pallas_call(kernel, in_specs=[smem, smem, smem, smem, vmem, anywhere,...]
    unnamed x19 -> x23, local copies, waits for them, and re-layouts: 8.22 us -> 8.73 us
  transfers between devices with their start and end apart: 7 -> 7, of which waited for: 5 -> 5; matrix products, arithmetic and copies ran while one was open for 5% -> 6% of each run, Pallas kernels for 16% -> 9%
where the time goes in v4:
time: 118 us
  Pallas kernels  34.9 us (30%)
  waiting for transfers between devices  33.2 us (28%)
  starting transfers between devices  20 us (17%)
  blocking collectives  14.4 us (12%)
  local copies, waits for them, and re-layouts  8.86 us (8%)
  other arithmetic  5.07 us (4%)
  between operations  1.47 us (1%)
    pallas_call x2, Pallas kernels, outgoing(): pl.pallas_call(kernel, in_specs=[smem, smem, smem, smem, vmem, anywhere,...  21.9 us
    all_to_all x1, waiting for transfers between devices, on_device(): moved = lax.all_to_all(first, FEAT, split_axis=0, concat_axis=0, tiled=True)  15.1 us
    all_to_all x1, blocking collectives, on_device(): lax.all_to_all((keep + got).astype(jnp.bfloat16), FEAT, split_axis=0, con...  14.4 us
    all_to_all x1, waiting for transfers between devices, on_device(): lax.all_to_all(second, FEAT, split_axis=0, concat_axis=0, tiled=True)  11.2 us
    pallas_call x1, Pallas kernels, finish(): pl.pallas_call(finish_kernel, in_specs=[pl.BlockSpec(memory_space=pltpu.S...  8.85 us
    unnamed x23, local copies, waits for them, and re-layouts  8.73 us
    all_to_all x1, starting transfers between devices, on_device(): moved = lax.all_to_all(first, FEAT, split_axis=0, concat_axis=0, tiled=True)  8.61 us
    ppermute x3, waiting for transfers between devices, on_device(): lax.ppermute(total, 'x', [(i, i ^ k) for i in range(4)])  4.83 us
  transfers between devices with their start and end apart: 7, of which 5 were waited for; matrix products, arithmetic and copies ran while one was open for 6% of the time, Pallas kernels for 9%

profile of v4, /device:TPU:1, one launch (start us, length us, event | category | flops | bytes accessed | tf_op | source)
XLA Modules:
  0.0 117.8 jit_solution(7727894393541773116)
XLA Ops:
  0.6 1.6 %fusion.which_ref = s32[256]{0:T(256)} fusion(s32[256,128]{1,0:T(8,128)} %bitcast.34), kind=kLoop, calls=%fused_computation.4 | loop fusion | flops 256 | bytes 2048 | tf_op jit(solution)/shard_map/shift_right_logical | solution.py:291
  2.2 1.3 %copy.24 = s32[1,128,3]{1,2,0:T(4,128)} copy(s32[1,128,3]{1,0,2:T(1,128)} %param.12) | data formatting | bytes 3072
  3.5 15.7 %first_outgoing.1 = bf16[16,64,1024]{2,1,0:T(8,128)(2,1)} custom-call(s32[1]{0:T(128)} %bitcast.core_ref, s32[256]{0:T(256)} %fusion.which_ref, s32[384]{0:T(512)} %bitcast.46, s32[128]{0:T(128)} %bitcast.48, s32[256,128]{1,0:T(8,128)} %bitcast.35, bf16[64,32768]{1,0:T(8,128)(2,1)} %bitcast.40, bf16[128,3,128,128]{3,2,1,0:T(8,128)(2,1)} %bitcast.38), custom_call_target="tpu_custom_call" | custom-call | flops 4000000000 | bytes 20971520 | tf_op jit(solution)/shard_map/first_outgoing/pallas_call | solution.py:143
  19.2 8.6 %all-to-all-start = ((bf16[16,64,1024]{2,1,0:T(8,128)(2,1)}), bf16[16,64,1024]{2,1,0:T(8,128)(2,1)S(1)}, u32[]{:S(2)}, u32[]{:S(2)}) async-start(bf16[16,64,1024]{2,1,0:T(8,128)(2,1)} %first_outgoing.1), calls=%async_computation | async-start | bytes 4194304 | tf_op jit(solution)/shard_map/all_to_all | solution.py:300
  27.8 6.2 %second_outgoing.1 = bf16[16,64,1024]{2,1,0:T(8,128)(2,1)} custom-call(s32[1]{0:T(128)} %bitcast.core_ref, s32[256]{0:T(256)} %fusion.which_ref, s32[384]{0:T(512)} %bitcast.47, s32[128]{0:T(128)} %bitcast.49, s32[256,128]{1,0:T(8,128)} %bitcast.36, bf16[64,32768]{1,0:T(8,128)(2,1)} %bitcast.41, bf16[128,3,128,128]{3,2,1,0:T(8,128)(2,1)} %bitcast.39), custom_call_target="tpu_custom_call" | custom-call | flops 4000000000 | bytes 20971520 | tf_op jit(solution)/shard_map/second_outgoing/pallas_call | solution.py:143
  34.1 15.1 %all-to-all-done = bf16[16,64,1024]{2,1,0:T(8,128)(2,1)S(1)} async-done(((bf16[16,64,1024]{2,1,0:T(8,128)(2,1)}), bf16[16,64,1024]{2,1,0:T(8,128)(2,1)S(1)}, u32[]{:S(2)}, u32[]{:S(2)}) %all-to-all-start) | async-done | bytes 2097184 | tf_op jit(solution)/shard_map/all_to_all | solution.py:300
  49.2 4.7 %all-to-all-start.1 = ((bf16[16,64,1024]{2,1,0:T(8,128)(2,1)}), bf16[16,64,1024]{2,1,0:T(8,128)(2,1)}, u32[]{:S(2)}, u32[]{:S(2)}) async-start(bf16[16,64,1024]{2,1,0:T(8,128)(2,1)} %second_outgoing.1), calls=%async_computation.1 | async-start | bytes 4194304 | tf_op jit(solution)/shard_map/all_to_all | solution.py:302
  54.6 1.0 copy.17
  55.6 1.0 copy.18
  56.7 2.1 %copy.20 = bf16[1,1024,256]{1,2,0:T(8,128)(2,1)} copy(bf16[1,1024,256]{2,1,0:T(8,128)(2,1)} %param.19) | data formatting | bytes 1048576 | tf_op args[9]
  58.9 1.3 %pad_maximum_fusion.weight_ref.weights_hbm = bf16[2,256,1024]{2,1,0:T(8,128)(2,1)S(1)} fusion(bf16[1,256,1024]{2,1,0:T(8,128)(2,1)} %bitcast.43, bf16[1,256,1024]{2,1,0:T(8,128)(2,1)} %bitcast.42), kind=kLoop, calls=%fused_computation | loop fusion | flops 524288 | bytes 2097152 | tf_op jit(solution)/shard_map/stack | solution.py:297
  60.2 4.1 %first_arrived.1 = (bf16[1024,1024]{1,0:T(8,128)(2,1)S(1)}, f32[256,1024]{1,0:T(8,128)S(1)}) custom-call(s32[3]{0:T(128)S(1)} %pad_add_fusion.place_ref, s32[256,128]{1,0:T(8,128)S(1)} %bitcast.37, bf16[1024,1024]{1,0:T(8,128)(2,1)S(1)} %bitcast.33, bf16[2,256,1024]{2,1,0:T(8,128)(2,1)S(1)} %pad_maximum_fusion.weight_ref.weights_hbm, f32[256,1]{1,0:T(8,128)S(1)} %copy.19.bias_ref), custom_call_target="tpu_custom_call" | custom-call | flops 2000000000 | bytes 6291456 | tf_op jit(solution)/shard_map/first_arrived/pallas_call | solution.py:177
  64.3 1.3 %copy-done.3 = bf16[1024,1024]{1,0:T(8,128)(2,1)} copy-done((bf16[1024,1024]{1,0:T(8,128)(2,1)}, bf16[1024,1024]{1,0:T(8,128)(2,1)S(1)}, u32[]{:S(2)}) %copy-start.3) | copy-done | bytes 2097176
  65.7 1.0 copy-done.4
  66.7 11.2 %all-to-all-done.1 = bf16[16,64,1024]{2,1,0:T(8,128)(2,1)} async-done(((bf16[16,64,1024]{2,1,0:T(8,128)(2,1)}), bf16[16,64,1024]{2,1,0:T(8,128)(2,1)}, u32[]{:S(2)}, u32[]{:S(2)}) %all-to-all-start.1) | async-done | bytes 2097184 | tf_op jit(solution)/shard_map/all_to_all | solution.py:302
  77.8 8.9 %finish.1 = (bf16[256,1024]{1,0:T(8,128)(2,1)}, f32[16,64,256]{2,1,0:T(8,128)}, bf16[16,64,256]{2,1,0:T(8,128)(2,1)}) custom-call(s32[3]{0:T(128)} %copy-done.2, f32[256,1024]{1,0:T(8,128)} %copy-done.4, bf16[1024,1024]{1,0:T(8,128)(2,1)} %bitcast.19.second_hbm, bf16[1024,1024]{1,0:T(8,128)(2,1)} %copy-done.3, bf16[2,256,1024]{2,1,0:T(8,128)(2,1)} %copy-done.1, ...), custom_call_target="tpu_custom_call" | custom-call | flops 2000000000 | bytes 9437184 | tf_op jit(solution)/shard_map/finish/pallas_call | solution.py:266
  86.8 2.1 %collective-permute-done = bf16[16,64,256]{2,1,0:T(8,128)(2,1)S(1)} collective-permute-done((bf16[16,64,256]{2,1,0:T(8,128)(2,1)}, bf16[16,64,256]{2,1,0:T(8,128)(2,1)S(1)}, u32[]{:S(2)}, u32[]{:S(2)}) %collective-permute-start) | collective-permute-done | bytes 524320 | tf_op jit(solution)/shard_map/ppermute | solution.py:307
  88.9 1.4 %add_convert_fusion = bf16[16,64,256]{2,1,0:T(8,128)(2,1)S(1)} fusion(f32[16,64,256]{2,1,0:T(8,128)} %get-tuple-element.11, bf16[16,64,256]{2,1,0:T(8,128)(2,1)S(1)} %collective-permute-done), kind=kLoop, calls=%fused_computation.2 | loop fusion | flops 786432 | bytes 2097152 | tf_op jit(solution)/shard_map/convert_element_type | solution.py:308
  90.3 14.4 %all_to_all.15 = bf16[16,64,256]{2,1,0:T(8,128)(2,1)S(1)} all-to-all(bf16[16,64,256]{2,1,0:T(8,128)(2,1)S(1)} %add_convert_fusion), channel_id=1, replica_groups=mesh['z'=4,'y'=4,'x'=4,'core'=2] {'z','y'}, dimensions={0} | all-to-all | bytes 1048576 | tf_op jit(solution)/shard_map/all_to_all | solution.py:308
  104.7 1.3 %collective-permute-start.1 = (f32[64,256]{1,0:T(8,128)S(1)}, f32[64,256]{1,0:T(8,128)S(1)}, u32[]{:S(2)}, u32[]{:S(2)}) collective-permute-start(f32[64,256]{1,0:T(8,128)S(1)} %convert_reduce_fusion), channel_id=1, source_target_pairs={{0,2},{2,0},{4,6},{6,4},{1,3},{3,1},{5,7},{7,5},{8,10},{10,8},{12,... | collective-permute-start | bytes 196616 | tf_op jit(solution)/shard_map/ppermute | solution.py:310
  106.0 2.5 %collective-permute-start.2 = (f32[64,256]{1,0:T(8,128)S(1)}, f32[64,256]{1,0:T(8,128)S(1)}, u32[]{:S(2)}, u32[]{:S(2)}) collective-permute-start(f32[64,256]{1,0:T(8,128)S(1)} %convert_reduce_fusion), channel_id=1, source_target_pairs={{0,4},{2,6},{4,0},{6,2},{1,5},{3,7},{5,1},{7,3},{8,12},{10,14},{12... | collective-permute-start | bytes 196616 | tf_op jit(solution)/shard_map/ppermute | solution.py:310
  108.6 2.2 %collective-permute-done.2 = f32[64,256]{1,0:T(8,128)S(1)} collective-permute-done((f32[64,256]{1,0:T(8,128)S(1)}, f32[64,256]{1,0:T(8,128)S(1)}, u32[]{:S(2)}, u32[]{:S(2)}) %collective-permute-start.2) | collective-permute-done | bytes 65568 | tf_op jit(solution)/shard_map/ppermute | solution.py:310
  110.8 2.7 %collective-permute-done.3 = f32[64,256]{1,0:T(8,128)S(1)} collective-permute-done((f32[64,256]{1,0:T(8,128)S(1)}, f32[64,256]{1,0:T(8,128)S(1)}, u32[]{:S(2)}, u32[]{:S(2)}) %collective-permute-start.3) | collective-permute-done | bytes 65568 | tf_op jit(solution)/shard_map/ppermute | solution.py:310
  113.5 2.7 %collective-permute-start.4 = (f32[64,256]{1,0:T(8,128)S(1)}, f32[64,256]{1,0:T(8,128)S(1)}, u32[]{:S(2)}, u32[]{:S(2)}) collective-permute-start(f32[64,256]{1,0:T(8,128)S(1)} %add_add_fusion), channel_id=1, source_target_pairs={{0,1},{1,0},{2,3},{3,2},{4,5},{5,4},{6,7},{7,6},{8,9},{9,8},{10,11... | collective-permute-start | bytes 196616 | tf_op jit(solution)/shard_map/ppermute | solution.py:312
  (26 shorter events, 2.3 us)
Async XLA Ops:
  19.2 30.0 %all-to-all-start = ((bf16[16,64,1024]{2,1,0:T(8,128)(2,1)}), bf16[16,64,1024]{2,1,0:T(8,128)(2,1)S(1)}, u32[]{:S(2)}, u32[]{:S(2)}) async-start(bf16[16,64,1024]{2,1,0:T(8,128)(2,1)} %first_outgoing.1), calls=%async_computation | async-start | bytes 4194304 | tf_op jit(solution)/shard_map/all_to_all | solution.py:300
  34.1 20.5 %copy-start.5 = (bf16[1024,256]{1,0:T(8,128)(2,1)S(1)}, bf16[1024,256]{1,0:T(8,128)(2,1)}, u32[]{:S(2)}) copy-start(bf16[1024,256]{1,0:T(8,128)(2,1)} %param.16) | copy-start | bytes 1572868
  34.1 21.5 %copy-start.6 = (bf16[1024,256]{1,0:T(8,128)(2,1)S(1)}, bf16[1024,256]{1,0:T(8,128)(2,1)}, u32[]{:S(2)}) copy-start(bf16[1024,256]{1,0:T(8,128)(2,1)} %param.17) | copy-start | bytes 1572868
  49.2 28.6 %all-to-all-start.1 = ((bf16[16,64,1024]{2,1,0:T(8,128)(2,1)}), bf16[16,64,1024]{2,1,0:T(8,128)(2,1)}, u32[]{:S(2)}, u32[]{:S(2)}) async-start(bf16[16,64,1024]{2,1,0:T(8,128)(2,1)} %second_outgoing.1), calls=%async_computation.1 | async-start | bytes 4194304 | tf_op jit(solution)/shard_map/all_to_all | solution.py:302
  53.9 2.7 %copy-start.8 = (f32[256]{0:T(256)S(1)}, f32[256]{0:T(256)}, u32[]{:S(2)}) copy-start(f32[256]{0:T(256)} %param.18) | copy-start | bytes 3076
  55.6 4.6 %copy-start = (s32[1,32768]{1,0:T(1,128)S(1)}, s32[1,32768]{1,0:T(1,128)}, u32[]{:S(2)}) copy-start(s32[1,32768]{1,0:T(1,128)} %param.11) | copy-start | bytes 393220
  58.9 5.4 %copy-start.2 = (s32[3]{0:T(128)}, s32[3]{0:T(128)S(1)}, u32[]{:S(2)}) copy-start(s32[3]{0:T(128)S(1)} %pad_add_fusion.place_ref) | copy-start | bytes 40
  60.2 4.1 %copy-start.1 = (bf16[2,256,1024]{2,1,0:T(8,128)(2,1)}, bf16[2,256,1024]{2,1,0:T(8,128)(2,1)S(1)}, u32[]{:S(2)}) copy-start(bf16[2,256,1024]{2,1,0:T(8,128)(2,1)S(1)} %pad_maximum_fusion.weight_ref.weights_hbm) | copy-start | bytes 3145732
  64.3 1.3 %copy-start.3 = (bf16[1024,1024]{1,0:T(8,128)(2,1)}, bf16[1024,1024]{1,0:T(8,128)(2,1)S(1)}, u32[]{:S(2)}) copy-start(bf16[1024,1024]{1,0:T(8,128)(2,1)S(1)} %get-tuple-element.9.first_hbm) | copy-start | bytes 6291460
  65.7 1.0 copy-start.4
  86.7 29.5 %copy-start.7 = (bf16[256,1024]{1,0:T(8,128)(2,1)S(1)}, bf16[256,1024]{1,0:T(8,128)(2,1)}, u32[]{:S(2)}) copy-start(bf16[256,1024]{1,0:T(8,128)(2,1)} %get-tuple-element.10) | copy-start | bytes 1572868
  86.7 2.2 %collective-permute-start = (bf16[16,64,256]{2,1,0:T(8,128)(2,1)}, bf16[16,64,256]{2,1,0:T(8,128)(2,1)S(1)}, u32[]{:S(2)}, u32[]{:S(2)}) collective-permute-start(bf16[16,64,256]{2,1,0:T(8,128)(2,1)} %get-tuple-element.12), channel_id=1, source_target_pairs={{0,1},{1,0},{2,3},{3,2},{4,5},{5,4},{6,7},{7,6},{8,9},{9,8},{10,11... | collective-permute-start | bytes 1572872 | tf_op jit(solution)/shard_map/ppermute | solution.py:307
  104.7 3.9 %collective-permute-start.1 = (f32[64,256]{1,0:T(8,128)S(1)}, f32[64,256]{1,0:T(8,128)S(1)}, u32[]{:S(2)}, u32[]{:S(2)}) collective-permute-start(f32[64,256]{1,0:T(8,128)S(1)} %convert_reduce_fusion), channel_id=1, source_target_pairs={{0,2},{2,0},{4,6},{6,4},{1,3},{3,1},{5,7},{7,5},{8,10},{10,8},{12,... | collective-permute-start | bytes 196616 | tf_op jit(solution)/shard_map/ppermute | solution.py:310
  106.0 4.8 %collective-permute-start.2 = (f32[64,256]{1,0:T(8,128)S(1)}, f32[64,256]{1,0:T(8,128)S(1)}, u32[]{:S(2)}, u32[]{:S(2)}) collective-permute-start(f32[64,256]{1,0:T(8,128)S(1)} %convert_reduce_fusion), channel_id=1, source_target_pairs={{0,4},{2,6},{4,0},{6,2},{1,5},{3,7},{5,1},{7,3},{8,12},{10,14},{12... | collective-permute-start | bytes 196616 | tf_op jit(solution)/shard_map/ppermute | solution.py:310
  108.4 5.0 %collective-permute-start.3 = (f32[64,256]{1,0:T(8,128)S(1)}, f32[64,256]{1,0:T(8,128)S(1)}, u32[]{:S(2)}, u32[]{:S(2)}) collective-permute-start(f32[64,256]{1,0:T(8,128)S(1)} %convert_reduce_fusion), channel_id=1, source_target_pairs={{0,6},{2,4},{4,2},{6,0},{1,7},{3,5},{5,3},{7,1},{8,14},{10,12},{12... | collective-permute-start | bytes 196616 | tf_op jit(solution)/shard_map/ppermute | solution.py:310
  113.5 3.7 %collective-permute-start.4 = (f32[64,256]{1,0:T(8,128)S(1)}, f32[64,256]{1,0:T(8,128)S(1)}, u32[]{:S(2)}, u32[]{:S(2)}) collective-permute-start(f32[64,256]{1,0:T(8,128)S(1)} %add_add_fusion), channel_id=1, source_target_pairs={{0,1},{1,0},{2,3},{3,2},{4,5},{5,4},{6,7},{7,6},{8,9},{9,8},{10,11... | collective-permute-start | bytes 196616 | tf_op jit(solution)/shard_map/ppermute | solution.py:312

commit v5 on v4

v5 whole, which is shorter than its diff:
```python
import jax
import jax.numpy as jnp
from jax import lax
from jax.experimental import pallas as pl
from jax.experimental.pallas import tpu as pltpu
from jax.sharding import Mesh, PartitionSpec as P

BLOCK = 128
MIB = 1 << 20
WHOLE = 60 * MIB
FEAT = ("z", "y")
GRP = ("x", "core")
NT = (((1,), (1,)), ((), ()))
NN = (((1,), (0,)), ((), ()))


def dot(left, right, dims=NN):
    return lax.dot_general(left, right, dims, preferred_element_type=jnp.float32)


def selector(within):
    rows = lax.broadcasted_iota(jnp.int32, (BLOCK, BLOCK), 0)
    return jnp.where(rows == within, 1.0, 0.0).astype(jnp.bfloat16)


def read_blocks(ids_ref, vector, which, sem):
    lanes = lax.broadcasted_iota(jnp.int32, (vector.shape[0], BLOCK), 1)
    first = jnp.where(lanes == 0, 1.0, 0.0).astype(jnp.bfloat16)
    blocks = lax.shift_right_logical(ids_ref[...], 7).astype(jnp.float32).astype(jnp.bfloat16)
    vector[...] = dot(first, blocks, NT).astype(jnp.int32)
    copy = pltpu.make_async_copy(vector, which, sem)
    copy.start()
    copy.wait()


def block_of(table, w):
    return table[:, pl.ds(pl.multiple_of(w * BLOCK, BLOCK), BLOCK)]


def in_run_order(chosen, ids_row):
    within = jnp.broadcast_to(jnp.bitwise_and(ids_row, BLOCK - 1), (8, BLOCK))
    chosen = chosen.astype(jnp.float32)
    rows = [jnp.take_along_axis(chosen[i : i + 8], within, axis=1) for i in range(0, chosen.shape[0], 8)]
    return jnp.concatenate(rows, axis=0).astype(jnp.bfloat16)


def pick_blocks(ids_ref, table_hbm, out_hbm, rows, vector, which, load, leave):
    owners, _, owned = rows.shape
    per = owned // BLOCK
    read_blocks(ids_ref, vector, which, load.at[owners])

    def start(r, carry):
        for b in range(per):
            pltpu.make_async_copy(
                block_of(table_hbm.at, which[0, r * per + b]),
                rows.at[r, :, b * BLOCK : (b + 1) * BLOCK],
                load.at[r],
            ).start()
        return carry

    lax.fori_loop(0, owners, start, 0)
    for r in range(owners):
        pltpu.make_async_copy(rows.at[r], rows.at[r], load.at[r]).wait()
        pltpu.make_async_copy(rows.at[r], out_hbm.at[r], leave.at[r]).start()
    for r in range(owners):
        pltpu.make_async_copy(rows.at[r], out_hbm.at[r], leave.at[r]).wait()


def place_blocks(ids_ref, table_hbm, out_hbm, rows, table, vector, which, load, leave):
    owners, _, owned = rows.shape
    per = owned // BLOCK
    known = table.at[:, pl.ds(0, table_hbm.shape[1])]
    load_table = pltpu.make_async_copy(table_hbm, known, load.at[0])
    load_table.start()
    read_blocks(ids_ref, vector, which, load.at[owners])
    load_table.wait()

    def owner(r, carry):
        placed = []
        for b in range(per):
            n = r * per + b
            placed.append(in_run_order(block_of(table, which[0, n]), ids_ref[pl.ds(n, 1), :]))
        for b in range(per):
            rows[r, :, b * BLOCK : (b + 1) * BLOCK] = placed[b]
        pltpu.make_async_copy(rows.at[r], out_hbm.at[r], leave.at[r]).start()
        return carry

    lax.fori_loop(0, owners, owner, 0)
    for r in range(owners):
        pltpu.make_async_copy(rows.at[r], out_hbm.at[r], leave.at[r]).wait()


def aggregate_blocks(
    lists_ref, counts_ref, ids_ref, table_hbm, tiles_hbm, out_hbm, rows, table, tiles, vector, which, load, leave
):
    blocks = ids_ref.shape[0]
    owners, width, _ = rows.shape
    dst_blocks, slots = tiles.shape[0], tiles.shape[1]
    per = dst_blocks // owners
    together = 4

    def load_tiles(r):
        part = pl.ds(r * per, per)
        return pltpu.make_async_copy(tiles_hbm.at[part], tiles.at[part], load.at[r])

    known = table.at[:, pl.ds(0, table_hbm.shape[1])]
    load_table = pltpu.make_async_copy(table_hbm, known, load.at[owners + 1])
    load_table.start()
    for r in range(owners):
        load_tiles(r).start()
    table[:, table_hbm.shape[1] :] = jnp.zeros((width, BLOCK), table.dtype)
    read_blocks(ids_ref, vector, which, load.at[owners])
    load_table.wait()

    def one(d):
        count = counts_ref[0, d]
        left = []
        for s in range(slots):
            used = s < count
            n = lists_ref[s, 0, d]
            w = jnp.where(used, which[0, n], blocks)
            source = in_run_order(block_of(table, w), ids_ref[pl.ds(n, 1), :])
            ones = jnp.full((16, BLOCK), jnp.where(used, 1.0, 0.0), jnp.float32).astype(jnp.bfloat16)
            left.append(jnp.concatenate([source, ones], axis=0))
        right = jnp.concatenate([tiles[d, s] for s in range(slots)], axis=1)
        total = dot(jnp.concatenate(left, axis=1), right, NT)
        return (total[:width] * (1.0 / total[width : width + 1])).astype(jnp.bfloat16)

    def some(i, carry):
        for k in range(together):
            load_tiles(i * together + k).wait()
        results = [one(i * together * per + k) for k in range(together * per)]
        for k in range(together * per):
            rows[i * together + k // per, :, (k % per) * BLOCK : (k % per + 1) * BLOCK] = results[k]
        for k in range(together):
            r = i * together + k
            pltpu.make_async_copy(rows.at[r], out_hbm.at[r], leave.at[r]).start()
        return carry

    lax.fori_loop(0, owners // together, some, 0)
    for r in range(owners):
        pltpu.make_async_copy(rows.at[r], out_hbm.at[r], leave.at[r]).wait()


def first_kernel(
    core_ref, lists_ref, counts_ref, ids_ref, table_hbm, tiles_hbm, out_hbm,
    rows, table, tiles, vector, which, load, leave,
):
    @pl.when(core_ref[0] == 0)
    def _():
        pick_blocks(ids_ref, table_hbm, out_hbm, rows, vector, which, load, leave)

    @pl.when(core_ref[0] == 1)
    def _():
        aggregate_blocks(
            lists_ref, counts_ref, ids_ref, table_hbm, tiles_hbm, out_hbm,
            rows, table, tiles, vector, which, load, leave,
        )


def second_kernel(
    core_ref, lists_ref, counts_ref, ids_ref, table_hbm, tiles_hbm, out_hbm,
    rows, table, tiles, vector, which, load, leave,
):
    @pl.when(core_ref[0] == 1)
    def _():
        place_blocks(ids_ref, table_hbm, out_hbm, rows, table, vector, which, load, leave)

    @pl.when(core_ref[0] == 0)
    def _():
        aggregate_blocks(
            lists_ref, counts_ref, ids_ref, table_hbm, tiles_hbm, out_hbm,
            rows, table, tiles, vector, which, load, leave,
        )


def outgoing(kernel, core, lists, counts, ids, table, tiles, owners, name):
    width, rows = table.shape
    blocks = rows // BLOCK
    smem, vmem = pl.BlockSpec(memory_space=pltpu.SMEM), pl.BlockSpec(memory_space=pltpu.VMEM)
    anywhere = pl.BlockSpec(memory_space=pl.ANY)
    out = (owners, width, tiles.shape[0] // owners * BLOCK)
    return pl.pallas_call(
        kernel,
        in_specs=[smem, smem, smem, vmem, anywhere, anywhere],
        out_specs=anywhere,
        out_shape=jax.ShapeDtypeStruct(out, jnp.bfloat16),
        scratch_shapes=[
            pltpu.VMEM(out, jnp.bfloat16),
            pltpu.VMEM((width, rows + BLOCK), jnp.bfloat16),
            pltpu.VMEM(tiles.shape, jnp.bfloat16),
            pltpu.VMEM((8, blocks), jnp.int32),
            pltpu.SMEM((8, blocks), jnp.int32),
            pltpu.SemaphoreType.DMA((owners + 2,)),
            pltpu.SemaphoreType.DMA((owners,)),
        ],
        compiler_params=pltpu.CompilerParams(vmem_limit_bytes=WHOLE),
        cost_estimate=pl.CostEstimate(flops=4_000_000_000, bytes_accessed=20 * MIB, transcendentals=0),
        name=name,
    )(core, lists, counts, ids, table, tiles)


def arrived_kernel(place_ref, ids_ref, moved_ref, weight_ref, bias_ref, rows_ref, pre_ref):
    step = pl.program_id(0)
    per = rows_ref.shape[1] // BLOCK
    in_order = lax.broadcasted_iota(jnp.int32, (1, BLOCK), 1)
    for b in range(per):
        row = place_ref[1] + step * per + b
        within = jnp.bitwise_and(ids_ref[pl.ds(row, 1), :], BLOCK - 1)
        within = jnp.where(place_ref[0] == 0, within, in_order)
        columns = slice(b * BLOCK, (b + 1) * BLOCK)
        rows_ref[:, columns] = dot(moved_ref[:, columns], selector(within)).astype(jnp.bfloat16)
    pre_ref[...] = dot(weight_ref[0], rows_ref[...]) + bias_ref[...]


def arrived(place, ids, moved, weights, bias):
    features, owned = moved.shape
    hidden = weights.shape[1]
    wide = 2 * BLOCK
    return pl.pallas_call(
        arrived_kernel,
        grid_spec=pltpu.PrefetchScalarGridSpec(
            num_scalar_prefetch=1,
            grid=(owned // wide,),
            in_specs=[
                pl.BlockSpec(memory_space=pltpu.VMEM),
                pl.BlockSpec((features, wide), lambda i, place: (0, i)),
                pl.BlockSpec((1, hidden, features), lambda i, place: (place[0], 0, 0)),
                pl.BlockSpec(memory_space=pltpu.VMEM),
            ],
            out_specs=[
                pl.BlockSpec((features, wide), lambda i, place: (0, i)),
                pl.BlockSpec((hidden, wide), lambda i, place: (0, i)),
            ],
        ),
        out_shape=[
            jax.ShapeDtypeStruct((features, owned), jnp.bfloat16),
            jax.ShapeDtypeStruct((hidden, owned), jnp.float32),
        ],
        compiler_params=pltpu.CompilerParams(vmem_limit_bytes=24 * MIB),
        cost_estimate=pl.CostEstimate(flops=2_000_000_000, bytes_accessed=6 * MIB, transcendentals=0),
        name="first_arrived",
    )(place, ids, moved, weights, bias)


def gelu_and_slope(pre):
    c, k = 0.7978845608028654, 0.044715
    square = pre * pre
    t = jnp.tanh(c * pre * (1.0 + k * square))
    half = 0.5 * (1.0 + t)
    slope = half + 0.5 * pre * (1.0 - t * t) * (c * (1.0 + 3.0 * k * square))
    return pre * half, slope


def finish_kernel(
    place_ref, pre_hbm, second_hbm, first_hbm, weights_hbm, upstream_hbm, hidden_hbm, keep_hbm, send_hbm,
    pre_ref, second_ref, first_ref, weight_ref, upstream_ref, slope, hidden_ref, keep_ref, send_ref, load, leave,
):
    owned = pre_ref.shape[1]
    wide = 2 * BLOCK
    core, limit = place_ref[0], place_ref[2]

    load_weight = pltpu.make_async_copy(weights_hbm.at[1 - core], weight_ref, load.at[0])
    load_second = pltpu.make_async_copy(second_hbm, second_ref, load.at[1])
    load_pre = pltpu.make_async_copy(pre_hbm, pre_ref, load.at[2])
    load_upstream = pltpu.make_async_copy(upstream_hbm, upstream_ref, load.at[3])
    load_first = pltpu.make_async_copy(first_hbm, first_ref, load.at[4])
    early = [load_weight, load_second, load_pre, load_upstream]
    for copy in early + [load_first]:
        copy.start()
    for copy in early:
        copy.wait()

    for j in range(0, owned, wide):
        columns = slice(j, j + wide)
        active, back = gelu_and_slope(dot(weight_ref[...], second_ref[:, columns]) + pre_ref[:, columns])
        positions = j + lax.broadcasted_iota(jnp.int32, (1, wide), 1)
        valid = jnp.where(positions < limit, 1.0, 0.0)
        hidden_ref[:, columns] = (active * valid).astype(jnp.bfloat16)
        slope[:, columns] = (upstream_ref[:, columns].astype(jnp.float32) * back * valid).astype(jnp.bfloat16)
    leave_hidden = pltpu.make_async_copy(hidden_ref, hidden_hbm, leave.at[0])
    leave_hidden.start()

    owners, share, _ = keep_ref.shape
    group = 4

    def grads(left_ref, out_ref):
        for i in range(0, owners, group):
            total = dot(left_ref[i * share : (i + group) * share, :], slope[...], NT)
            out_ref[i : i + group] = total.reshape(group, share, -1).astype(out_ref.dtype)

    grads(second_ref, send_ref)
    leave_send = pltpu.make_async_copy(send_ref, send_hbm, leave.at[1])
    leave_send.start()
    load_first.wait()
    grads(first_ref, keep_ref)
    leave_keep = pltpu.make_async_copy(keep_ref, keep_hbm, leave.at[2])
    leave_keep.start()
    leave_hidden.wait()
    leave_send.wait()
    leave_keep.wait()


def finish(place, pre, second, first, weights, upstream, owners):
    hidden, owned = pre.shape
    features = second.shape[0]
    part = (owners, features // owners, hidden)
    anywhere = pl.BlockSpec(memory_space=pl.ANY)
    outs = [
        jax.ShapeDtypeStruct((hidden, owned), jnp.bfloat16),
        jax.ShapeDtypeStruct(part, jnp.float32),
        jax.ShapeDtypeStruct(part, jnp.bfloat16),
    ]
    return pl.pallas_call(
        finish_kernel,
        in_specs=[pl.BlockSpec(memory_space=pltpu.SMEM)] + [anywhere] * 5,
        out_specs=[anywhere] * 3,
        out_shape=outs,
        scratch_shapes=[pltpu.VMEM(a.shape, a.dtype) for a in (pre, second, first, weights[0], upstream)]
        + [pltpu.VMEM((hidden, owned), jnp.bfloat16)]
        + [pltpu.VMEM(a.shape, a.dtype) for a in outs]
        + [pltpu.SemaphoreType.DMA((5,)), pltpu.SemaphoreType.DMA((3,))],
        compiler_params=pltpu.CompilerParams(vmem_limit_bytes=WHOLE),
        cost_estimate=pl.CostEstimate(flops=2_000_000_000, bytes_accessed=9 * MIB, transcendentals=262144),
        name="finish",
    )(place, pre, second, first, weights, upstream)


def on_device(
    node_table, node_ids, block_lists, block_counts, tiles, batch_sizes, w_self, w_neigh, bias, cotangent
):
    owners = lax.axis_size(FEAT)
    rank, core = lax.axis_index(FEAT), lax.axis_index("core")
    table = jnp.swapaxes(node_table[0], 0, 1)
    width = table.shape[0]
    ids = node_ids[0].reshape(-1, BLOCK)
    owned = cotangent.shape[1]

    lists = jnp.transpose(block_lists, (2, 0, 1))
    place = jnp.stack([core, rank * (owned // BLOCK), batch_sizes[0] - rank * owned])
    operands = (core.reshape(1), lists, block_counts, ids, table, tiles[0], owners)
    weights = jnp.stack([w_self.T, w_neigh.T])

    first = outgoing(first_kernel, *operands, "first_outgoing")
    moved = lax.all_to_all(first, FEAT, split_axis=0, concat_axis=0, tiled=True)
    second = outgoing(second_kernel, *operands, "second_outgoing")
    second = lax.all_to_all(second, FEAT, split_axis=0, concat_axis=0, tiled=True)
    first, pre = arrived(place, ids, moved.reshape(-1, owned), weights, bias[:, None])
    second = second.reshape(-1, owned)
    hidden, keep, send = finish(place, pre, second, first, weights, cotangent[0].T, owners)

    got = lax.ppermute(send, "core", [(0, 1), (1, 0)])
    parts = lax.all_to_all((keep + got).astype(jnp.bfloat16), FEAT, split_axis=0, concat_axis=0, tiled=True)
    total = jnp.sum(parts, axis=0, dtype=jnp.float32)
    others = [lax.ppermute(total, "x", [(i, i ^ k) for i in range(4)]) for k in (1, 2, 3)]
    total = (total + others[0]) + (others[1] + others[2])
    other = lax.ppermute(total, "core", [(0, 1), (1, 0)])
    first_core = core == 0
    return (
        hidden.T[None],
        jnp.where(first_core, total, other),
        jnp.where(first_core, other, total),
    )


def solution(mesh):
    axes = Mesh(mesh.devices.reshape(4, 4, 4, 2), ("z", "y", "x", "core"))
    in_specs = (
        P(GRP, None, FEAT),
        P(GRP, None),
        P(GRP, None, None),
        P(GRP, None),
        P(GRP, None, None, None, None),
        P(GRP),
        P(),
        P(),
        P(),
        P(GRP, FEAT, None),
    )
    out_specs = (P(GRP, FEAT, None), P(FEAT, None), P(FEAT, None))
    return jax.shard_map(on_device, mesh=axes, in_specs=in_specs, out_specs=out_specs, check_vma=False)
```

time: 118 us -> 114 us (0.966)
  Pallas kernels: 34.9 us -> 28 us
  waiting for transfers between devices: 33.2 us -> 39.9 us
  other arithmetic: 5.07 us -> 3.49 us
  local copies, waits for them, and re-layouts: 8.86 us -> 7.61 us
    pallas_call x2, Pallas kernels: 21.9 us -> 17.4 us  [outgoing(): pl.pallas_call(kernel, in_specs=[smem, smem, smem, vmem, anywhere, anywhe...]
    all_to_all x1, waiting for transfers between devices: 15.1 us -> 19.4 us  [on_device(): moved = lax.all_to_all(first, FEAT, split_axis=0, concat_axis=0, tiled=True)]
    all_to_all x1, waiting for transfers between devices: 11.2 us -> 13.5 us  [on_device(): lax.all_to_all(second, FEAT, split_axis=0, concat_axis=0, tiled=True)]
    pallas_call x1, Pallas kernels: 8.85 us -> 6.5 us  [finish(): pl.pallas_call(finish_kernel, in_specs=[pl.BlockSpec(memory_space=pltpu.S...]
    shift_right_logical x1 -> x0, other arithmetic: 1.58 us -> none  [on_device(): which = lax.shift_right_logical(ids[:, 0], 7)]
    unnamed x23 -> x22, local copies, waits for them, and re-layouts: 8.73 us -> 7.48 us
where the time goes in v5:
time: 114 us
  waiting for transfers between devices  39.9 us (35%)
  Pallas kernels  28 us (25%)
  starting transfers between devices  19.6 us (17%)
  blocking collectives  13.7 us (12%)
  local copies, waits for them, and re-layouts  7.61 us (7%)
  other arithmetic  3.49 us (3%)
  between operations  1.47 us (1%)
    all_to_all x1, waiting for transfers between devices, on_device(): moved = lax.all_to_all(first, FEAT, split_axis=0, concat_axis=0, tiled=True)  19.4 us
    pallas_call x2, Pallas kernels, outgoing(): pl.pallas_call(kernel, in_specs=[smem, smem, smem, vmem, anywhere, anywhe...  17.4 us
    all_to_all x1, blocking collectives, on_device(): lax.all_to_all((keep + got).astype(jnp.bfloat16), FEAT, split_axis=0, con...  13.7 us
    all_to_all x1, waiting for transfers between devices, on_device(): lax.all_to_all(second, FEAT, split_axis=0, concat_axis=0, tiled=True)  13.5 us
    all_to_all x1, starting transfers between devices, on_device(): moved = lax.all_to_all(first, FEAT, split_axis=0, concat_axis=0, tiled=True)  8.61 us
    unnamed x22, local copies, waits for them, and re-layouts  7.48 us
    pallas_call x1, Pallas kernels, finish(): pl.pallas_call(finish_kernel, in_specs=[pl.BlockSpec(memory_space=pltpu.S...  6.5 us
    ppermute x3, waiting for transfers between devices, on_device(): lax.ppermute(total, 'x', [(i, i ^ k) for i in range(4)])  4.87 us
  transfers between devices with their start and end apart: 7, of which 5 were waited for; matrix products, arithmetic and copies ran while one was open for 6% of the time, Pallas kernels for 9%

profile of v5, /device:TPU:1, one launch (start us, length us, event | category | flops | bytes accessed | tf_op | source)
XLA Modules:
  0.0 113.8 jit_solution(12579864337325347801)
XLA Ops:
  0.6 11.3 %first_outgoing.1 = bf16[16,64,1024]{2,1,0:T(8,128)(2,1)} custom-call(s32[1]{0:T(128)} %bitcast.core_ref, s32[3,1,128]{2,1,0:T(1,128)} %bitcast.38, s32[1,128]{1,0:T(1,128)} %counts_ref.3, s32[256,128]{1,0:T(8,128)} %bitcast.27, bf16[64,32768]{1,0:T(8,128)(2,1)} %bitcast.32, bf16[128,3,128,128]{3,2,1,0:T(8,128)(2,1)} %bitcast.30), custom_call_target="tpu_custom_call" | custom-call | flops 4000000000 | bytes 20971520 | tf_op jit(solution)/shard_map/first_outgoing/pallas_call | solution.py:183
  11.9 8.6 %all-to-all-start = ((bf16[16,64,1024]{2,1,0:T(8,128)(2,1)}), bf16[16,64,1024]{2,1,0:T(8,128)(2,1)S(1)}, u32[]{:S(2)}, u32[]{:S(2)}) async-start(bf16[16,64,1024]{2,1,0:T(8,128)(2,1)} %first_outgoing.1), calls=%async_computation | async-start | bytes 4194304 | tf_op jit(solution)/shard_map/all_to_all | solution.py:345
  20.6 6.1 %second_outgoing.1 = bf16[16,64,1024]{2,1,0:T(8,128)(2,1)} custom-call(s32[1]{0:T(128)} %bitcast.core_ref, s32[3,1,128]{2,1,0:T(1,128)} %bitcast.39, s32[1,128]{1,0:T(1,128)} %counts_ref.3, s32[256,128]{1,0:T(8,128)} %bitcast.28, bf16[64,32768]{1,0:T(8,128)(2,1)} %bitcast.33, bf16[128,3,128,128]{3,2,1,0:T(8,128)(2,1)} %bitcast.31), custom_call_target="tpu_custom_call" | custom-call | flops 4000000000 | bytes 20971520 | tf_op jit(solution)/shard_map/second_outgoing/pallas_call | solution.py:183
  26.7 19.4 %all-to-all-done = bf16[16,64,1024]{2,1,0:T(8,128)(2,1)S(1)} async-done(((bf16[16,64,1024]{2,1,0:T(8,128)(2,1)}), bf16[16,64,1024]{2,1,0:T(8,128)(2,1)S(1)}, u32[]{:S(2)}, u32[]{:S(2)}) %all-to-all-start) | async-done | bytes 2097184 | tf_op jit(solution)/shard_map/all_to_all | solution.py:345
  46.1 4.5 %all-to-all-start.1 = ((bf16[16,64,1024]{2,1,0:T(8,128)(2,1)}), bf16[16,64,1024]{2,1,0:T(8,128)(2,1)}, u32[]{:S(2)}, u32[]{:S(2)}) async-start(bf16[16,64,1024]{2,1,0:T(8,128)(2,1)} %second_outgoing.1), calls=%async_computation.1 | async-start | bytes 4194304 | tf_op jit(solution)/shard_map/all_to_all | solution.py:347
  51.2 1.0 copy.17
  52.3 1.0 copy.18
  53.4 2.1 %copy.20 = bf16[1,1024,256]{1,2,0:T(8,128)(2,1)} copy(bf16[1,1024,256]{2,1,0:T(8,128)(2,1)} %param.19) | data formatting | bytes 1048576 | tf_op args[9]
  55.6 1.3 %pad_maximum_fusion.weight_ref.weights_hbm = bf16[2,256,1024]{2,1,0:T(8,128)(2,1)S(1)} fusion(bf16[1,256,1024]{2,1,0:T(8,128)(2,1)} %bitcast.35, bf16[1,256,1024]{2,1,0:T(8,128)(2,1)} %bitcast.34), kind=kLoop, calls=%fused_computation | loop fusion | flops 524288 | bytes 2097152 | tf_op jit(solution)/shard_map/stack | solution.py:342
  56.9 4.1 %first_arrived.1 = (bf16[1024,1024]{1,0:T(8,128)(2,1)S(1)}, f32[256,1024]{1,0:T(8,128)S(1)}) custom-call(s32[3]{0:T(128)S(1)} %pad_add_fusion.place_ref, s32[256,128]{1,0:T(8,128)S(1)} %bitcast.29, bf16[1024,1024]{1,0:T(8,128)(2,1)S(1)} %bitcast.26, bf16[2,256,1024]{2,1,0:T(8,128)(2,1)S(1)} %pad_maximum_fusion.weight_ref.weights_hbm, f32[256,1]{1,0:T(8,128)S(1)} %copy.19.bias_ref), custom_call_target="tpu_custom_call" | custom-call | flops 2000000000 | bytes 6291456 | tf_op jit(solution)/shard_map/first_arrived/pallas_call | solution.py:220
  61.0 1.4 %copy-done.3 = bf16[1024,1024]{1,0:T(8,128)(2,1)} copy-done((bf16[1024,1024]{1,0:T(8,128)(2,1)}, bf16[1024,1024]{1,0:T(8,128)(2,1)S(1)}, u32[]{:S(2)}) %copy-start.3) | copy-done | bytes 2097176
  62.3 1.0 copy-done.4
  63.3 13.5 %all-to-all-done.1 = bf16[16,64,1024]{2,1,0:T(8,128)(2,1)} async-done(((bf16[16,64,1024]{2,1,0:T(8,128)(2,1)}), bf16[16,64,1024]{2,1,0:T(8,128)(2,1)}, u32[]{:S(2)}, u32[]{:S(2)}) %all-to-all-start.1) | async-done | bytes 2097184 | tf_op jit(solution)/shard_map/all_to_all | solution.py:347
  76.9 6.5 %finish.1 = (bf16[256,1024]{1,0:T(8,128)(2,1)}, f32[16,64,256]{2,1,0:T(8,128)}, bf16[16,64,256]{2,1,0:T(8,128)(2,1)}) custom-call(s32[3]{0:T(128)} %copy-done.2, f32[256,1024]{1,0:T(8,128)} %copy-done.4, bf16[1024,1024]{1,0:T(8,128)(2,1)} %bitcast.16.second_hbm, bf16[1024,1024]{1,0:T(8,128)(2,1)} %copy-done.3, bf16[2,256,1024]{2,1,0:T(8,128)(2,1)} %copy-done, ...), custom_call_target="tpu_custom_call" | custom-call | flops 2000000000 | bytes 9437184 | tf_op jit(solution)/shard_map/finish/pallas_call | solution.py:314
  83.5 2.1 %collective-permute-done = bf16[16,64,256]{2,1,0:T(8,128)(2,1)S(1)} collective-permute-done((bf16[16,64,256]{2,1,0:T(8,128)(2,1)}, bf16[16,64,256]{2,1,0:T(8,128)(2,1)S(1)}, u32[]{:S(2)}, u32[]{:S(2)}) %collective-permute-start) | collective-permute-done | bytes 524320 | tf_op jit(solution)/shard_map/ppermute | solution.py:352
  85.6 1.4 %add_convert_fusion = bf16[16,64,256]{2,1,0:T(8,128)(2,1)S(1)} fusion(f32[16,64,256]{2,1,0:T(8,128)} %get-tuple-element.11, bf16[16,64,256]{2,1,0:T(8,128)(2,1)S(1)} %collective-permute-done), kind=kLoop, calls=%fused_computation.2 | loop fusion | flops 786432 | bytes 2097152 | tf_op jit(solution)/shard_map/convert_element_type | solution.py:353
  87.0 13.7 %all_to_all.15 = bf16[16,64,256]{2,1,0:T(8,128)(2,1)S(1)} all-to-all(bf16[16,64,256]{2,1,0:T(8,128)(2,1)S(1)} %add_convert_fusion), channel_id=1, replica_groups=mesh['z'=4,'y'=4,'x'=4,'core'=2] {'z','y'}, dimensions={0} | all-to-all | bytes 1048576 | tf_op jit(solution)/shard_map/all_to_all | solution.py:353
  100.8 1.4 %collective-permute-start.1 = (f32[64,256]{1,0:T(8,128)S(1)}, f32[64,256]{1,0:T(8,128)S(1)}, u32[]{:S(2)}, u32[]{:S(2)}) collective-permute-start(f32[64,256]{1,0:T(8,128)S(1)} %convert_reduce_fusion), channel_id=1, source_target_pairs={{0,2},{2,0},{4,6},{6,4},{1,3},{3,1},{5,7},{7,5},{8,10},{10,8},{12,... | collective-permute-start | bytes 196616 | tf_op jit(solution)/shard_map/ppermute | solution.py:355
  102.2 2.5 %collective-permute-start.2 = (f32[64,256]{1,0:T(8,128)S(1)}, f32[64,256]{1,0:T(8,128)S(1)}, u32[]{:S(2)}, u32[]{:S(2)}) collective-permute-start(f32[64,256]{1,0:T(8,128)S(1)} %convert_reduce_fusion), channel_id=1, source_target_pairs={{0,4},{2,6},{4,0},{6,2},{1,5},{3,7},{5,1},{7,3},{8,12},{10,14},{12... | collective-permute-start | bytes 196616 | tf_op jit(solution)/shard_map/ppermute | solution.py:355
  104.7 2.3 %collective-permute-done.2 = f32[64,256]{1,0:T(8,128)S(1)} collective-permute-done((f32[64,256]{1,0:T(8,128)S(1)}, f32[64,256]{1,0:T(8,128)S(1)}, u32[]{:S(2)}, u32[]{:S(2)}) %collective-permute-start.2) | collective-permute-done | bytes 65568 | tf_op jit(solution)/shard_map/ppermute | solution.py:355
  107.0 2.6 %collective-permute-done.3 = f32[64,256]{1,0:T(8,128)S(1)} collective-permute-done((f32[64,256]{1,0:T(8,128)S(1)}, f32[64,256]{1,0:T(8,128)S(1)}, u32[]{:S(2)}, u32[]{:S(2)}) %collective-permute-start.3) | collective-permute-done | bytes 65568 | tf_op jit(solution)/shard_map/ppermute | solution.py:355
  109.6 2.5 %collective-permute-start.4 = (f32[64,256]{1,0:T(8,128)S(1)}, f32[64,256]{1,0:T(8,128)S(1)}, u32[]{:S(2)}, u32[]{:S(2)}) collective-permute-start(f32[64,256]{1,0:T(8,128)S(1)} %add_add_fusion), channel_id=1, source_target_pairs={{0,1},{1,0},{2,3},{3,2},{4,5},{5,4},{6,7},{7,6},{8,9},{9,8},{10,11... | collective-permute-start | bytes 196616 | tf_op jit(solution)/shard_map/ppermute | solution.py:357
  112.1 1.0 copy.21
  113.1 0.7 broadcast_select_fusion
  (24 shorter events, 0.5 us)
Async XLA Ops:
  11.9 34.2 %all-to-all-start = ((bf16[16,64,1024]{2,1,0:T(8,128)(2,1)}), bf16[16,64,1024]{2,1,0:T(8,128)(2,1)S(1)}, u32[]{:S(2)}, u32[]{:S(2)}) async-start(bf16[16,64,1024]{2,1,0:T(8,128)(2,1)} %first_outgoing.1), calls=%async_computation | async-start | bytes 4194304 | tf_op jit(solution)/shard_map/all_to_all | solution.py:345
  26.7 24.5 %copy-start.5 = (bf16[1024,256]{1,0:T(8,128)(2,1)S(1)}, bf16[1024,256]{1,0:T(8,128)(2,1)}, u32[]{:S(2)}) copy-start(bf16[1024,256]{1,0:T(8,128)(2,1)} %param.16) | copy-start | bytes 1572868
  26.7 25.5 %copy-start.6 = (bf16[1024,256]{1,0:T(8,128)(2,1)S(1)}, bf16[1024,256]{1,0:T(8,128)(2,1)}, u32[]{:S(2)}) copy-start(bf16[1024,256]{1,0:T(8,128)(2,1)} %param.17) | copy-start | bytes 1572868
  46.1 30.8 %all-to-all-start.1 = ((bf16[16,64,1024]{2,1,0:T(8,128)(2,1)}), bf16[16,64,1024]{2,1,0:T(8,128)(2,1)}, u32[]{:S(2)}, u32[]{:S(2)}) async-start(bf16[16,64,1024]{2,1,0:T(8,128)(2,1)} %second_outgoing.1), calls=%async_computation.1 | async-start | bytes 4194304 | tf_op jit(solution)/shard_map/all_to_all | solution.py:347
  50.6 2.7 %copy-start.8 = (f32[256]{0:T(256)S(1)}, f32[256]{0:T(256)}, u32[]{:S(2)}) copy-start(f32[256]{0:T(256)} %param.18) | copy-start | bytes 3076
  52.2 4.6 %copy-start.1 = (s32[1,32768]{1,0:T(1,128)S(1)}, s32[1,32768]{1,0:T(1,128)}, u32[]{:S(2)}) copy-start(s32[1,32768]{1,0:T(1,128)} %param.11) | copy-start | bytes 393220
  55.6 5.4 %copy-start.2 = (s32[3]{0:T(128)}, s32[3]{0:T(128)S(1)}, u32[]{:S(2)}) copy-start(s32[3]{0:T(128)S(1)} %pad_add_fusion.place_ref) | copy-start | bytes 40
  56.9 4.1 %copy-start = (bf16[2,256,1024]{2,1,0:T(8,128)(2,1)}, bf16[2,256,1024]{2,1,0:T(8,128)(2,1)S(1)}, u32[]{:S(2)}) copy-start(bf16[2,256,1024]{2,1,0:T(8,128)(2,1)S(1)} %pad_maximum_fusion.weight_ref.weights_hbm) | copy-start | bytes 3145732
  61.0 1.4 %copy-start.3 = (bf16[1024,1024]{1,0:T(8,128)(2,1)}, bf16[1024,1024]{1,0:T(8,128)(2,1)S(1)}, u32[]{:S(2)}) copy-start(bf16[1024,1024]{1,0:T(8,128)(2,1)S(1)} %get-tuple-element.9.first_hbm) | copy-start | bytes 6291460
  62.3 1.0 copy-start.4
  83.4 28.7 %copy-start.7 = (bf16[256,1024]{1,0:T(8,128)(2,1)S(1)}, bf16[256,1024]{1,0:T(8,128)(2,1)}, u32[]{:S(2)}) copy-start(bf16[256,1024]{1,0:T(8,128)(2,1)} %get-tuple-element.10) | copy-start | bytes 1572868
  83.4 2.2 %collective-permute-start = (bf16[16,64,256]{2,1,0:T(8,128)(2,1)}, bf16[16,64,256]{2,1,0:T(8,128)(2,1)S(1)}, u32[]{:S(2)}, u32[]{:S(2)}) collective-permute-start(bf16[16,64,256]{2,1,0:T(8,128)(2,1)} %get-tuple-element.12), channel_id=1, source_target_pairs={{0,1},{1,0},{2,3},{3,2},{4,5},{5,4},{6,7},{7,6},{8,9},{9,8},{10,11... | collective-permute-start | bytes 1572872 | tf_op jit(solution)/shard_map/ppermute | solution.py:352
  100.8 3.9 %collective-permute-start.1 = (f32[64,256]{1,0:T(8,128)S(1)}, f32[64,256]{1,0:T(8,128)S(1)}, u32[]{:S(2)}, u32[]{:S(2)}) collective-permute-start(f32[64,256]{1,0:T(8,128)S(1)} %convert_reduce_fusion), channel_id=1, source_target_pairs={{0,2},{2,0},{4,6},{6,4},{1,3},{3,1},{5,7},{7,5},{8,10},{10,8},{12,... | collective-permute-start | bytes 196616 | tf_op jit(solution)/shard_map/ppermute | solution.py:355
  102.2 4.8 %collective-permute-start.2 = (f32[64,256]{1,0:T(8,128)S(1)}, f32[64,256]{1,0:T(8,128)S(1)}, u32[]{:S(2)}, u32[]{:S(2)}) collective-permute-start(f32[64,256]{1,0:T(8,128)S(1)} %convert_reduce_fusion), channel_id=1, source_target_pairs={{0,4},{2,6},{4,0},{6,2},{1,5},{3,7},{5,1},{7,3},{8,12},{10,14},{12... | collective-permute-start | bytes 196616 | tf_op jit(solution)/shard_map/ppermute | solution.py:355
  104.6 5.0 %collective-permute-start.3 = (f32[64,256]{1,0:T(8,128)S(1)}, f32[64,256]{1,0:T(8,128)S(1)}, u32[]{:S(2)}, u32[]{:S(2)}) collective-permute-start(f32[64,256]{1,0:T(8,128)S(1)} %convert_reduce_fusion), channel_id=1, source_target_pairs={{0,6},{2,4},{4,2},{6,0},{1,7},{3,5},{5,3},{7,1},{8,14},{10,12},{12... | collective-permute-start | bytes 196616 | tf_op jit(solution)/shard_map/ppermute | solution.py:355
  109.6 3.5 %collective-permute-start.4 = (f32[64,256]{1,0:T(8,128)S(1)}, f32[64,256]{1,0:T(8,128)S(1)}, u32[]{:S(2)}, u32[]{:S(2)}) collective-permute-start(f32[64,256]{1,0:T(8,128)S(1)} %add_add_fusion), channel_id=1, source_target_pairs={{0,1},{1,0},{2,3},{3,2},{4,5},{5,4},{6,7},{7,6},{8,9},{9,8},{10,11... | collective-permute-start | bytes 196616 | tf_op jit(solution)/shard_map/ppermute | solution.py:357

commit v6 on v5

v6 whole, which is shorter than its diff:
```python
import jax
import jax.numpy as jnp
from jax import lax
from jax.experimental import pallas as pl
from jax.experimental.pallas import tpu as pltpu
from jax.sharding import Mesh, PartitionSpec as P

BLOCK = 128
MIB = 1 << 20
WHOLE = 60 * MIB
FEAT = ("z", "y")
GRP = ("x", "core")
NT = (((1,), (1,)), ((), ()))
NN = (((1,), (0,)), ((), ()))


def dot(left, right, dims=NN):
    return lax.dot_general(left, right, dims, preferred_element_type=jnp.float32)


def selector(within):
    rows = lax.broadcasted_iota(jnp.int32, (BLOCK, BLOCK), 0)
    return jnp.where(rows == within, 1.0, 0.0).astype(jnp.bfloat16)


def read_blocks(ids_ref, vector, which, sem):
    lanes = lax.broadcasted_iota(jnp.int32, (vector.shape[0], BLOCK), 1)
    first = jnp.where(lanes == 0, 1.0, 0.0).astype(jnp.bfloat16)
    blocks = lax.shift_right_logical(ids_ref[...], 7).astype(jnp.float32).astype(jnp.bfloat16)
    vector[...] = dot(first, blocks, NT).astype(jnp.int32)
    copy = pltpu.make_async_copy(vector, which, sem)
    copy.start()
    copy.wait()


def block_of(table, w):
    return table[:, pl.ds(pl.multiple_of(w * BLOCK, BLOCK), BLOCK)]


def in_run_order(chosen, ids_row):
    within = jnp.broadcast_to(jnp.bitwise_and(ids_row, BLOCK - 1), (8, BLOCK))
    chosen = chosen.astype(jnp.float32)
    rows = [jnp.take_along_axis(chosen[i : i + 8], within, axis=1) for i in range(0, chosen.shape[0], 8)]
    return jnp.concatenate(rows, axis=0).astype(jnp.bfloat16)


def outgoing_kernel(
    lists_ref, counts_ref, ids_ref, table_hbm, tiles_hbm, out_hbm, rows, table, tiles, vector, which, load, leave
):
    blocks = ids_ref.shape[0]
    owners, width, owned = rows.shape
    width = width // 2
    per = owned // BLOCK
    slots, dst_blocks = lists_ref.shape[0], lists_ref.shape[2]
    together = 4

    def load_tiles(r):
        part = pl.ds(r * per, per)
        return pltpu.make_async_copy(tiles_hbm.at[part], tiles.at[part], load.at[r])

    known = table.at[:, pl.ds(0, table_hbm.shape[1])]
    load_table = pltpu.make_async_copy(table_hbm, known, load.at[owners + 1])
    load_table.start()
    for r in range(owners):
        load_tiles(r).start()
    table[:, table_hbm.shape[1] :] = jnp.zeros((width, BLOCK), table.dtype)
    read_blocks(ids_ref, vector, which, load.at[owners])
    load_table.wait()

    def aggregated(d):
        count = counts_ref[0, d]
        left = []
        for s in range(slots):
            used = s < count
            n = lists_ref[s, 0, d]
            w = jnp.where(used, which[0, n], blocks)
            source = in_run_order(block_of(table, w), ids_ref[pl.ds(n, 1), :])
            ones = jnp.full((16, BLOCK), jnp.where(used, 1.0, 0.0), jnp.float32).astype(jnp.bfloat16)
            left.append(jnp.concatenate([source, ones], axis=0))
        right = jnp.concatenate([tiles[d, s] for s in range(slots)], axis=1)
        total = dot(jnp.concatenate(left, axis=1), right, NT)
        return (total[:width] * (1.0 / total[width : width + 1])).astype(jnp.bfloat16)

    def some(i, carry):
        for k in range(together):
            load_tiles(i * together + k).wait()
        first = i * together * per
        results = [aggregated(first + k) for k in range(together * per)]
        own = [block_of(table, which[0, first + k]) for k in range(together * per)]
        for k in range(together * per):
            r, columns = i * together + k // per, slice((k % per) * BLOCK, (k % per + 1) * BLOCK)
            rows[r, :width, columns] = own[k]
            rows[r, width:, columns] = results[k]
        for k in range(together):
            r = i * together + k
            pltpu.make_async_copy(rows.at[r], out_hbm.at[r], leave.at[r]).start()
        return carry

    lax.fori_loop(0, dst_blocks // per // together, some, 0)
    for r in range(owners):
        pltpu.make_async_copy(rows.at[r], out_hbm.at[r], leave.at[r]).wait()


def outgoing(lists, counts, ids, table, tiles, owners):
    width, rows = table.shape
    blocks = rows // BLOCK
    smem, vmem = pl.BlockSpec(memory_space=pltpu.SMEM), pl.BlockSpec(memory_space=pltpu.VMEM)
    anywhere = pl.BlockSpec(memory_space=pl.ANY)
    out = (owners, 2 * width, tiles.shape[0] // owners * BLOCK)
    return pl.pallas_call(
        outgoing_kernel,
        in_specs=[smem, smem, vmem, anywhere, anywhere],
        out_specs=anywhere,
        out_shape=jax.ShapeDtypeStruct(out, jnp.bfloat16),
        scratch_shapes=[
            pltpu.VMEM(out, jnp.bfloat16),
            pltpu.VMEM((width, rows + BLOCK), jnp.bfloat16),
            pltpu.VMEM(tiles.shape, jnp.bfloat16),
            pltpu.VMEM((8, blocks), jnp.int32),
            pltpu.SMEM((8, blocks), jnp.int32),
            pltpu.SemaphoreType.DMA((owners + 2,)),
            pltpu.SemaphoreType.DMA((owners,)),
        ],
        compiler_params=pltpu.CompilerParams(vmem_limit_bytes=WHOLE),
        cost_estimate=pl.CostEstimate(flops=4_000_000_000, bytes_accessed=20 * MIB, transcendentals=0),
        name="pick_and_aggregate",
    )(lists, counts, ids, table, tiles)


def gelu_and_slope(pre):
    c, k = 0.7978845608028654, 0.044715
    square = pre * pre
    t = jnp.tanh(c * pre * (1.0 + k * square))
    half = 0.5 * (1.0 + t)
    slope = half + 0.5 * pre * (1.0 - t * t) * (c * (1.0 + 3.0 * k * square))
    return pre * half, slope


def move_lanes(rows, order):
    order = jnp.broadcast_to(order, (8, BLOCK))
    moved = [jnp.take_along_axis(rows[i : i + 8], order, axis=1) for i in range(0, rows.shape[0], 8)]
    return jnp.concatenate(moved, axis=0)


def finish_kernel(
    place_ref, bias_ref, ids_hbm, moved_hbm, weights_hbm, upstream_hbm, hidden_hbm, keep_hbm, send_hbm,
    ids_ref, rows, weights, upstream_ref, slopes, hidden_ref, keep_ref, send_ref, load, leave,
):
    owners, share, owned = rows.shape[1:]
    features = owners * share
    per = owned // BLOCK
    core, rank, limit = place_ref[0], place_ref[1], place_ref[2]
    own_slot, agg_slot = core, 1 - core

    load_ids = pltpu.make_async_copy(ids_hbm.at[pl.ds(pl.multiple_of(rank * per, per), per)], ids_ref, load.at[0])
    load_weights = pltpu.make_async_copy(weights_hbm, weights, load.at[1])
    half = owned // 2
    load_rows = []
    for h in range(2):
        columns = slice(h * half, (h + 1) * half)
        for k, slot in enumerate((own_slot, agg_slot)):
            load_rows.append(
                pltpu.make_async_copy(
                    moved_hbm.at[:, k * share : (k + 1) * share, columns],
                    rows.at[slot, :, :, columns],
                    load.at[2 + 2 * h + k],
                )
            )
    load_upstream = pltpu.make_async_copy(upstream_hbm, upstream_ref, load.at[6])
    load_ids.start()
    load_weights.start()
    load_rows[0].start()
    load_rows[1].start()
    load_upstream.start()
    load_rows[2].start()
    load_rows[3].start()

    load_ids.wait()
    lanes = lax.broadcasted_iota(jnp.int32, (8, BLOCK), 1).astype(jnp.bfloat16)
    orders = [jnp.bitwise_and(ids_ref[b : b + 1, :], BLOCK - 1) for b in range(per)]
    inverse = [dot(lanes, selector(order), NT).astype(jnp.int32) for order in orders]
    load_weights.wait()
    load_upstream.wait()

    def rows_of(slot, columns):
        return rows[slot, :, :, columns].reshape(features, BLOCK)

    for h in range(2):
        load_rows[2 * h].wait()
        load_rows[2 * h + 1].wait()
        for b in range(h * per // 2, (h + 1) * per // 2):
            columns = slice(b * BLOCK, (b + 1) * BLOCK)
            own = move_lanes(dot(weights[0], rows_of(own_slot, columns)), orders[b])
            pre = own + dot(weights[1], rows_of(agg_slot, columns)) + bias_ref[...]
            active, back = gelu_and_slope(pre)
            positions = b * BLOCK + lax.broadcasted_iota(jnp.int32, (1, BLOCK), 1)
            valid = jnp.where(positions < limit, 1.0, 0.0)
            hidden_ref[:, columns] = (active * valid).astype(jnp.bfloat16)
            slope = (upstream_ref[:, columns].astype(jnp.float32) * back * valid).astype(jnp.bfloat16)
            slopes[agg_slot, :, columns] = slope
            slopes[own_slot, :, columns] = move_lanes(slope.astype(jnp.float32), inverse[b]).astype(jnp.bfloat16)
    leave_hidden = pltpu.make_async_copy(hidden_ref, hidden_hbm, leave.at[0])
    leave_hidden.start()

    group = 4

    def grads(slot, out_ref):
        for i in range(0, owners, group):
            left = rows[slot, i : i + group].reshape(group * share, owned)
            total = dot(left, slopes[slot], NT)
            out_ref[i : i + group] = total.reshape(group, share, -1).astype(out_ref.dtype)

    grads(1, send_ref)
    leave_send = pltpu.make_async_copy(send_ref, send_hbm, leave.at[1])
    leave_send.start()
    grads(0, keep_ref)
    leave_keep = pltpu.make_async_copy(keep_ref, keep_hbm, leave.at[2])
    leave_keep.start()
    leave_hidden.wait()
    leave_send.wait()
    leave_keep.wait()


def finish(place, bias, ids, moved, weights, upstream):
    owners, share, owned = moved.shape[0], moved.shape[1] // 2, moved.shape[2]
    hidden = weights.shape[1]
    part = (owners, share, hidden)
    anywhere = pl.BlockSpec(memory_space=pl.ANY)
    outs = [
        jax.ShapeDtypeStruct((hidden, owned), jnp.bfloat16),
        jax.ShapeDtypeStruct(part, jnp.float32),
        jax.ShapeDtypeStruct(part, jnp.bfloat16),
    ]
    return pl.pallas_call(
        finish_kernel,
        in_specs=[pl.BlockSpec(memory_space=pltpu.SMEM), pl.BlockSpec(memory_space=pltpu.VMEM)] + [anywhere] * 4,
        out_specs=[anywhere] * 3,
        out_shape=outs,
        scratch_shapes=[
            pltpu.VMEM((owned // BLOCK, BLOCK), jnp.int32),
            pltpu.VMEM((2, owners, share, owned), jnp.bfloat16),
            pltpu.VMEM(weights.shape, jnp.bfloat16),
            pltpu.VMEM(upstream.shape, jnp.bfloat16),
            pltpu.VMEM((2, hidden, owned), jnp.bfloat16),
        ]
        + [pltpu.VMEM(a.shape, a.dtype) for a in outs]
        + [pltpu.SemaphoreType.DMA((7,)), pltpu.SemaphoreType.DMA((3,))],
        compiler_params=pltpu.CompilerParams(vmem_limit_bytes=WHOLE),
        cost_estimate=pl.CostEstimate(flops=2_000_000_000, bytes_accessed=9 * MIB, transcendentals=262144),
        name="finish",
    )(place, bias, ids, moved, weights, upstream)


def on_device(
    node_table, node_ids, block_lists, block_counts, tiles, batch_sizes, w_self, w_neigh, bias, cotangent
):
    owners = lax.axis_size(FEAT)
    rank, core = lax.axis_index(FEAT), lax.axis_index("core")
    table = jnp.swapaxes(node_table[0], 0, 1)
    width = table.shape[0]
    ids = node_ids[0].reshape(-1, BLOCK)
    owned = cotangent.shape[1]

    lists = jnp.transpose(block_lists, (2, 0, 1))
    place = jnp.stack([core, rank, batch_sizes[0] - rank * owned])
    weights = jnp.stack([w_self.T, w_neigh.T])

    rows = outgoing(lists, block_counts, ids, table, tiles[0], owners)
    moved = lax.all_to_all(rows, FEAT, split_axis=0, concat_axis=0, tiled=True)
    hidden, keep, send = finish(place, bias[:, None], ids, moved, weights, cotangent[0].T)

    got = lax.ppermute(send, "core", [(0, 1), (1, 0)])
    parts = lax.all_to_all((keep + got).astype(jnp.bfloat16), FEAT, split_axis=0, concat_axis=0, tiled=True)
    total = jnp.sum(parts, axis=0, dtype=jnp.float32)
    others = [lax.ppermute(total, "x", [(i, i ^ k) for i in range(4)]) for k in (1, 2, 3)]
    total = (total + others[0]) + (others[1] + others[2])
    other = lax.ppermute(total, "core", [(0, 1), (1, 0)])
    first_core = core == 0
    return (
        hidden.T[None],
        jnp.where(first_core, total, other),
        jnp.where(first_core, other, total),
    )


def solution(mesh):
    axes = Mesh(mesh.devices.reshape(4, 4, 4, 2), ("z", "y", "x", "core"))
    in_specs = (
        P(GRP, None, FEAT),
        P(GRP, None),
        P(GRP, None, None),
        P(GRP, None),
        P(GRP, None, None, None, None),
        P(GRP),
        P(),
        P(),
        P(),
        P(GRP, FEAT, None),
    )
    out_specs = (P(GRP, FEAT, None), P(FEAT, None), P(FEAT, None))
    return jax.shard_map(on_device, mesh=axes, in_specs=in_specs, out_specs=out_specs, check_vma=False)
```

time: 114 us -> 126 us (1.11)
  waiting for transfers between devices: 39.9 us -> 64.3 us
  Pallas kernels: 28 us -> 20.4 us
  local copies, waits for them, and re-layouts: 7.61 us -> 3.23 us
  starting transfers between devices: 19.6 us -> 17.5 us
    all_to_all x2 -> x1, waiting for transfers between devices: 32.9 us -> 57.7 us  [on_device(): moved = lax.all_to_all(rows, FEAT, split_axis=0, concat_axis=0, tiled=True)]
    pallas_call x3 -> x1, Pallas kernels: 21.5 us -> 11.5 us  [outgoing(): pl.pallas_call(outgoing_kernel, in_specs=[smem, smem, vmem, anywhere, any...]
    unnamed x22 -> x14, local copies, waits for them, and re-layouts: 7.48 us -> 2.44 us
    all_to_all x2 -> x1, starting transfers between devices: 13.1 us -> 8.8 us  [on_device(): moved = lax.all_to_all(rows, FEAT, split_axis=0, concat_axis=0, tiled=True)]
    pallas_call x1, Pallas kernels: 6.5 us -> 8.96 us  [finish(): pl.pallas_call(finish_kernel, in_specs=[pl.BlockSpec(memory_space=pltpu.S...]
    ppermute x1, starting transfers between devices: 0.08 us -> 1.93 us  [on_device(): got = lax.ppermute(send, 'core', [(0, 1), (1, 0)])]
  transfers between devices with their start and end apart: 7 -> 6, of which waited for: 5 -> 4; matrix products, arithmetic and copies ran while one was open for 6% -> 4% of each run, Pallas kernels for 9% -> 0%
where the time goes in v6:
time: 126 us
  waiting for transfers between devices  64.3 us (51%)
  Pallas kernels  20.4 us (16%)
  starting transfers between devices  17.5 us (14%)
  blocking collectives  14.8 us (12%)
  other arithmetic  3.86 us (3%)
  local copies, waits for them, and re-layouts  3.23 us (3%)
  between operations  1.41 us (1%)
    all_to_all x1, waiting for transfers between devices, on_device(): moved = lax.all_to_all(rows, FEAT, split_axis=0, concat_axis=0, tiled=True)  57.7 us
    all_to_all x1, blocking collectives, on_device(): lax.all_to_all((keep + got).astype(jnp.bfloat16), FEAT, split_axis=0, con...  14.8 us
    pallas_call x1, Pallas kernels, outgoing(): pl.pallas_call(outgoing_kernel, in_specs=[smem, smem, vmem, anywhere, any...  11.5 us
    pallas_call x1, Pallas kernels, finish(): pl.pallas_call(finish_kernel, in_specs=[pl.BlockSpec(memory_space=pltpu.S...  8.96 us
    all_to_all x1, starting transfers between devices, on_device(): moved = lax.all_to_all(rows, FEAT, split_axis=0, concat_axis=0, tiled=True)  8.8 us
    ppermute x3, waiting for transfers between devices, on_device(): lax.ppermute(total, 'x', [(i, i ^ k) for i in range(4)])  4.86 us
    ppermute x3, starting transfers between devices, on_device(): lax.ppermute(total, 'x', [(i, i ^ k) for i in range(4)])  3.94 us
    ppermute x1, starting transfers between devices, on_device(): other = lax.ppermute(total, 'core', [(0, 1), (1, 0)])  2.86 us
  transfers between devices with their start and end apart: 6, of which 4 were waited for; matrix products, arithmetic and copies ran while one was open for 4% of the time, Pallas kernels for 0%

profile of v6, /device:TPU:1, one launch (start us, length us, event | category | flops | bytes accessed | tf_op | source)
XLA Modules:
  0.0 125.5 jit_solution(215289779592891681)
XLA Ops:
  0.6 11.5 %pick_and_aggregate.1 = bf16[16,128,1024]{2,1,0:T(8,128)(2,1)} custom-call(s32[3,1,128]{2,1,0:T(1,128)} %bitcast.32, s32[1,128]{1,0:T(1,128)} %counts_ref.1, s32[256,128]{1,0:T(8,128)} %bitcast.30, bf16[64,32768]{1,0:T(8,128)(2,1)} %bitcast.25, bf16[128,3,128,128]{3,2,1,0:T(8,128)(2,1)} %bitcast.24), custom_call_target="tpu_custom_call" | custom-call | flops 4000000000 | bytes 20971520 | tf_op jit(solution)/shard_map/pick_and_aggregate/pallas_call | solution.py:110
  12.1 0.0 copy-start.1
  12.2 8.8 %all-to-all-start = ((bf16[16,128,1024]{2,1,0:T(8,128)(2,1)}), bf16[16,128,1024]{2,1,0:T(8,128)(2,1)}, u32[]{:S(2)}, u32[]{:S(2)}) async-start(bf16[16,128,1024]{2,1,0:T(8,128)(2,1)} %pick_and_aggregate.1), calls=%async_computation | async-start | bytes 8388608 | tf_op jit(solution)/shard_map/all_to_all | solution.py:269
  21.6 0.2 copy.17
  21.9 0.2 copy.18
  22.1 1.0 copy.19
  23.1 0.8 copy.20.bias_ref
  23.9 0.6 pad_add_fusion.place_ref
  24.5 1.2 pad_maximum_fusion.weights_hbm
  25.6 57.7 %all-to-all-done.moved_hbm = bf16[16,128,1024]{2,1,0:T(8,128)(2,1)} async-done(((bf16[16,128,1024]{2,1,0:T(8,128)(2,1)}), bf16[16,128,1024]{2,1,0:T(8,128)(2,1)}, u32[]{:S(2)}, u32[]{:S(2)}) %all-to-all-start) | async-done | bytes 4194336 | tf_op jit(solution)/shard_map/all_to_all | solution.py:269
  83.3 9.0 %finish.1 = (bf16[256,1024]{1,0:T(8,128)(2,1)}, f32[16,64,256]{2,1,0:T(8,128)}, bf16[16,64,256]{2,1,0:T(8,128)(2,1)}) custom-call(s32[3]{0:T(128)} %pad_add_fusion.place_ref, f32[256,1]{1,0:T(8,128)} %copy.20.bias_ref, s32[256,128]{1,0:T(8,128)} %bitcast.31, bf16[16,128,1024]{2,1,0:T(8,128)(2,1)} %all-to-all-done.moved_hbm, ...), custom_call_target="tpu_custom_call" | custom-call | flops 2000000000 | bytes 9437184 | tf_op jit(solution)/shard_map/finish/pallas_call | solution.py:234
  92.3 1.9 %collective-permute-start = (bf16[16,64,256]{2,1,0:T(8,128)(2,1)}, bf16[16,64,256]{2,1,0:T(8,128)(2,1)S(1)}, u32[]{:S(2)}, u32[]{:S(2)}) collective-permute-start(bf16[16,64,256]{2,1,0:T(8,128)(2,1)} %get-tuple-element.8), channel_id=1, source_target_pairs={{0,1},{1,0},{2,3},{3,2},{4,5},{5,4},{6,7},{7,6},{8,9},{9,8},{10,11... | collective-permute-start | bytes 1572872 | tf_op jit(solution)/shard_map/ppermute | solution.py:272
  94.2 1.7 %collective-permute-done = bf16[16,64,256]{2,1,0:T(8,128)(2,1)S(1)} collective-permute-done((bf16[16,64,256]{2,1,0:T(8,128)(2,1)}, bf16[16,64,256]{2,1,0:T(8,128)(2,1)S(1)}, u32[]{:S(2)}, u32[]{:S(2)}) %collective-permute-start) | collective-permute-done | bytes 524320 | tf_op jit(solution)/shard_map/ppermute | solution.py:272
  95.9 1.4 %add_convert_fusion = bf16[16,64,256]{2,1,0:T(8,128)(2,1)S(1)} fusion(f32[16,64,256]{2,1,0:T(8,128)} %get-tuple-element.7, bf16[16,64,256]{2,1,0:T(8,128)(2,1)S(1)} %collective-permute-done), kind=kLoop, calls=%fused_computation.2 | loop fusion | flops 786432 | bytes 2097152 | tf_op jit(solution)/shard_map/convert_element_type | solution.py:273
  97.3 14.8 %all_to_all.10 = bf16[16,64,256]{2,1,0:T(8,128)(2,1)S(1)} all-to-all(bf16[16,64,256]{2,1,0:T(8,128)(2,1)S(1)} %add_convert_fusion), channel_id=1, replica_groups=mesh['z'=4,'y'=4,'x'=4,'core'=2] {'z','y'}, dimensions={0} | all-to-all | bytes 1048576 | tf_op jit(solution)/shard_map/all_to_all | solution.py:273
  112.1 0.1 convert_reduce_fusion
  112.2 1.3 %collective-permute-start.1 = (f32[64,256]{1,0:T(8,128)S(1)}, f32[64,256]{1,0:T(8,128)S(1)}, u32[]{:S(2)}, u32[]{:S(2)}) collective-permute-start(f32[64,256]{1,0:T(8,128)S(1)} %convert_reduce_fusion), channel_id=1, source_target_pairs={{0,2},{2,0},{4,6},{6,4},{1,3},{3,1},{5,7},{7,5},{8,10},{10,8},{12,... | collective-permute-start | bytes 196616 | tf_op jit(solution)/shard_map/ppermute | solution.py:275
  113.5 2.5 %collective-permute-start.2 = (f32[64,256]{1,0:T(8,128)S(1)}, f32[64,256]{1,0:T(8,128)S(1)}, u32[]{:S(2)}, u32[]{:S(2)}) collective-permute-start(f32[64,256]{1,0:T(8,128)S(1)} %convert_reduce_fusion), channel_id=1, source_target_pairs={{0,4},{2,6},{4,0},{6,2},{1,5},{3,7},{5,1},{7,3},{8,12},{10,14},{12... | collective-permute-start | bytes 196616 | tf_op jit(solution)/shard_map/ppermute | solution.py:275
  116.0 0.2 collective-permute-start.3
  116.1 2.2 %collective-permute-done.2 = f32[64,256]{1,0:T(8,128)S(1)} collective-permute-done((f32[64,256]{1,0:T(8,128)S(1)}, f32[64,256]{1,0:T(8,128)S(1)}, u32[]{:S(2)}, u32[]{:S(2)}) %collective-permute-start.2) | collective-permute-done | bytes 65568 | tf_op jit(solution)/shard_map/ppermute | solution.py:275
  118.3 2.7 %collective-permute-done.3 = f32[64,256]{1,0:T(8,128)S(1)} collective-permute-done((f32[64,256]{1,0:T(8,128)S(1)}, f32[64,256]{1,0:T(8,128)S(1)}, u32[]{:S(2)}, u32[]{:S(2)}) %collective-permute-start.3) | collective-permute-done | bytes 65568 | tf_op jit(solution)/shard_map/ppermute | solution.py:275
  121.0 2.9 %collective-permute-start.4 = (f32[64,256]{1,0:T(8,128)S(1)}, f32[64,256]{1,0:T(8,128)S(1)}, u32[]{:S(2)}, u32[]{:S(2)}) collective-permute-start(f32[64,256]{1,0:T(8,128)S(1)} %add_add_fusion), channel_id=1, source_target_pairs={{0,1},{1,0},{2,3},{3,2},{4,5},{5,4},{6,7},{7,6},{8,9},{9,8},{10,11... | collective-permute-start | bytes 196616 | tf_op jit(solution)/shard_map/ppermute | solution.py:277
  123.9 1.0 copy.21
  124.9 0.7 broadcast_select_fusion
  (12 shorter events, 0.0 us)
Async XLA Ops:
  12.1 9.5 %copy-start = (bf16[1024,256]{1,0:T(8,128)(2,1)S(1)}, bf16[1024,256]{1,0:T(8,128)(2,1)}, u32[]{:S(2)}) copy-start(bf16[1024,256]{1,0:T(8,128)(2,1)} %param.16) | copy-start | bytes 1572868
  12.1 9.7 %copy-start.1 = (bf16[1024,256]{1,0:T(8,128)(2,1)S(1)}, bf16[1024,256]{1,0:T(8,128)(2,1)}, u32[]{:S(2)}) copy-start(bf16[1024,256]{1,0:T(8,128)(2,1)} %param.17) | copy-start | bytes 1572868
  12.1 9.9 %copy-start.2 = (bf16[1,1024,256]{2,1,0:T(8,128)(2,1)S(1)}, bf16[1,1024,256]{2,1,0:T(8,128)(2,1)}, u32[]{:S(2)}) copy-start(bf16[1,1024,256]{2,1,0:T(8,128)(2,1)} %param.19) | copy-start | bytes 1572868
  12.2 10.9 %copy-start.4 = (f32[256]{0:T(256)S(1)}, f32[256]{0:T(256)}, u32[]{:S(2)}) copy-start(f32[256]{0:T(256)} %param.18) | copy-start | bytes 3076
  12.2 71.1 %all-to-all-start = ((bf16[16,128,1024]{2,1,0:T(8,128)(2,1)}), bf16[16,128,1024]{2,1,0:T(8,128)(2,1)}, u32[]{:S(2)}, u32[]{:S(2)}) async-start(bf16[16,128,1024]{2,1,0:T(8,128)(2,1)} %pick_and_aggregate.1), calls=%async_computation | async-start | bytes 8388608 | tf_op jit(solution)/shard_map/all_to_all | solution.py:269
  92.2 31.6 %copy-start.3 = (bf16[256,1024]{1,0:T(8,128)(2,1)S(1)}, bf16[256,1024]{1,0:T(8,128)(2,1)}, u32[]{:S(2)}) copy-start(bf16[256,1024]{1,0:T(8,128)(2,1)} %get-tuple-element.6) | copy-start | bytes 1572868
  92.3 3.7 %collective-permute-start = (bf16[16,64,256]{2,1,0:T(8,128)(2,1)}, bf16[16,64,256]{2,1,0:T(8,128)(2,1)S(1)}, u32[]{:S(2)}, u32[]{:S(2)}) collective-permute-start(bf16[16,64,256]{2,1,0:T(8,128)(2,1)} %get-tuple-element.8), channel_id=1, source_target_pairs={{0,1},{1,0},{2,3},{3,2},{4,5},{5,4},{6,7},{7,6},{8,9},{9,8},{10,11... | collective-permute-start | bytes 1572872 | tf_op jit(solution)/shard_map/ppermute | solution.py:272
  112.2 3.9 %collective-permute-start.1 = (f32[64,256]{1,0:T(8,128)S(1)}, f32[64,256]{1,0:T(8,128)S(1)}, u32[]{:S(2)}, u32[]{:S(2)}) collective-permute-start(f32[64,256]{1,0:T(8,128)S(1)} %convert_reduce_fusion), channel_id=1, source_target_pairs={{0,2},{2,0},{4,6},{6,4},{1,3},{3,1},{5,7},{7,5},{8,10},{10,8},{12,... | collective-permute-start | bytes 196616 | tf_op jit(solution)/shard_map/ppermute | solution.py:275
  113.5 4.8 %collective-permute-start.2 = (f32[64,256]{1,0:T(8,128)S(1)}, f32[64,256]{1,0:T(8,128)S(1)}, u32[]{:S(2)}, u32[]{:S(2)}) collective-permute-start(f32[64,256]{1,0:T(8,128)S(1)} %convert_reduce_fusion), channel_id=1, source_target_pairs={{0,4},{2,6},{4,0},{6,2},{1,5},{3,7},{5,1},{7,3},{8,12},{10,14},{12... | collective-permute-start | bytes 196616 | tf_op jit(solution)/shard_map/ppermute | solution.py:275
  116.0 5.0 %collective-permute-start.3 = (f32[64,256]{1,0:T(8,128)S(1)}, f32[64,256]{1,0:T(8,128)S(1)}, u32[]{:S(2)}, u32[]{:S(2)}) collective-permute-start(f32[64,256]{1,0:T(8,128)S(1)} %convert_reduce_fusion), channel_id=1, source_target_pairs={{0,6},{2,4},{4,2},{6,0},{1,7},{3,5},{5,3},{7,1},{8,14},{10,12},{12... | collective-permute-start | bytes 196616 | tf_op jit(solution)/shard_map/ppermute | solution.py:275
  121.0 3.9 %collective-permute-start.4 = (f32[64,256]{1,0:T(8,128)S(1)}, f32[64,256]{1,0:T(8,128)S(1)}, u32[]{:S(2)}, u32[]{:S(2)}) collective-permute-start(f32[64,256]{1,0:T(8,128)S(1)} %add_add_fusion), channel_id=1, source_target_pairs={{0,1},{1,0},{2,3},{3,2},{4,5},{5,4},{6,7},{7,6},{8,9},{9,8},{10,11... | collective-permute-start | bytes 196616 | tf_op jit(solution)/shard_map/ppermute | solution.py:277

commit v7 on v5

--- a/solution.py
+++ b/solution.py
@@ -44,53 +44,45 @@
     return jnp.concatenate(rows, axis=0).astype(jnp.bfloat16)
 
 
-def pick_blocks(ids_ref, table_hbm, out_hbm, rows, vector, which, load, leave):
-    owners, _, owned = rows.shape
+def pick_kernel(ids_ref, table_hbm, out_ref, vector, which, load):
+    owners, _, owned = out_ref.shape
     per = owned // BLOCK
-    read_blocks(ids_ref, vector, which, load.at[owners])
+    read_blocks(ids_ref, vector, which, load.at[1])
 
     def start(r, carry):
         for b in range(per):
             pltpu.make_async_copy(
                 block_of(table_hbm.at, which[0, r * per + b]),
-                rows.at[r, :, b * BLOCK : (b + 1) * BLOCK],
-                load.at[r],
+                out_ref.at[r, :, b * BLOCK : (b + 1) * BLOCK],
+                load.at[0],
             ).start()
         return carry
 
     lax.fori_loop(0, owners, start, 0)
-    for r in range(owners):
-        pltpu.make_async_copy(rows.at[r], rows.at[r], load.at[r]).wait()
-        pltpu.make_async_copy(rows.at[r], out_hbm.at[r], leave.at[r]).start()
-    for r in range(owners):
-        pltpu.make_async_copy(rows.at[r], out_hbm.at[r], leave.at[r]).wait()
-
-
-def place_blocks(ids_ref, table_hbm, out_hbm, rows, table, vector, which, load, leave):
-    owners, _, owned = rows.shape
-    per = owned // BLOCK
-    known = table.at[:, pl.ds(0, table_hbm.shape[1])]
-    load_table = pltpu.make_async_copy(table_hbm, known, load.at[0])
-    load_table.start()
-    read_blocks(ids_ref, vector, which, load.at[owners])
-    load_table.wait()
-
-    def owner(r, carry):
-        placed = []
-        for b in range(per):
-            n = r * per + b
-            placed.append(in_run_order(block_of(table, which[0, n]), ids_ref[pl.ds(n, 1), :]))
-        for b in range(per):
-            rows[r, :, b * BLOCK : (b + 1) * BLOCK] = placed[b]
-        pltpu.make_async_copy(rows.at[r], out_hbm.at[r], leave.at[r]).start()
-        return carry
-
-    lax.fori_loop(0, owners, owner, 0)
-    for r in range(owners):
-        pltpu.make_async_copy(rows.at[r], out_hbm.at[r], leave.at[r]).wait()
-
-
-def aggregate_blocks(
+    pltpu.make_async_copy(out_ref, out_ref, load.at[0]).wait()
+
+
+def pick(ids, table, owners):
+    width, rows = table.shape
+    blocks = rows // BLOCK
+    vmem, anywhere = pl.BlockSpec(memory_space=pltpu.VMEM), pl.BlockSpec(memory_space=pl.ANY)
+    return pl.pallas_call(
+        pick_kernel,
+        in_specs=[vmem, anywhere],
+        out_specs=vmem,
+        out_shape=jax.ShapeDtypeStruct((owners, width, rows // 2 // owners), jnp.bfloat16),
+        scratch_shapes=[
+            pltpu.VMEM((8, blocks), jnp.int32),
+            pltpu.SMEM((8, blocks), jnp.int32),
+            pltpu.SemaphoreType.DMA((2,)),
+        ],
+        compiler_params=pltpu.CompilerParams(vmem_limit_bytes=WHOLE),
+        cost_estimate=pl.CostEstimate(flops=0, bytes_accessed=4 * MIB, transcendentals=0),
+        name="pick",
+    )(ids, table)
+
+
+def aggregate_kernel(
     lists_ref, counts_ref, ids_ref, table_hbm, tiles_hbm, out_hbm, rows, table, tiles, vector, which, load, leave
 ):
     blocks = ids_ref.shape[0]
@@ -142,47 +134,15 @@
         pltpu.make_async_copy(rows.at[r], out_hbm.at[r], leave.at[r]).wait()
 
 
-def first_kernel(
-    core_ref, lists_ref, counts_ref, ids_ref, table_hbm, tiles_hbm, out_hbm,
-    rows, table, tiles, vector, which, load, leave,
-):
-    @pl.when(core_ref[0] == 0)
-    def _():
-        pick_blocks(ids_ref, table_hbm, out_hbm, rows, vector, which, load, leave)
-
-    @pl.when(core_ref[0] == 1)
-    def _():
-        aggregate_blocks(
-            lists_ref, counts_ref, ids_ref, table_hbm, tiles_hbm, out_hbm,
-            rows, table, tiles, vector, which, load, leave,
-        )
-
-
-def second_kernel(
-    core_ref, lists_ref, counts_ref, ids_ref, table_hbm, tiles_hbm, out_hbm,
-    rows, table, tiles, vector, which, load, leave,
-):
-    @pl.when(core_ref[0] == 1)
-    def _():
-        place_blocks(ids_ref, table_hbm, out_hbm, rows, table, vector, which, load, leave)
-
-    @pl.when(core_ref[0] == 0)
-    def _():
-        aggregate_blocks(
-            lists_ref, counts_ref, ids_ref, table_hbm, tiles_hbm, out_hbm,
-            rows, table, tiles, vector, which, load, leave,
-        )
-
-
-def outgoing(kernel, core, lists, counts, ids, table, tiles, owners, name):
+def aggregate(lists, counts, ids, table, tiles, owners):
     width, rows = table.shape
     blocks = rows // BLOCK
     smem, vmem = pl.BlockSpec(memory_space=pltpu.SMEM), pl.BlockSpec(memory_space=pltpu.VMEM)
     anywhere = pl.BlockSpec(memory_space=pl.ANY)
     out = (owners, width, tiles.shape[0] // owners * BLOCK)
     return pl.pallas_call(
-        kernel,
-        in_specs=[smem, smem, smem, vmem, anywhere, anywhere],
+        aggregate_kernel,
+        in_specs=[smem, smem, vmem, anywhere, anywhere],
         out_specs=anywhere,
         out_shape=jax.ShapeDtypeStruct(out, jnp.bfloat16),
         scratch_shapes=[
@@ -196,26 +156,24 @@
         ],
         compiler_params=pltpu.CompilerParams(vmem_limit_bytes=WHOLE),
         cost_estimate=pl.CostEstimate(flops=4_000_000_000, bytes_accessed=20 * MIB, transcendentals=0),
-        name=name,
-    )(core, lists, counts, ids, table, tiles)
+        name="aggregate",
+    )(lists, counts, ids, table, tiles)
 
 
 def arrived_kernel(place_ref, ids_ref, moved_ref, weight_ref, bias_ref, rows_ref, pre_ref):
     step = pl.program_id(0)
     per = rows_ref.shape[1] // BLOCK
-    in_order = lax.broadcasted_iota(jnp.int32, (1, BLOCK), 1)
     for b in range(per):
         row = place_ref[1] + step * per + b
         within = jnp.bitwise_and(ids_ref[pl.ds(row, 1), :], BLOCK - 1)
-        within = jnp.where(place_ref[0] == 0, within, in_order)
         columns = slice(b * BLOCK, (b + 1) * BLOCK)
         rows_ref[:, columns] = dot(moved_ref[:, columns], selector(within)).astype(jnp.bfloat16)
-    pre_ref[...] = dot(weight_ref[0], rows_ref[...]) + bias_ref[...]
-
-
-def arrived(place, ids, moved, weights, bias):
+    pre_ref[...] = dot(weight_ref[...], rows_ref[...]) + bias_ref[...]
+
+
+def arrived(place, ids, moved, weight, bias):
     features, owned = moved.shape
-    hidden = weights.shape[1]
+    hidden = weight.shape[0]
     wide = 2 * BLOCK
     return pl.pallas_call(
         arrived_kernel,
@@ -225,7 +183,7 @@
             in_specs=[
                 pl.BlockSpec(memory_space=pltpu.VMEM),
                 pl.BlockSpec((features, wide), lambda i, place: (0, i)),
-                pl.BlockSpec((1, hidden, features), lambda i, place: (place[0], 0, 0)),
+                pl.BlockSpec(memory_space=pltpu.VMEM),
                 pl.BlockSpec(memory_space=pltpu.VMEM),
             ],
             out_specs=[
@@ -239,8 +197,8 @@
         ],
         compiler_params=pltpu.CompilerParams(vmem_limit_bytes=24 * MIB),
         cost_estimate=pl.CostEstimate(flops=2_000_000_000, bytes_accessed=6 * MIB, transcendentals=0),
-        name="first_arrived",
-    )(place, ids, moved, weights, bias)
+        name="own_arrived",
+    )(place, ids, moved, weight, bias)
 
 
 def gelu_and_slope(pre):
@@ -253,27 +211,29 @@
 
 
 def finish_kernel(
-    place_ref, pre_hbm, second_hbm, first_hbm, weights_hbm, upstream_hbm, hidden_hbm, keep_hbm, send_hbm,
-    pre_ref, second_ref, first_ref, weight_ref, upstream_ref, slope, hidden_ref, keep_ref, send_ref, load, leave,
+    place_ref, pre_hbm, agg_hbm, own_hbm, weight_hbm, upstream_hbm, hidden_hbm, keep_hbm, send_hbm,
+    pre_ref, rows, weight_ref, upstream_ref, slope, hidden_ref, keep_ref, send_ref, load, leave,
 ):
     owned = pre_ref.shape[1]
     wide = 2 * BLOCK
     core, limit = place_ref[0], place_ref[2]
 
-    load_weight = pltpu.make_async_copy(weights_hbm.at[1 - core], weight_ref, load.at[0])
-    load_second = pltpu.make_async_copy(second_hbm, second_ref, load.at[1])
+    own_slot, agg_slot = core, 1 - core
+
+    load_weight = pltpu.make_async_copy(weight_hbm, weight_ref, load.at[0])
+    load_agg = pltpu.make_async_copy(agg_hbm, rows.at[agg_slot], load.at[1])
     load_pre = pltpu.make_async_copy(pre_hbm, pre_ref, load.at[2])
     load_upstream = pltpu.make_async_copy(upstream_hbm, upstream_ref, load.at[3])
-    load_first = pltpu.make_async_copy(first_hbm, first_ref, load.at[4])
-    early = [load_weight, load_second, load_pre, load_upstream]
-    for copy in early + [load_first]:
+    load_own = pltpu.make_async_copy(own_hbm, rows.at[own_slot], load.at[4])
+    early = [load_weight, load_agg, load_pre, load_upstream]
+    for copy in early + [load_own]:
         copy.start()
     for copy in early:
         copy.wait()
 
     for j in range(0, owned, wide):
         columns = slice(j, j + wide)
-        active, back = gelu_and_slope(dot(weight_ref[...], second_ref[:, columns]) + pre_ref[:, columns])
+        active, back = gelu_and_slope(dot(weight_ref[...], rows[agg_slot, :, columns]) + pre_ref[:, columns])
         positions = j + lax.broadcasted_iota(jnp.int32, (1, wide), 1)
         valid = jnp.where(positions < limit, 1.0, 0.0)
         hidden_ref[:, columns] = (active * valid).astype(jnp.bfloat16)
@@ -284,16 +244,16 @@
     owners, share, _ = keep_ref.shape
     group = 4
 
-    def grads(left_ref, out_ref):
+    def grads(slot, out_ref):
         for i in range(0, owners, group):
-            total = dot(left_ref[i * share : (i + group) * share, :], slope[...], NT)
+            total = dot(rows[slot, i * share : (i + group) * share, :], slope[...], NT)
             out_ref[i : i + group] = total.reshape(group, share, -1).astype(out_ref.dtype)
 
-    grads(second_ref, send_ref)
+    load_own.wait()
+    grads(1, send_ref)
     leave_send = pltpu.make_async_copy(send_ref, send_hbm, leave.at[1])
     leave_send.start()
-    load_first.wait()
-    grads(first_ref, keep_ref)
+    grads(0, keep_ref)
     leave_keep = pltpu.make_async_copy(keep_ref, keep_hbm, leave.at[2])
     leave_keep.start()
     leave_hidden.wait()
@@ -301,9 +261,9 @@
     leave_keep.wait()
 
 
-def finish(place, pre, second, first, weights, upstream, owners):
+def finish(place, pre, agg, own, weight, upstream, owners):
     hidden, owned = pre.shape
-    features = second.shape[0]
+    features = agg.shape[0]
     part = (owners, features // owners, hidden)
     anywhere = pl.BlockSpec(memory_space=pl.ANY)
     outs = [
@@ -316,14 +276,19 @@
         in_specs=[pl.BlockSpec(memory_space=pltpu.SMEM)] + [anywhere] * 5,
         out_specs=[anywhere] * 3,
         out_shape=outs,
-        scratch_shapes=[pltpu.VMEM(a.shape, a.dtype) for a in (pre, second, first, weights[0], upstream)]
-        + [pltpu.VMEM((hidden, owned), jnp.bfloat16)]
+        scratch_shapes=[
+            pltpu.VMEM(pre.shape, pre.dtype),
+            pltpu.VMEM((2, features, owned), jnp.bfloat16),
+            pltpu.VMEM(weight.shape, weight.dtype),
+            pltpu.VMEM(upstream.shape, upstream.dtype),
+            pltpu.VMEM((hidden, owned), jnp.bfloat16),
+        ]
         + [pltpu.VMEM(a.shape, a.dtype) for a in outs]
         + [pltpu.SemaphoreType.DMA((5,)), pltpu.SemaphoreType.DMA((3,))],
         compiler_params=pltpu.CompilerParams(vmem_limit_bytes=WHOLE),
         cost_estimate=pl.CostEstimate(flops=2_000_000_000, bytes_accessed=9 * MIB, transcendentals=262144),
         name="finish",
-    )(place, pre, second, first, weights, upstream)
+    )(place, pre, agg, own, weight, upstream)
 
 
 def on_device(
@@ -338,21 +303,19 @@
 
     lists = jnp.transpose(block_lists, (2, 0, 1))
     place = jnp.stack([core, rank * (owned // BLOCK), batch_sizes[0] - rank * owned])
-    operands = (core.reshape(1), lists, block_counts, ids, table, tiles[0], owners)
-    weights = jnp.stack([w_self.T, w_neigh.T])
-
-    first = outgoing(first_kernel, *operands, "first_outgoing")
-    moved = lax.all_to_all(first, FEAT, split_axis=0, concat_axis=0, tiled=True)
-    second = outgoing(second_kernel, *operands, "second_outgoing")
-    second = lax.all_to_all(second, FEAT, split_axis=0, concat_axis=0, tiled=True)
-    first, pre = arrived(place, ids, moved.reshape(-1, owned), weights, bias[:, None])
-    second = second.reshape(-1, owned)
-    hidden, keep, send = finish(place, pre, second, first, weights, cotangent[0].T, owners)
+
+    mine = pick(ids, table, owners)
+    moved = lax.all_to_all(mine, FEAT, split_axis=0, concat_axis=0, tiled=True)
+    agg = aggregate(lists, block_counts, ids, table, tiles[0], owners)
+    agg = lax.all_to_all(agg, FEAT, split_axis=0, concat_axis=0, tiled=True).reshape(-1, owned)
+    own, pre = arrived(place, ids, moved.reshape(-1, owned), w_self.T, bias[:, None])
+    hidden, keep, send = finish(place, pre, agg, own, w_neigh.T, cotangent[0].T, owners)
 
     got = lax.ppermute(send, "core", [(0, 1), (1, 0)])
     parts = lax.all_to_all((keep + got).astype(jnp.bfloat16), FEAT, split_axis=0, concat_axis=0, tiled=True)
-    total = jnp.sum(parts, axis=0, dtype=jnp.float32)
+    total = jnp.sum(parts, axis=0, dtype=jnp.float32).astype(jnp.bfloat16)
     others = [lax.ppermute(total, "x", [(i, i ^ k) for i in range(4)]) for k in (1, 2, 3)]
+    total, *others = [term.astype(jnp.float32) for term in (total, *others)]
     total = (total + others[0]) + (others[1] + others[2])
     other = lax.ppermute(total, "core", [(0, 1), (1, 0)])
     first_core = core == 0

time: 114 us -> 117 us (1.026)
  starting transfers between devices: 19.6 us -> 24.8 us
  Pallas kernels: 28 us -> 26.6 us
  other arithmetic: 3.49 us -> 2.2 us
    ppermute x1, starting transfers between devices: 0.08 us -> 4.85 us  [on_device(): got = lax.ppermute(send, 'core', [(0, 1), (1, 0)])]
    pallas_call x2, Pallas kernels: 17.4 us -> 16 us  [the longest x1 11.3 us: aggregate(): pl.pallas_call(aggregate_kernel, in_specs=[smem, smem, vmem, anywhere, an...]
    all_to_all x2, waiting for transfers between devices: 32.9 us -> 34.3 us  [the longest x1 19.2 us: on_device(): moved = lax.all_to_all(mine, FEAT, split_axis=0, concat_axis=0, tiled=True)]
    another operation x1 -> x0, other arithmetic: 1.3 us -> none  [on_device(): weights = jnp.stack([w_self.T, w_neigh.T])]
    unnamed x22 -> x18, local copies, waits for them, and re-layouts: 7.48 us -> 7.65 us
  transfers between devices with their start and end apart: 7 -> 7, of which waited for: 5 -> 5; matrix products, arithmetic and copies ran while one was open for 6% -> 5% of each run, Pallas kernels for 9% -> 13%
where the time goes in v7:
time: 117 us
  waiting for transfers between devices  40.3 us (34%)
  Pallas kernels  26.6 us (23%)
  starting transfers between devices  24.8 us (21%)
  blocking collectives  13.5 us (12%)
  local copies, waits for them, and re-layouts  7.78 us (7%)
  other arithmetic  2.2 us (2%)
  between operations  1.47 us (1%)
    all_to_all x1, waiting for transfers between devices, on_device(): moved = lax.all_to_all(mine, FEAT, split_axis=0, concat_axis=0, tiled=True)  19.2 us
    all_to_all x1, waiting for transfers between devices, on_device(): lax.all_to_all(agg, FEAT, split_axis=0, concat_axis=0, tiled=True)  15.1 us
    all_to_all x1, blocking collectives, on_device(): lax.all_to_all((keep + got).astype(jnp.bfloat16), FEAT, split_axis=0, con...  13.5 us
    pallas_call x1, Pallas kernels, aggregate(): pl.pallas_call(aggregate_kernel, in_specs=[smem, smem, vmem, anywhere, an...  11.3 us
    all_to_all x1, starting transfers between devices, on_device(): moved = lax.all_to_all(mine, FEAT, split_axis=0, concat_axis=0, tiled=True)  8.61 us
    unnamed x18, local copies, waits for them, and re-layouts  7.65 us
    pallas_call x1, Pallas kernels, finish(): pl.pallas_call(finish_kernel, in_specs=[pl.BlockSpec(memory_space=pltpu.S...  6.55 us
    ppermute x1, starting transfers between devices, on_device(): got = lax.ppermute(send, 'core', [(0, 1), (1, 0)])  4.85 us
  transfers between devices with their start and end apart: 7, of which 5 were waited for; matrix products, arithmetic and copies ran while one was open for 5% of the time, Pallas kernels for 13%

profile of v7, /device:TPU:1, one launch (start us, length us, event | category | flops | bytes accessed | tf_op | source)
XLA Modules:
  0.0 116.5 jit_solution(11641419269740974202)
XLA Ops:
  0.6 4.7 %pick.1 = bf16[16,64,1024]{2,1,0:T(8,128)(2,1)} custom-call(s32[256,128]{1,0:T(8,128)} %bitcast.23, bf16[64,32768]{1,0:T(8,128)(2,1)} %bitcast.27), custom_call_target="tpu_custom_call" | custom-call | bytes 4194304 | tf_op jit(solution)/shard_map/pick/pallas_call | solution.py:69
  5.3 8.6 %all-to-all-start = ((bf16[16,64,1024]{2,1,0:T(8,128)(2,1)}), bf16[16,64,1024]{2,1,0:T(8,128)(2,1)S(1)}, u32[]{:S(2)}, u32[]{:S(2)}) async-start(bf16[16,64,1024]{2,1,0:T(8,128)(2,1)} %pick.1), calls=%async_computation | async-start | bytes 4194304 | tf_op jit(solution)/shard_map/all_to_all | solution.py:308
  13.9 11.3 %aggregate.1 = bf16[16,64,1024]{2,1,0:T(8,128)(2,1)} custom-call(s32[3,1,128]{2,1,0:T(1,128)} %bitcast.33, s32[1,128]{1,0:T(1,128)} %counts_ref.1, s32[256,128]{1,0:T(8,128)} %bitcast.24, bf16[64,32768]{1,0:T(8,128)(2,1)} %bitcast.28, bf16[128,3,128,128]{3,2,1,0:T(8,128)(2,1)} %bitcast.29), custom_call_target="tpu_custom_call" | custom-call | flops 4000000000 | bytes 20971520 | tf_op jit(solution)/shard_map/aggregate/pallas_call | solution.py:143
  25.3 19.2 %all-to-all-done = bf16[16,64,1024]{2,1,0:T(8,128)(2,1)S(1)} async-done(((bf16[16,64,1024]{2,1,0:T(8,128)(2,1)}), bf16[16,64,1024]{2,1,0:T(8,128)(2,1)S(1)}, u32[]{:S(2)}, u32[]{:S(2)}) %all-to-all-start) | async-done | bytes 2097184 | tf_op jit(solution)/shard_map/all_to_all | solution.py:308
  44.4 4.4 %all-to-all-start.1 = ((bf16[16,64,1024]{2,1,0:T(8,128)(2,1)}), bf16[16,64,1024]{2,1,0:T(8,128)(2,1)}, u32[]{:S(2)}, u32[]{:S(2)}) async-start(bf16[16,64,1024]{2,1,0:T(8,128)(2,1)} %aggregate.1), calls=%async_computation.1 | async-start | bytes 4194304 | tf_op jit(solution)/shard_map/all_to_all | solution.py:310
  49.6 0.2 copy.17
  50.0 2.0 %copy.19 = bf16[1024,256]{0,1:T(8,128)(2,1)} copy(bf16[1024,256]{1,0:T(8,128)(2,1)} %param.17) | data formatting | bytes 1048576 | tf_op args[7]
  52.0 2.1 %copy.20 = bf16[1,1024,256]{1,2,0:T(8,128)(2,1)} copy(bf16[1,1024,256]{2,1,0:T(8,128)(2,1)} %param.19) | data formatting | bytes 1048576 | tf_op args[9]
  54.1 4.0 %own_arrived.1 = (bf16[1024,1024]{1,0:T(8,128)(2,1)S(1)}, f32[256,1024]{1,0:T(8,128)S(1)}) custom-call(s32[3]{0:T(128)S(1)} %pad_add_fusion.place_ref, s32[256,128]{1,0:T(8,128)S(1)} %bitcast.25, bf16[1024,1024]{1,0:T(8,128)(2,1)S(1)} %bitcast.22, bf16[256,1024]{1,0:T(8,128)(2,1)S(1)} %bitcast.26, f32[256,1]{1,0:T(8,128)S(1)} %copy.18.bias_ref), custom_call_target="tpu_custom_call" | custom-call | flops 2000000000 | bytes 6291456 | tf_op jit(solution)/shard_map/own_arrived/pallas_call | solution.py:178
  58.2 1.3 %copy-done.2 = bf16[1024,1024]{1,0:T(8,128)(2,1)} copy-done((bf16[1024,1024]{1,0:T(8,128)(2,1)}, bf16[1024,1024]{1,0:T(8,128)(2,1)S(1)}, u32[]{:S(2)}) %copy-start.2) | copy-done | bytes 2097176
  59.5 1.0 copy-done.3
  60.5 15.1 %all-to-all-done.1 = bf16[16,64,1024]{2,1,0:T(8,128)(2,1)} async-done(((bf16[16,64,1024]{2,1,0:T(8,128)(2,1)}), bf16[16,64,1024]{2,1,0:T(8,128)(2,1)}, u32[]{:S(2)}, u32[]{:S(2)}) %all-to-all-start.1) | async-done | bytes 2097184 | tf_op jit(solution)/shard_map/all_to_all | solution.py:310
  75.6 6.6 %finish.1 = (bf16[256,1024]{1,0:T(8,128)(2,1)}, f32[16,64,256]{2,1,0:T(8,128)}, bf16[16,64,256]{2,1,0:T(8,128)(2,1)}) custom-call(s32[3]{0:T(128)} %copy-done.1, f32[256,1024]{1,0:T(8,128)} %copy-done.3, bf16[1024,1024]{1,0:T(8,128)(2,1)} %bitcast.13.agg_hbm, bf16[1024,1024]{1,0:T(8,128)(2,1)} %copy-done.2, bf16[256,1024]{1,0:T(8,128)(2,1)} %bitcast.31, ...), custom_call_target="tpu_custom_call" | custom-call | flops 2000000000 | bytes 9437184 | tf_op jit(solution)/shard_map/finish/pallas_call | solution.py:274
  82.2 4.8 %collective-permute-start = (bf16[16,64,256]{2,1,0:T(8,128)(2,1)}, bf16[16,64,256]{2,1,0:T(8,128)(2,1)S(1)}, u32[]{:S(2)}, u32[]{:S(2)}) collective-permute-start(bf16[16,64,256]{2,1,0:T(8,128)(2,1)} %get-tuple-element.12), channel_id=1, source_target_pairs={{0,1},{1,0},{2,3},{3,2},{4,5},{5,4},{6,7},{7,6},{8,9},{9,8},{10,11... | collective-permute-start | bytes 1572872 | tf_op jit(solution)/shard_map/ppermute | solution.py:314
  87.0 1.7 %collective-permute-done = bf16[16,64,256]{2,1,0:T(8,128)(2,1)S(1)} collective-permute-done((bf16[16,64,256]{2,1,0:T(8,128)(2,1)}, bf16[16,64,256]{2,1,0:T(8,128)(2,1)S(1)}, u32[]{:S(2)}, u32[]{:S(2)}) %collective-permute-start) | collective-permute-done | bytes 524320 | tf_op jit(solution)/shard_map/ppermute | solution.py:314
  88.8 1.4 %add_convert_fusion = bf16[16,64,256]{2,1,0:T(8,128)(2,1)S(1)} fusion(f32[16,64,256]{2,1,0:T(8,128)} %get-tuple-element.11, bf16[16,64,256]{2,1,0:T(8,128)(2,1)S(1)} %collective-permute-done), kind=kLoop, calls=%fused_computation | loop fusion | flops 786432 | bytes 2097152 | tf_op jit(solution)/shard_map/convert_element_type | solution.py:315
  90.2 13.5 %all_to_all.15 = bf16[16,64,256]{2,1,0:T(8,128)(2,1)S(1)} all-to-all(bf16[16,64,256]{2,1,0:T(8,128)(2,1)S(1)} %add_convert_fusion), channel_id=1, replica_groups=mesh['z'=4,'y'=4,'x'=4,'core'=2] {'z','y'}, dimensions={0} | all-to-all | bytes 1048576 | tf_op jit(solution)/shard_map/all_to_all | solution.py:315
  103.7 1.3 %collective-permute-start.1 = (bf16[64,256]{1,0:T(8,128)(2,1)S(1)}, bf16[64,256]{1,0:T(8,128)(2,1)S(1)}, u32[]{:S(2)}, u32[]{:S(2)}) collective-permute-start(bf16[64,256]{1,0:T(8,128)(2,1)S(1)} %reduce_sum.12), channel_id=1, source_target_pairs={{0,2},{2,0},{4,6},{6,4},{1,3},{3,1},{5,7},{7,5},{8,10},{10,8},{12,... | collective-permute-start | bytes 98312 | tf_op jit(solution)/shard_map/ppermute | solution.py:317
  105.0 2.5 %collective-permute-start.2 = (bf16[64,256]{1,0:T(8,128)(2,1)S(1)}, bf16[64,256]{1,0:T(8,128)(2,1)S(1)}, u32[]{:S(2)}, u32[]{:S(2)}) collective-permute-start(bf16[64,256]{1,0:T(8,128)(2,1)S(1)} %reduce_sum.12), channel_id=1, source_target_pairs={{0,4},{2,6},{4,0},{6,2},{1,5},{3,7},{5,1},{7,3},{8,12},{10,14},{12... | collective-permute-start | bytes 98312 | tf_op jit(solution)/shard_map/ppermute | solution.py:317
  107.6 1.6 %collective-permute-done.2 = bf16[64,256]{1,0:T(8,128)(2,1)S(1)} collective-permute-done((bf16[64,256]{1,0:T(8,128)(2,1)S(1)}, bf16[64,256]{1,0:T(8,128)(2,1)S(1)}, u32[]{:S(2)}, u32[]{:S(2)}) %collective-permute-start.2) | collective-permute-done | bytes 32800 | tf_op jit(solution)/shard_map/ppermute | solution.py:317
  109.3 2.7 %collective-permute-done.3 = bf16[64,256]{1,0:T(8,128)(2,1)S(1)} collective-permute-done((bf16[64,256]{1,0:T(8,128)(2,1)S(1)}, bf16[64,256]{1,0:T(8,128)(2,1)S(1)}, u32[]{:S(2)}, u32[]{:S(2)}) %collective-permute-start.3) | collective-permute-done | bytes 32800 | tf_op jit(solution)/shard_map/ppermute | solution.py:317
  112.0 2.9 %collective-permute-start.4 = (f32[64,256]{1,0:T(8,128)S(1)}, f32[64,256]{1,0:T(8,128)S(1)}, u32[]{:S(2)}, u32[]{:S(2)}) collective-permute-start(f32[64,256]{1,0:T(8,128)S(1)} %add_add_fusion), channel_id=1, source_target_pairs={{0,1},{1,0},{2,3},{3,2},{4,5},{5,4},{6,7},{7,6},{8,9},{9,8},{10,11... | collective-permute-start | bytes 196616 | tf_op jit(solution)/shard_map/ppermute | solution.py:320
  114.9 1.0 copy.21
  115.9 0.7 broadcast_select_fusion
  (19 shorter events, 0.5 us)
Async XLA Ops:
  5.3 39.1 %all-to-all-start = ((bf16[16,64,1024]{2,1,0:T(8,128)(2,1)}), bf16[16,64,1024]{2,1,0:T(8,128)(2,1)S(1)}, u32[]{:S(2)}, u32[]{:S(2)}) async-start(bf16[16,64,1024]{2,1,0:T(8,128)(2,1)} %pick.1), calls=%async_computation | async-start | bytes 4194304 | tf_op jit(solution)/shard_map/all_to_all | solution.py:308
  25.2 24.4 %copy-start.4 = (bf16[1024,256]{1,0:T(8,128)(2,1)S(1)}, bf16[1024,256]{1,0:T(8,128)(2,1)}, u32[]{:S(2)}) copy-start(bf16[1024,256]{1,0:T(8,128)(2,1)} %param.16) | copy-start | bytes 1572868
  25.2 24.6 %copy-start.6 = (f32[256]{0:T(256)S(1)}, f32[256]{0:T(256)}, u32[]{:S(2)}) copy-start(f32[256]{0:T(256)} %param.18) | copy-start | bytes 3076
  44.4 31.2 %all-to-all-start.1 = ((bf16[16,64,1024]{2,1,0:T(8,128)(2,1)}), bf16[16,64,1024]{2,1,0:T(8,128)(2,1)}, u32[]{:S(2)}, u32[]{:S(2)}) async-start(bf16[16,64,1024]{2,1,0:T(8,128)(2,1)} %aggregate.1), calls=%async_computation.1 | async-start | bytes 4194304 | tf_op jit(solution)/shard_map/all_to_all | solution.py:310
  48.9 5.3 %copy-start = (s32[1,32768]{1,0:T(1,128)S(1)}, s32[1,32768]{1,0:T(1,128)}, u32[]{:S(2)}) copy-start(s32[1,32768]{1,0:T(1,128)} %param.11) | copy-start | bytes 393220
  54.1 4.1 %copy-start.1 = (s32[3]{0:T(128)}, s32[3]{0:T(128)S(1)}, u32[]{:S(2)}) copy-start(s32[3]{0:T(128)S(1)} %pad_add_fusion.place_ref) | copy-start | bytes 40
  58.2 1.3 %copy-start.2 = (bf16[1024,1024]{1,0:T(8,128)(2,1)}, bf16[1024,1024]{1,0:T(8,128)(2,1)S(1)}, u32[]{:S(2)}) copy-start(bf16[1024,1024]{1,0:T(8,128)(2,1)S(1)} %get-tuple-element.9.own_hbm) | copy-start | bytes 6291460
  59.5 1.0 copy-start.3
  82.2 32.7 %copy-start.5 = (bf16[256,1024]{1,0:T(8,128)(2,1)S(1)}, bf16[256,1024]{1,0:T(8,128)(2,1)}, u32[]{:S(2)}) copy-start(bf16[256,1024]{1,0:T(8,128)(2,1)} %get-tuple-element.10) | copy-start | bytes 1572868
  82.2 6.6 %collective-permute-start = (bf16[16,64,256]{2,1,0:T(8,128)(2,1)}, bf16[16,64,256]{2,1,0:T(8,128)(2,1)S(1)}, u32[]{:S(2)}, u32[]{:S(2)}) collective-permute-start(bf16[16,64,256]{2,1,0:T(8,128)(2,1)} %get-tuple-element.12), channel_id=1, source_target_pairs={{0,1},{1,0},{2,3},{3,2},{4,5},{5,4},{6,7},{7,6},{8,9},{9,8},{10,11... | collective-permute-start | bytes 1572872 | tf_op jit(solution)/shard_map/ppermute | solution.py:314
  103.7 3.9 %collective-permute-start.1 = (bf16[64,256]{1,0:T(8,128)(2,1)S(1)}, bf16[64,256]{1,0:T(8,128)(2,1)S(1)}, u32[]{:S(2)}, u32[]{:S(2)}) collective-permute-start(bf16[64,256]{1,0:T(8,128)(2,1)S(1)} %reduce_sum.12), channel_id=1, source_target_pairs={{0,2},{2,0},{4,6},{6,4},{1,3},{3,1},{5,7},{7,5},{8,10},{10,8},{12,... | collective-permute-start | bytes 98312 | tf_op jit(solution)/shard_map/ppermute | solution.py:317
  105.0 4.3 %collective-permute-start.2 = (bf16[64,256]{1,0:T(8,128)(2,1)S(1)}, bf16[64,256]{1,0:T(8,128)(2,1)S(1)}, u32[]{:S(2)}, u32[]{:S(2)}) collective-permute-start(bf16[64,256]{1,0:T(8,128)(2,1)S(1)} %reduce_sum.12), channel_id=1, source_target_pairs={{0,4},{2,6},{4,0},{6,2},{1,5},{3,7},{5,1},{7,3},{8,12},{10,14},{12... | collective-permute-start | bytes 98312 | tf_op jit(solution)/shard_map/ppermute | solution.py:317
  107.4 4.5 %collective-permute-start.3 = (bf16[64,256]{1,0:T(8,128)(2,1)S(1)}, bf16[64,256]{1,0:T(8,128)(2,1)S(1)}, u32[]{:S(2)}, u32[]{:S(2)}) collective-permute-start(bf16[64,256]{1,0:T(8,128)(2,1)S(1)} %reduce_sum.12), channel_id=1, source_target_pairs={{0,6},{2,4},{4,2},{6,0},{1,7},{3,5},{5,3},{7,1},{8,14},{10,12},{12... | collective-permute-start | bytes 98312 | tf_op jit(solution)/shard_map/ppermute | solution.py:317
  112.0 3.9 %collective-permute-start.4 = (f32[64,256]{1,0:T(8,128)S(1)}, f32[64,256]{1,0:T(8,128)S(1)}, u32[]{:S(2)}, u32[]{:S(2)}) collective-permute-start(f32[64,256]{1,0:T(8,128)S(1)} %add_add_fusion), channel_id=1, source_target_pairs={{0,1},{1,0},{2,3},{3,2},{4,5},{5,4},{6,7},{7,6},{8,9},{9,8},{10,11... | collective-permute-start | bytes 196616 | tf_op jit(solution)/shard_map/ppermute | solution.py:320

commit v8 on v5

--- a/solution.py
+++ b/solution.py
@@ -106,11 +106,13 @@
     known = table.at[:, pl.ds(0, table_hbm.shape[1])]
     load_table = pltpu.make_async_copy(table_hbm, known, load.at[owners + 1])
     load_table.start()
-    for r in range(owners):
+    for r in range(together):
         load_tiles(r).start()
     table[:, table_hbm.shape[1] :] = jnp.zeros((width, BLOCK), table.dtype)
     read_blocks(ids_ref, vector, which, load.at[owners])
     load_table.wait()
+    for r in range(together, owners):
+        load_tiles(r).start()
 
     def one(d):
         count = counts_ref[0, d]
@@ -261,23 +263,32 @@
     core, limit = place_ref[0], place_ref[2]
 
     load_weight = pltpu.make_async_copy(weights_hbm.at[1 - core], weight_ref, load.at[0])
-    load_second = pltpu.make_async_copy(second_hbm, second_ref, load.at[1])
-    load_pre = pltpu.make_async_copy(pre_hbm, pre_ref, load.at[2])
-    load_upstream = pltpu.make_async_copy(upstream_hbm, upstream_ref, load.at[3])
-    load_first = pltpu.make_async_copy(first_hbm, first_ref, load.at[4])
-    early = [load_weight, load_second, load_pre, load_upstream]
-    for copy in early + [load_first]:
+    load_first = pltpu.make_async_copy(first_hbm, first_ref, load.at[1])
+    halves = []
+    for h in range(2):
+        columns = slice(h * owned // 2, (h + 1) * owned // 2)
+        pairs = ((second_hbm, second_ref), (pre_hbm, pre_ref), (upstream_hbm, upstream_ref))
+        halves.append(
+            [
+                pltpu.make_async_copy(source.at[:, columns], target.at[:, columns], load.at[2 + 3 * h + k])
+                for k, (source, target) in enumerate(pairs)
+            ]
+        )
+    load_weight.start()
+    for copy in halves[0] + halves[1] + [load_first]:
         copy.start()
-    for copy in early:
-        copy.wait()
-
-    for j in range(0, owned, wide):
-        columns = slice(j, j + wide)
-        active, back = gelu_and_slope(dot(weight_ref[...], second_ref[:, columns]) + pre_ref[:, columns])
-        positions = j + lax.broadcasted_iota(jnp.int32, (1, wide), 1)
-        valid = jnp.where(positions < limit, 1.0, 0.0)
-        hidden_ref[:, columns] = (active * valid).astype(jnp.bfloat16)
-        slope[:, columns] = (upstream_ref[:, columns].astype(jnp.float32) * back * valid).astype(jnp.bfloat16)
+    load_weight.wait()
+
+    for h in range(2):
+        for copy in halves[h]:
+            copy.wait()
+        for j in range(h * owned // 2, (h + 1) * owned // 2, wide):
+            columns = slice(j, j + wide)
+            active, back = gelu_and_slope(dot(weight_ref[...], second_ref[:, columns]) + pre_ref[:, columns])
+            positions = j + lax.broadcasted_iota(jnp.int32, (1, wide), 1)
+            valid = jnp.where(positions < limit, 1.0, 0.0)
+            hidden_ref[:, columns] = (active * valid).astype(jnp.bfloat16)
+            slope[:, columns] = (upstream_ref[:, columns].astype(jnp.float32) * back * valid).astype(jnp.bfloat16)
     leave_hidden = pltpu.make_async_copy(hidden_ref, hidden_hbm, leave.at[0])
     leave_hidden.start()
 
@@ -319,7 +330,7 @@
         scratch_shapes=[pltpu.VMEM(a.shape, a.dtype) for a in (pre, second, first, weights[0], upstream)]
         + [pltpu.VMEM((hidden, owned), jnp.bfloat16)]
         + [pltpu.VMEM(a.shape, a.dtype) for a in outs]
-        + [pltpu.SemaphoreType.DMA((5,)), pltpu.SemaphoreType.DMA((3,))],
+        + [pltpu.SemaphoreType.DMA((8,)), pltpu.SemaphoreType.DMA((3,))],
         compiler_params=pltpu.CompilerParams(vmem_limit_bytes=WHOLE),
         cost_estimate=pl.CostEstimate(flops=2_000_000_000, bytes_accessed=9 * MIB, transcendentals=262144),
         name="finish",
@@ -351,16 +362,12 @@
 
     got = lax.ppermute(send, "core", [(0, 1), (1, 0)])
     parts = lax.all_to_all((keep + got).astype(jnp.bfloat16), FEAT, split_axis=0, concat_axis=0, tiled=True)
-    total = jnp.sum(parts, axis=0, dtype=jnp.float32)
-    others = [lax.ppermute(total, "x", [(i, i ^ k) for i in range(4)]) for k in (1, 2, 3)]
-    total = (total + others[0]) + (others[1] + others[2])
-    other = lax.ppermute(total, "core", [(0, 1), (1, 0)])
-    first_core = core == 0
-    return (
-        hidden.T[None],
-        jnp.where(first_core, total, other),
-        jnp.where(first_core, other, total),
-    )
+    part = jnp.sum(parts, axis=0, dtype=jnp.float32).astype(jnp.bfloat16)
+    copies = jnp.broadcast_to(part[None], (lax.axis_size(GRP), *part.shape))
+    terms = lax.all_to_all(copies, GRP, split_axis=0, concat_axis=0, tiled=True)
+    terms = terms.reshape(-1, lax.axis_size("core"), *part.shape)
+    total = jnp.sum(terms, axis=0, dtype=jnp.float32)
+    return (hidden.T[None], total[0], total[1])
 
 
 def solution(mesh):

time: 114 us -> 115 us (level)
  local copies, waits for them, and re-layouts: 7.61 us -> 8.95 us
    ppermute x4 -> x0, starting transfers between devices: 6.44 us -> none  [the longest x3 3.94 us: on_device(): lax.ppermute(total, 'x', [(i, i ^ k) for i in range(4)])]
    all_to_all x0 -> x1, starting transfers between devices: none -> 5.64 us  [on_device(): terms = lax.all_to_all(copies, GRP, split_axis=0, concat_axis=0, tiled=True)]
    all_to_all x0 -> x1, waiting for transfers between devices: none -> 5.5 us  [on_device(): terms = lax.all_to_all(copies, GRP, split_axis=0, concat_axis=0, tiled=True)]
    ppermute x4 -> x0, waiting for transfers between devices: 4.87 us -> none  [the longest x3 4.87 us: on_device(): lax.ppermute(total, 'x', [(i, i ^ k) for i in range(4)])]
  transfers between devices with their start and end apart: 7 -> 4, of which waited for: 5 -> 4; matrix products, arithmetic and copies ran while one was open for 6% -> 6% of each run, Pallas kernels for 9% -> 9%
where the time goes in v8:
time: 115 us; the launch traced here: 114 us
  waiting for transfers between devices  40.7 us (35%)
  Pallas kernels  27.6 us (24%)
  starting transfers between devices  18.8 us (16%)
  blocking collectives  13.7 us (12%)
  local copies, waits for them, and re-layouts  8.95 us (8%)
  other arithmetic  2.91 us (3%)
  between operations  1.46 us (1%)
    all_to_all x1, waiting for transfers between devices, on_device(): moved = lax.all_to_all(first, FEAT, split_axis=0, concat_axis=0, tiled=True)  19.4 us
    pallas_call x2, Pallas kernels, outgoing(): pl.pallas_call(kernel, in_specs=[smem, smem, smem, vmem, anywhere, anywhe...  17.4 us
    all_to_all x1, blocking collectives, on_device(): lax.all_to_all((keep + got).astype(jnp.bfloat16), FEAT, split_axis=0, con...  13.7 us
    all_to_all x1, waiting for transfers between devices, on_device(): lax.all_to_all(second, FEAT, split_axis=0, concat_axis=0, tiled=True)  13.7 us
    all_to_all x1, starting transfers between devices, on_device(): moved = lax.all_to_all(first, FEAT, split_axis=0, concat_axis=0, tiled=True)  8.61 us
    unnamed x22, local copies, waits for them, and re-layouts  7.45 us
    pallas_call x1, Pallas kernels, finish(): pl.pallas_call(finish_kernel, in_specs=[pl.BlockSpec(memory_space=pltpu.S...  6.15 us
    all_to_all x1, starting transfers between devices, on_device(): terms = lax.all_to_all(copies, GRP, split_axis=0, concat_axis=0, tiled=True)  5.64 us
  transfers between devices with their start and end apart: 4, of which 4 were waited for; matrix products, arithmetic and copies ran while one was open for 6% of the time, Pallas kernels for 9%

profile of v8, /device:TPU:1, one launch (start us, length us, event | category | flops | bytes accessed | tf_op | source)
XLA Modules:
  0.0 114.2 jit_solution(5344819578173316128)
XLA Ops:
  0.6 11.3 %first_outgoing.1 = bf16[16,64,1024]{2,1,0:T(8,128)(2,1)} custom-call(s32[1]{0:T(128)} %bitcast.core_ref, s32[3,1,128]{2,1,0:T(1,128)} %bitcast.45, s32[1,128]{1,0:T(1,128)} %counts_ref.3, s32[256,128]{1,0:T(8,128)} %bitcast.33, bf16[64,32768]{1,0:T(8,128)(2,1)} %bitcast.38, bf16[128,3,128,128]{3,2,1,0:T(8,128)(2,1)} %bitcast.36), custom_call_target="tpu_custom_call" | custom-call | flops 4000000000 | bytes 20971520 | tf_op jit(solution)/shard_map/first_outgoing/pallas_call | solution.py:185
  11.9 8.6 %all-to-all-start = ((bf16[16,64,1024]{2,1,0:T(8,128)(2,1)}), bf16[16,64,1024]{2,1,0:T(8,128)(2,1)S(1)}, u32[]{:S(2)}, u32[]{:S(2)}) async-start(bf16[16,64,1024]{2,1,0:T(8,128)(2,1)} %first_outgoing.1), calls=%async_computation | async-start | bytes 4194304 | tf_op jit(solution)/shard_map/all_to_all | solution.py:356
  20.5 6.1 %second_outgoing.1 = bf16[16,64,1024]{2,1,0:T(8,128)(2,1)} custom-call(s32[1]{0:T(128)} %bitcast.core_ref, s32[3,1,128]{2,1,0:T(1,128)} %bitcast.46, s32[1,128]{1,0:T(1,128)} %counts_ref.3, s32[256,128]{1,0:T(8,128)} %bitcast.34, bf16[64,32768]{1,0:T(8,128)(2,1)} %bitcast.39, bf16[128,3,128,128]{3,2,1,0:T(8,128)(2,1)} %bitcast.37), custom_call_target="tpu_custom_call" | custom-call | flops 4000000000 | bytes 20971520 | tf_op jit(solution)/shard_map/second_outgoing/pallas_call | solution.py:185
  26.7 19.4 %all-to-all-done = bf16[16,64,1024]{2,1,0:T(8,128)(2,1)S(1)} async-done(((bf16[16,64,1024]{2,1,0:T(8,128)(2,1)}), bf16[16,64,1024]{2,1,0:T(8,128)(2,1)S(1)}, u32[]{:S(2)}, u32[]{:S(2)}) %all-to-all-start) | async-done | bytes 2097184 | tf_op jit(solution)/shard_map/all_to_all | solution.py:356
  46.1 4.4 %all-to-all-start.1 = ((bf16[16,64,1024]{2,1,0:T(8,128)(2,1)}), bf16[16,64,1024]{2,1,0:T(8,128)(2,1)}, u32[]{:S(2)}, u32[]{:S(2)}) async-start(bf16[16,64,1024]{2,1,0:T(8,128)(2,1)} %second_outgoing.1), calls=%async_computation.1 | async-start | bytes 4194304 | tf_op jit(solution)/shard_map/all_to_all | solution.py:358
  51.2 1.0 copy.22
  52.2 1.0 copy.23
  53.2 0.1 copy.24.bias_ref
  53.4 2.1 %copy.25 = bf16[1,1024,256]{1,2,0:T(8,128)(2,1)} copy(bf16[1,1024,256]{2,1,0:T(8,128)(2,1)} %param.19) | data formatting | bytes 1048576 | tf_op args[9]
  55.5 1.3 %pad_maximum_fusion.weight_ref.weights_hbm = bf16[2,256,1024]{2,1,0:T(8,128)(2,1)S(1)} fusion(bf16[1,256,1024]{2,1,0:T(8,128)(2,1)} %bitcast.41, bf16[1,256,1024]{2,1,0:T(8,128)(2,1)} %bitcast.40), kind=kLoop, calls=%fused_computation | loop fusion | flops 524288 | bytes 2097152 | tf_op jit(solution)/shard_map/stack | solution.py:353
  56.9 4.1 %first_arrived.1 = (bf16[1024,1024]{1,0:T(8,128)(2,1)S(1)}, f32[256,1024]{1,0:T(8,128)S(1)}) custom-call(s32[3]{0:T(128)S(1)} %pad_add_fusion.place_ref, s32[256,128]{1,0:T(8,128)S(1)} %bitcast.35, bf16[1024,1024]{1,0:T(8,128)(2,1)S(1)} %bitcast.32, bf16[2,256,1024]{2,1,0:T(8,128)(2,1)S(1)} %pad_maximum_fusion.weight_ref.weights_hbm, f32[256,1]{1,0:T(8,128)S(1)} %copy.24.bias_ref), custom_call_target="tpu_custom_call" | custom-call | flops 2000000000 | bytes 6291456 | tf_op jit(solution)/shard_map/first_arrived/pallas_call | solution.py:222
  60.9 1.3 %copy-done.3 = bf16[1024,1024]{1,0:T(8,128)(2,1)} copy-done((bf16[1024,1024]{1,0:T(8,128)(2,1)}, bf16[1024,1024]{1,0:T(8,128)(2,1)S(1)}, u32[]{:S(2)}) %copy-start.3) | copy-done | bytes 2097176
  62.3 1.0 copy-done.4
  63.3 13.7 %all-to-all-done.1 = bf16[16,64,1024]{2,1,0:T(8,128)(2,1)} async-done(((bf16[16,64,1024]{2,1,0:T(8,128)(2,1)}), bf16[16,64,1024]{2,1,0:T(8,128)(2,1)}, u32[]{:S(2)}, u32[]{:S(2)}) %all-to-all-start.1) | async-done | bytes 2097184 | tf_op jit(solution)/shard_map/all_to_all | solution.py:358
  77.0 6.1 %finish.1 = (bf16[256,1024]{1,0:T(8,128)(2,1)}, f32[16,64,256]{2,1,0:T(8,128)}, bf16[16,64,256]{2,1,0:T(8,128)(2,1)}) custom-call(s32[3]{0:T(128)} %copy-done.2, f32[256,1024]{1,0:T(8,128)} %copy-done.4, bf16[1024,1024]{1,0:T(8,128)(2,1)} %bitcast.16.second_hbm, bf16[1024,1024]{1,0:T(8,128)(2,1)} %copy-done.3, bf16[2,256,1024]{2,1,0:T(8,128)(2,1)} %copy-done, ...), custom_call_target="tpu_custom_call" | custom-call | flops 2000000000 | bytes 9437184 | tf_op jit(solution)/shard_map/finish/pallas_call | solution.py:325
  83.2 0.1 collective-permute-start
  83.3 2.1 %collective-permute-done = bf16[16,64,256]{2,1,0:T(8,128)(2,1)S(1)} collective-permute-done((bf16[16,64,256]{2,1,0:T(8,128)(2,1)}, bf16[16,64,256]{2,1,0:T(8,128)(2,1)S(1)}, u32[]{:S(2)}, u32[]{:S(2)}) %collective-permute-start) | collective-permute-done | bytes 524320 | tf_op jit(solution)/shard_map/ppermute | solution.py:363
  85.4 1.4 %add_convert_fusion = bf16[16,64,256]{2,1,0:T(8,128)(2,1)S(1)} fusion(f32[16,64,256]{2,1,0:T(8,128)} %get-tuple-element.11, bf16[16,64,256]{2,1,0:T(8,128)(2,1)S(1)} %collective-permute-done), kind=kLoop, calls=%fused_computation.1 | loop fusion | flops 786432 | bytes 2097152 | tf_op jit(solution)/shard_map/convert_element_type | solution.py:364
  86.8 13.7 %all_to_all.20 = bf16[16,64,256]{2,1,0:T(8,128)(2,1)S(1)} all-to-all(bf16[16,64,256]{2,1,0:T(8,128)(2,1)S(1)} %add_convert_fusion), channel_id=1, replica_groups=mesh['z'=4,'y'=4,'x'=4,'core'=2] {'z','y'}, dimensions={0} | all-to-all | bytes 1048576 | tf_op jit(solution)/shard_map/all_to_all | solution.py:364
  100.6 0.7 broadcast_in_dim.14
  101.3 5.6 %all-to-all-start.3 = ((bf16[8,64,256]{2,1,0:T(8,128)(2,1)}), bf16[8,64,256]{2,1,0:T(8,128)(2,1)S(1)}, u32[]{:S(2)}, u32[]{:S(2)}) async-start(bf16[8,64,256]{2,1,0:T(8,128)(2,1)} %broadcast_in_dim.14), calls=%async_computation.3 | async-start | bytes 524288 | tf_op jit(solution)/shard_map/all_to_all | solution.py:367
  107.0 1.0 copy.26
  108.0 5.5 %all-to-all-done.3 = bf16[8,64,256]{2,1,0:T(8,128)(2,1)S(1)} async-done(((bf16[8,64,256]{2,1,0:T(8,128)(2,1)}), bf16[8,64,256]{2,1,0:T(8,128)(2,1)S(1)}, u32[]{:S(2)}, u32[]{:S(2)}) %all-to-all-start.3) | async-done | bytes 262176 | tf_op jit(solution)/shard_map/all_to_all | solution.py:367
  113.5 0.7 slice_bitcast_fusion
  (19 shorter events, 0.2 us)
Async XLA Ops:
  11.9 34.2 %all-to-all-start = ((bf16[16,64,1024]{2,1,0:T(8,128)(2,1)}), bf16[16,64,1024]{2,1,0:T(8,128)(2,1)S(1)}, u32[]{:S(2)}, u32[]{:S(2)}) async-start(bf16[16,64,1024]{2,1,0:T(8,128)(2,1)} %first_outgoing.1), calls=%async_computation | async-start | bytes 4194304 | tf_op jit(solution)/shard_map/all_to_all | solution.py:356
  26.7 24.5 %copy-start.5 = (bf16[1024,256]{1,0:T(8,128)(2,1)S(1)}, bf16[1024,256]{1,0:T(8,128)(2,1)}, u32[]{:S(2)}) copy-start(bf16[1024,256]{1,0:T(8,128)(2,1)} %param.16) | copy-start | bytes 1572868
  26.7 25.5 %copy-start.6 = (bf16[1024,256]{1,0:T(8,128)(2,1)S(1)}, bf16[1024,256]{1,0:T(8,128)(2,1)}, u32[]{:S(2)}) copy-start(bf16[1024,256]{1,0:T(8,128)(2,1)} %param.17) | copy-start | bytes 1572868
  46.1 30.9 %all-to-all-start.1 = ((bf16[16,64,1024]{2,1,0:T(8,128)(2,1)}), bf16[16,64,1024]{2,1,0:T(8,128)(2,1)}, u32[]{:S(2)}, u32[]{:S(2)}) async-start(bf16[16,64,1024]{2,1,0:T(8,128)(2,1)} %second_outgoing.1), calls=%async_computation.1 | async-start | bytes 4194304 | tf_op jit(solution)/shard_map/all_to_all | solution.py:358
  50.5 2.7 %copy-start.8 = (f32[256]{0:T(256)S(1)}, f32[256]{0:T(256)}, u32[]{:S(2)}) copy-start(f32[256]{0:T(256)} %param.18) | copy-start | bytes 3076
  52.2 4.6 %copy-start.1 = (s32[1,32768]{1,0:T(1,128)S(1)}, s32[1,32768]{1,0:T(1,128)}, u32[]{:S(2)}) copy-start(s32[1,32768]{1,0:T(1,128)} %param.11) | copy-start | bytes 393220
  55.5 5.4 %copy-start.2 = (s32[3]{0:T(128)}, s32[3]{0:T(128)S(1)}, u32[]{:S(2)}) copy-start(s32[3]{0:T(128)S(1)} %pad_add_fusion.place_ref) | copy-start | bytes 40
  56.8 4.1 %copy-start = (bf16[2,256,1024]{2,1,0:T(8,128)(2,1)}, bf16[2,256,1024]{2,1,0:T(8,128)(2,1)S(1)}, u32[]{:S(2)}) copy-start(bf16[2,256,1024]{2,1,0:T(8,128)(2,1)S(1)} %pad_maximum_fusion.weight_ref.weights_hbm) | copy-start | bytes 3145732
  60.9 1.3 %copy-start.3 = (bf16[1024,1024]{1,0:T(8,128)(2,1)}, bf16[1024,1024]{1,0:T(8,128)(2,1)S(1)}, u32[]{:S(2)}) copy-start(bf16[1024,1024]{1,0:T(8,128)(2,1)S(1)} %get-tuple-element.9.first_hbm) | copy-start | bytes 6291460
  62.3 1.0 copy-start.4
  83.2 2.2 %collective-permute-start = (bf16[16,64,256]{2,1,0:T(8,128)(2,1)}, bf16[16,64,256]{2,1,0:T(8,128)(2,1)S(1)}, u32[]{:S(2)}, u32[]{:S(2)}) collective-permute-start(bf16[16,64,256]{2,1,0:T(8,128)(2,1)} %get-tuple-element.12), channel_id=1, source_target_pairs={{0,1},{1,0},{2,3},{3,2},{4,5},{5,4},{6,7},{7,6},{8,9},{9,8},{10,11... | collective-permute-start | bytes 1572872 | tf_op jit(solution)/shard_map/ppermute | solution.py:363
  85.4 21.6 %copy-start.7 = (bf16[256,1024]{1,0:T(8,128)(2,1)S(1)}, bf16[256,1024]{1,0:T(8,128)(2,1)}, u32[]{:S(2)}) copy-start(bf16[256,1024]{1,0:T(8,128)(2,1)} %get-tuple-element.10) | copy-start | bytes 1572868
  101.3 12.1 %all-to-all-start.3 = ((bf16[8,64,256]{2,1,0:T(8,128)(2,1)}), bf16[8,64,256]{2,1,0:T(8,128)(2,1)S(1)}, u32[]{:S(2)}, u32[]{:S(2)}) async-start(bf16[8,64,256]{2,1,0:T(8,128)(2,1)} %broadcast_in_dim.14), calls=%async_computation.3 | async-start | bytes 524288 | tf_op jit(solution)/shard_map/all_to_all | solution.py:367

commit v9 on v6

--- a/solution.py
+++ b/solution.py
@@ -45,7 +45,7 @@
 
 
 def outgoing_kernel(
-    lists_ref, counts_ref, ids_ref, table_hbm, tiles_hbm, out_hbm, rows, table, tiles, vector, which, load, leave
+    batch_ref, lists_ref, counts_ref, ids_ref, table_hbm, tiles_hbm, out_hbm, size_ref, rows, table, tiles, vector, which, load, leave
 ):
     blocks = ids_ref.shape[0]
     owners, width, owned = rows.shape
@@ -61,11 +61,14 @@
     known = table.at[:, pl.ds(0, table_hbm.shape[1])]
     load_table = pltpu.make_async_copy(table_hbm, known, load.at[owners + 1])
     load_table.start()
-    for r in range(owners):
+    for r in range(together):
         load_tiles(r).start()
+    size_ref[...] = jnp.full(size_ref.shape, batch_ref[0], jnp.int32)
     table[:, table_hbm.shape[1] :] = jnp.zeros((width, BLOCK), table.dtype)
     read_blocks(ids_ref, vector, which, load.at[owners])
     load_table.wait()
+    for r in range(together, owners):
+        load_tiles(r).start()
 
     def aggregated(d):
         count = counts_ref[0, d]
@@ -101,7 +104,7 @@
         pltpu.make_async_copy(rows.at[r], out_hbm.at[r], leave.at[r]).wait()
 
 
-def outgoing(lists, counts, ids, table, tiles, owners):
+def outgoing(batch, lists, counts, ids, table, tiles, owners):
     width, rows = table.shape
     blocks = rows // BLOCK
     smem, vmem = pl.BlockSpec(memory_space=pltpu.SMEM), pl.BlockSpec(memory_space=pltpu.VMEM)
@@ -109,9 +112,9 @@
     out = (owners, 2 * width, tiles.shape[0] // owners * BLOCK)
     return pl.pallas_call(
         outgoing_kernel,
-        in_specs=[smem, smem, vmem, anywhere, anywhere],
-        out_specs=anywhere,
-        out_shape=jax.ShapeDtypeStruct(out, jnp.bfloat16),
+        in_specs=[smem, smem, smem, vmem, anywhere, anywhere],
+        out_specs=[anywhere, vmem],
+        out_shape=[jax.ShapeDtypeStruct(out, jnp.bfloat16), jax.ShapeDtypeStruct((8, BLOCK), jnp.int32)],
         scratch_shapes=[
             pltpu.VMEM(out, jnp.bfloat16),
             pltpu.VMEM((width, rows + BLOCK), jnp.bfloat16),
@@ -124,7 +127,7 @@
         compiler_params=pltpu.CompilerParams(vmem_limit_bytes=WHOLE),
         cost_estimate=pl.CostEstimate(flops=4_000_000_000, bytes_accessed=20 * MIB, transcendentals=0),
         name="pick_and_aggregate",
-    )(lists, counts, ids, table, tiles)
+    )(batch, lists, counts, ids, table, tiles)
 
 
 def gelu_and_slope(pre):
@@ -143,17 +146,20 @@
 
 
 def finish_kernel(
-    place_ref, bias_ref, ids_hbm, moved_hbm, weights_hbm, upstream_hbm, hidden_hbm, keep_hbm, send_hbm,
-    ids_ref, rows, weights, upstream_ref, slopes, hidden_ref, keep_ref, send_ref, load, leave,
+    size_ref, bias_ref, ids_hbm, moved_hbm, self_hbm, neigh_hbm, upstream_hbm, hidden_hbm, keep_hbm, send_hbm,
+    ids_ref, rows, weights, turned, upstream_ref, slopes, hidden_ref, keep_ref, send_ref, load, leave,
 ):
     owners, share, owned = rows.shape[1:]
     features = owners * share
     per = owned // BLOCK
-    core, rank, limit = place_ref[0], place_ref[1], place_ref[2]
+    rank, core = lax.axis_index(FEAT), lax.axis_index("core")
     own_slot, agg_slot = core, 1 - core
 
     load_ids = pltpu.make_async_copy(ids_hbm.at[pl.ds(pl.multiple_of(rank * per, per), per)], ids_ref, load.at[0])
-    load_weights = pltpu.make_async_copy(weights_hbm, weights, load.at[1])
+    load_weights = [
+        pltpu.make_async_copy(source, weights.at[k], load.at[1 + k]) for k, source in enumerate((self_hbm, neigh_hbm))
+    ]
+    load_upstream = pltpu.make_async_copy(upstream_hbm, upstream_ref, load.at[3])
     half = owned // 2
     load_rows = []
     for h in range(2):
@@ -163,24 +169,21 @@
                 pltpu.make_async_copy(
                     moved_hbm.at[:, k * share : (k + 1) * share, columns],
                     rows.at[slot, :, :, columns],
-                    load.at[2 + 2 * h + k],
+                    load.at[4 + 2 * h + k],
                 )
             )
-    load_upstream = pltpu.make_async_copy(upstream_hbm, upstream_ref, load.at[6])
-    load_ids.start()
-    load_weights.start()
-    load_rows[0].start()
-    load_rows[1].start()
-    load_upstream.start()
-    load_rows[2].start()
-    load_rows[3].start()
-
+    for copy in [load_ids] + load_weights + load_rows[:2] + [load_upstream] + load_rows[2:]:
+        copy.start()
+
+    limit = size_ref[:1, :] - rank * owned
     load_ids.wait()
     lanes = lax.broadcasted_iota(jnp.int32, (8, BLOCK), 1).astype(jnp.bfloat16)
     orders = [jnp.bitwise_and(ids_ref[b : b + 1, :], BLOCK - 1) for b in range(per)]
     inverse = [dot(lanes, selector(order), NT).astype(jnp.int32) for order in orders]
-    load_weights.wait()
-    load_upstream.wait()
+    offset = jnp.broadcast_to(bias_ref[...], (BLOCK, bias_ref.shape[1])).T
+    for k in range(2):
+        load_weights[k].wait()
+        turned[k] = weights[k].T
 
     def rows_of(slot, columns):
         return rows[slot, :, :, columns].reshape(features, BLOCK)
@@ -188,15 +191,18 @@
     for h in range(2):
         load_rows[2 * h].wait()
         load_rows[2 * h + 1].wait()
+        if h == 0:
+            load_upstream.wait()
         for b in range(h * per // 2, (h + 1) * per // 2):
             columns = slice(b * BLOCK, (b + 1) * BLOCK)
-            own = move_lanes(dot(weights[0], rows_of(own_slot, columns)), orders[b])
-            pre = own + dot(weights[1], rows_of(agg_slot, columns)) + bias_ref[...]
+            own = move_lanes(dot(turned[0], rows_of(own_slot, columns)), orders[b])
+            pre = own + dot(turned[1], rows_of(agg_slot, columns)) + offset
             active, back = gelu_and_slope(pre)
             positions = b * BLOCK + lax.broadcasted_iota(jnp.int32, (1, BLOCK), 1)
             valid = jnp.where(positions < limit, 1.0, 0.0)
             hidden_ref[:, columns] = (active * valid).astype(jnp.bfloat16)
-            slope = (upstream_ref[:, columns].astype(jnp.float32) * back * valid).astype(jnp.bfloat16)
+            upstream = upstream_ref[columns, :].astype(jnp.float32).T
+            slope = (upstream * back * valid).astype(jnp.bfloat16)
             slopes[agg_slot, :, columns] = slope
             slopes[own_slot, :, columns] = move_lanes(slope.astype(jnp.float32), inverse[b]).astype(jnp.bfloat16)
     leave_hidden = pltpu.make_async_copy(hidden_ref, hidden_hbm, leave.at[0])
@@ -221,11 +227,11 @@
     leave_keep.wait()
 
 
-def finish(place, bias, ids, moved, weights, upstream):
+def finish(size, bias, ids, moved, w_self, w_neigh, upstream):
     owners, share, owned = moved.shape[0], moved.shape[1] // 2, moved.shape[2]
-    hidden = weights.shape[1]
+    features, hidden = w_self.shape
     part = (owners, share, hidden)
-    anywhere = pl.BlockSpec(memory_space=pl.ANY)
+    vmem, anywhere = pl.BlockSpec(memory_space=pltpu.VMEM), pl.BlockSpec(memory_space=pl.ANY)
     outs = [
         jax.ShapeDtypeStruct((hidden, owned), jnp.bfloat16),
         jax.ShapeDtypeStruct(part, jnp.float32),
@@ -233,47 +239,43 @@
     ]
     return pl.pallas_call(
         finish_kernel,
-        in_specs=[pl.BlockSpec(memory_space=pltpu.SMEM), pl.BlockSpec(memory_space=pltpu.VMEM)] + [anywhere] * 4,
+        in_specs=[vmem, vmem] + [anywhere] * 5,
         out_specs=[anywhere] * 3,
         out_shape=outs,
         scratch_shapes=[
             pltpu.VMEM((owned // BLOCK, BLOCK), jnp.int32),
             pltpu.VMEM((2, owners, share, owned), jnp.bfloat16),
-            pltpu.VMEM(weights.shape, jnp.bfloat16),
+            pltpu.VMEM((2, features, hidden), jnp.bfloat16),
+            pltpu.VMEM((2, hidden, features), jnp.bfloat16),
             pltpu.VMEM(upstream.shape, jnp.bfloat16),
             pltpu.VMEM((2, hidden, owned), jnp.bfloat16),
         ]
         + [pltpu.VMEM(a.shape, a.dtype) for a in outs]
-        + [pltpu.SemaphoreType.DMA((7,)), pltpu.SemaphoreType.DMA((3,))],
+        + [pltpu.SemaphoreType.DMA((8,)), pltpu.SemaphoreType.DMA((3,))],
         compiler_params=pltpu.CompilerParams(vmem_limit_bytes=WHOLE),
         cost_estimate=pl.CostEstimate(flops=2_000_000_000, bytes_accessed=9 * MIB, transcendentals=262144),
         name="finish",
-    )(place, bias, ids, moved, weights, upstream)
+    )(size, bias, ids, moved, w_self, w_neigh, upstream)
 
 
 def on_device(
     node_table, node_ids, block_lists, block_counts, tiles, batch_sizes, w_self, w_neigh, bias, cotangent
 ):
     owners = lax.axis_size(FEAT)
-    rank, core = lax.axis_index(FEAT), lax.axis_index("core")
+    core = lax.axis_index("core")
     table = jnp.swapaxes(node_table[0], 0, 1)
-    width = table.shape[0]
     ids = node_ids[0].reshape(-1, BLOCK)
-    owned = cotangent.shape[1]
 
     lists = jnp.transpose(block_lists, (2, 0, 1))
-    place = jnp.stack([core, rank, batch_sizes[0] - rank * owned])
-    weights = jnp.stack([w_self.T, w_neigh.T])
-
-    rows = outgoing(lists, block_counts, ids, table, tiles[0], owners)
+    rows, size = outgoing(batch_sizes, lists, block_counts, ids, table, tiles[0], owners)
     moved = lax.all_to_all(rows, FEAT, split_axis=0, concat_axis=0, tiled=True)
-    hidden, keep, send = finish(place, bias[:, None], ids, moved, weights, cotangent[0].T)
+    hidden, keep, send = finish(size, bias[None], ids, moved, w_self, w_neigh, cotangent[0])
 
     got = lax.ppermute(send, "core", [(0, 1), (1, 0)])
     parts = lax.all_to_all((keep + got).astype(jnp.bfloat16), FEAT, split_axis=0, concat_axis=0, tiled=True)
     total = jnp.sum(parts, axis=0, dtype=jnp.float32)
-    others = [lax.ppermute(total, "x", [(i, i ^ k) for i in range(4)]) for k in (1, 2, 3)]
-    total = (total + others[0]) + (others[1] + others[2])
+    others = [lax.ppermute(total, "x", [(i, (i + k) % 4) for i in range(4)]) for k in (3, 1, 2)]
+    total = (total + others[2]) + (others[0] + others[1])
     other = lax.ppermute(total, "core", [(0, 1), (1, 0)])
     first_core = core == 0
     return (

time: 126 us -> 112 us (0.89)
  waiting for transfers between devices: 64.3 us -> 5.04 us
  blocking collectives: 14.8 us -> 71.9 us
  starting transfers between devices: 17.5 us -> 9.62 us
  local copies, waits for them, and re-layouts: 3.23 us -> 1.01 us
  other arithmetic: 3.86 us -> 2.12 us
    all_to_all x0 -> x1, blocking collectives: none -> 58.5 us  [on_device(): moved = lax.all_to_all(rows, FEAT, split_axis=0, concat_axis=0, tiled=True)]
    all_to_all x1 -> x0, waiting for transfers between devices: 57.7 us -> none  [on_device(): moved = lax.all_to_all(rows, FEAT, split_axis=0, concat_axis=0, tiled=True)]
    all_to_all x1 -> x0, starting transfers between devices: 8.8 us -> none  [on_device(): moved = lax.all_to_all(rows, FEAT, split_axis=0, concat_axis=0, tiled=True)]
    another operation x2 -> x0, other arithmetic: 1.75 us -> none  [the longest x1 1.15 us: on_device(): weights = jnp.stack([w_self.T, w_neigh.T])]
    ppermute x3, waiting for transfers between devices: 4.86 us -> 3.29 us  [on_device(): lax.ppermute(total, 'x', [(i, (i + k) % 4) for i in range(4)])]
    unnamed x14 -> x3, local copies, waits for them, and re-layouts: 2.44 us -> 1.01 us
    all_to_all x1, blocking collectives: 14.8 us -> 13.4 us  [on_device(): lax.all_to_all((keep + got).astype(jnp.bfloat16), FEAT, split_axis=0, con...]
  transfers between devices with their start and end apart: 6 -> 5, of which waited for: 4 -> 2; matrix products, arithmetic and copies ran while one was open for 4% -> 1% of each run, Pallas kernels for 0% -> 0%
where the time goes in v9:
time: 112 us
  blocking collectives  71.9 us (64%)
  Pallas kernels  20.8 us (19%)
  starting transfers between devices  9.62 us (9%)
  waiting for transfers between devices  5.04 us (4%)
  other arithmetic  2.12 us (2%)
  between operations  1.32 us (1%)
    all_to_all x1, blocking collectives, on_device(): moved = lax.all_to_all(rows, FEAT, split_axis=0, concat_axis=0, tiled=True)  58.5 us
    all_to_all x1, blocking collectives, on_device(): lax.all_to_all((keep + got).astype(jnp.bfloat16), FEAT, split_axis=0, con...  13.4 us
    pallas_call x1, Pallas kernels, outgoing(): pl.pallas_call(outgoing_kernel, in_specs=[smem, smem, smem, vmem, anywher...  12.1 us
    pallas_call x1, Pallas kernels, finish(): pl.pallas_call(finish_kernel, in_specs=[vmem, vmem] + [anywhere] * 5, out...  8.67 us
    ppermute x3, starting transfers between devices, on_device(): lax.ppermute(total, 'x', [(i, (i + k) % 4) for i in range(4)])  4.28 us
    ppermute x3, waiting for transfers between devices, on_device(): lax.ppermute(total, 'x', [(i, (i + k) % 4) for i in range(4)])  3.29 us
    ppermute x1, starting transfers between devices, on_device(): other = lax.ppermute(total, 'core', [(0, 1), (1, 0)])  3.28 us
  transfers between devices with their start and end apart: 5, of which 2 were waited for; matrix products, arithmetic and copies ran while one was open for 1% of the time, Pallas kernels for 0%

profile of v9, /device:TPU:1, one launch (start us, length us, event | category | flops | bytes accessed | tf_op | source)
XLA Modules:
  0.0 111.8 jit_solution(6480772436038105123)
XLA Ops:
  1.3 12.1 %pick_and_aggregate.1 = (bf16[16,128,1024]{2,1,0:T(8,128)(2,1)}, s32[8,128]{1,0:T(8,128)}) custom-call(s32[1]{0:T(128)S(6)} %copy.14.batch_ref, s32[3,1,128]{2,1,0:T(1,128)} %bitcast.16, s32[1,128]{1,0:T(1,128)} %counts_ref.1, s32[256,128]{1,0:T(8,128)} %bitcast.14, bf16[64,32768]{1,0:T(8,128)(2,1)} %bitcast.12, bf16[128,3,128,128]{3,2,1,0:T(8,128)(2,1)} %bitcast.11), custom_call_target="tpu_custom_call" | custom-call | flops 4000000000 | bytes 20971520 | tf_op jit(solution)/shard_map/pick_and_aggregate/pallas_call | solution.py:113
  13.4 58.5 %all_to_all.10.moved_hbm = bf16[16,128,1024]{2,1,0:T(8,128)(2,1)} all-to-all(bf16[16,128,1024]{2,1,0:T(8,128)(2,1)} %get-tuple-element.9), channel_id=1, replica_groups=mesh['z'=4,'y'=4,'x'=4,'core'=2] {'z','y'}, dimensions={0} | all-to-all | bytes 8388608 | tf_op jit(solution)/shard_map/all_to_all | solution.py:271
  71.9 8.7 %finish.1 = (bf16[256,1024]{1,0:T(8,128)(2,1)}, f32[16,64,256]{2,1,0:T(8,128)}, bf16[16,64,256]{2,1,0:T(8,128)(2,1)}) custom-call(s32[8,128]{1,0:T(8,128)} %get-tuple-element.8.size_ref, f32[1,256]{1,0:T(1,128)} %bitcast.18, s32[256,128]{1,0:T(8,128)} %bitcast.15, bf16[16,128,1024]{2,1,0:T(8,128)(2,1)} %all_to_all.10.moved_hbm, bf16[1024,256]{1,0:T(8,128)(2,1)} %self_hbm.1, ...), custom_call_target="tpu_custom_call" | custom-call | flops 2000000000 | bytes 9437184 | tf_op jit(solution)/shard_map/finish/pallas_call | solution.py:240
  80.6 0.0 copy-start
  80.6 2.1 %collective-permute-start = (bf16[16,64,256]{2,1,0:T(8,128)(2,1)}, bf16[16,64,256]{2,1,0:T(8,128)(2,1)S(1)}, u32[]{:S(2)}, u32[]{:S(2)}) collective-permute-start(bf16[16,64,256]{2,1,0:T(8,128)(2,1)} %get-tuple-element.12), channel_id=1, source_target_pairs={{0,1},{1,0},{2,3},{3,2},{4,5},{5,4},{6,7},{7,6},{8,9},{9,8},{10,11... | collective-permute-start | bytes 1572872 | tf_op jit(solution)/shard_map/ppermute | solution.py:274
  82.7 1.7 %collective-permute-done = bf16[16,64,256]{2,1,0:T(8,128)(2,1)S(1)} collective-permute-done((bf16[16,64,256]{2,1,0:T(8,128)(2,1)}, bf16[16,64,256]{2,1,0:T(8,128)(2,1)S(1)}, u32[]{:S(2)}, u32[]{:S(2)}) %collective-permute-start) | collective-permute-done | bytes 524320 | tf_op jit(solution)/shard_map/ppermute | solution.py:274
  84.4 1.4 %add_convert_fusion = bf16[16,64,256]{2,1,0:T(8,128)(2,1)S(1)} fusion(f32[16,64,256]{2,1,0:T(8,128)} %get-tuple-element.11, bf16[16,64,256]{2,1,0:T(8,128)(2,1)S(1)} %collective-permute-done), kind=kLoop, calls=%fused_computation.1 | loop fusion | flops 786432 | bytes 2097152 | tf_op jit(solution)/shard_map/convert_element_type | solution.py:275
  85.8 13.4 %all_to_all.11 = bf16[16,64,256]{2,1,0:T(8,128)(2,1)S(1)} all-to-all(bf16[16,64,256]{2,1,0:T(8,128)(2,1)S(1)} %add_convert_fusion), channel_id=1, replica_groups=mesh['z'=4,'y'=4,'x'=4,'core'=2] {'z','y'}, dimensions={0} | all-to-all | bytes 1048576 | tf_op jit(solution)/shard_map/all_to_all | solution.py:275
  99.2 0.1 convert_reduce_fusion
  99.2 2.5 %collective-permute-start.2 = (f32[64,256]{1,0:T(8,128)S(1)}, f32[64,256]{1,0:T(8,128)S(1)}, u32[]{:S(2)}, u32[]{:S(2)}) collective-permute-start(f32[64,256]{1,0:T(8,128)S(1)} %convert_reduce_fusion), channel_id=1, source_target_pairs={{0,6},{2,0},{4,2},{6,4},{1,7},{3,1},{5,3},{7,5},{8,14},{10,8},{12,... | collective-permute-start | bytes 196616 | tf_op jit(solution)/shard_map/ppermute | solution.py:277
  101.8 0.0 collective-permute-start.3
  101.8 1.7 %collective-permute-start.1 = (f32[64,256]{1,0:T(8,128)S(1)}, f32[64,256]{1,0:T(8,128)S(1)}, u32[]{:S(2)}, u32[]{:S(2)}) collective-permute-start(f32[64,256]{1,0:T(8,128)S(1)} %convert_reduce_fusion), channel_id=1, source_target_pairs={{0,4},{2,6},{4,0},{6,2},{1,5},{3,7},{5,1},{7,3},{8,12},{10,14},{12... | collective-permute-start | bytes 196616 | tf_op jit(solution)/shard_map/ppermute | solution.py:277
  103.5 0.0 collective-permute-done.2
  103.5 3.3 %collective-permute-done.3 = f32[64,256]{1,0:T(8,128)S(1)} collective-permute-done((f32[64,256]{1,0:T(8,128)S(1)}, f32[64,256]{1,0:T(8,128)S(1)}, u32[]{:S(2)}, u32[]{:S(2)}) %collective-permute-start.3) | collective-permute-done | bytes 65568 | tf_op jit(solution)/shard_map/ppermute | solution.py:277
  106.8 0.0 collective-permute-done.1
  106.8 3.3 %collective-permute-start.4 = (f32[64,256]{1,0:T(8,128)S(1)}, f32[64,256]{1,0:T(8,128)S(1)}, u32[]{:S(2)}, u32[]{:S(2)}) collective-permute-start(f32[64,256]{1,0:T(8,128)S(1)} %add_add_fusion), channel_id=1, source_target_pairs={{0,1},{1,0},{2,3},{3,2},{4,5},{5,4},{6,7},{7,6},{8,9},{9,8},{10,11... | collective-permute-start | bytes 196616 | tf_op jit(solution)/shard_map/ppermute | solution.py:279
  110.1 0.0 copy-done
  110.1 1.0 copy.13
  111.1 0.0 collective-permute-done.4
  111.1 0.7 broadcast_select_fusion
  (1 shorter events, 0.0 us)
Async XLA Ops:
  80.6 29.5 %copy-start = (bf16[256,1024]{1,0:T(8,128)(2,1)S(1)}, bf16[256,1024]{1,0:T(8,128)(2,1)}, u32[]{:S(2)}) copy-start(bf16[256,1024]{1,0:T(8,128)(2,1)} %get-tuple-element.10) | copy-start | bytes 1572868
  80.6 3.8 %collective-permute-start = (bf16[16,64,256]{2,1,0:T(8,128)(2,1)}, bf16[16,64,256]{2,1,0:T(8,128)(2,1)S(1)}, u32[]{:S(2)}, u32[]{:S(2)}) collective-permute-start(bf16[16,64,256]{2,1,0:T(8,128)(2,1)} %get-tuple-element.12), channel_id=1, source_target_pairs={{0,1},{1,0},{2,3},{3,2},{4,5},{5,4},{6,7},{7,6},{8,9},{9,8},{10,11... | collective-permute-start | bytes 1572872 | tf_op jit(solution)/shard_map/ppermute | solution.py:274
  99.2 4.3 %collective-permute-start.2 = (f32[64,256]{1,0:T(8,128)S(1)}, f32[64,256]{1,0:T(8,128)S(1)}, u32[]{:S(2)}, u32[]{:S(2)}) collective-permute-start(f32[64,256]{1,0:T(8,128)S(1)} %convert_reduce_fusion), channel_id=1, source_target_pairs={{0,6},{2,0},{4,2},{6,4},{1,7},{3,1},{5,3},{7,5},{8,14},{10,8},{12,... | collective-permute-start | bytes 196616 | tf_op jit(solution)/shard_map/ppermute | solution.py:277
  101.8 5.0 %collective-permute-start.3 = (f32[64,256]{1,0:T(8,128)S(1)}, f32[64,256]{1,0:T(8,128)S(1)}, u32[]{:S(2)}, u32[]{:S(2)}) collective-permute-start(f32[64,256]{1,0:T(8,128)S(1)} %convert_reduce_fusion), channel_id=1, source_target_pairs={{0,2},{2,4},{4,6},{6,0},{1,3},{3,5},{5,7},{7,1},{8,10},{10,12},{12... | collective-permute-start | bytes 196616 | tf_op jit(solution)/shard_map/ppermute | solution.py:277
  101.8 5.0 %collective-permute-start.1 = (f32[64,256]{1,0:T(8,128)S(1)}, f32[64,256]{1,0:T(8,128)S(1)}, u32[]{:S(2)}, u32[]{:S(2)}) collective-permute-start(f32[64,256]{1,0:T(8,128)S(1)} %convert_reduce_fusion), channel_id=1, source_target_pairs={{0,4},{2,6},{4,0},{6,2},{1,5},{3,7},{5,1},{7,3},{8,12},{10,14},{12... | collective-permute-start | bytes 196616 | tf_op jit(solution)/shard_map/ppermute | solution.py:277
  106.8 4.3 %collective-permute-start.4 = (f32[64,256]{1,0:T(8,128)S(1)}, f32[64,256]{1,0:T(8,128)S(1)}, u32[]{:S(2)}, u32[]{:S(2)}) collective-permute-start(f32[64,256]{1,0:T(8,128)S(1)} %add_add_fusion), channel_id=1, source_target_pairs={{0,1},{1,0},{2,3},{3,2},{4,5},{5,4},{6,7},{7,6},{8,9},{9,8},{10,11... | collective-permute-start | bytes 196616 | tf_op jit(solution)/shard_map/ppermute | solution.py:279

commit v10 on v9

--- a/solution.py
+++ b/solution.py
@@ -146,113 +146,69 @@
 
 
 def finish_kernel(
-    size_ref, bias_ref, ids_hbm, moved_hbm, self_hbm, neigh_hbm, upstream_hbm, hidden_hbm, keep_hbm, send_hbm,
-    ids_ref, rows, weights, turned, upstream_ref, slopes, hidden_ref, keep_ref, send_ref, load, leave,
+    size_ref, bias_ref, ids_ref, moved_ref, self_ref, neigh_ref, upstream_ref, hidden_ref, keep_ref, send_ref,
+    turned, slopes,
 ):
-    owners, share, owned = rows.shape[1:]
+    owners, share, hidden = keep_ref.shape
+    owned = moved_ref.shape[2]
     features = owners * share
     per = owned // BLOCK
     rank, core = lax.axis_index(FEAT), lax.axis_index("core")
-    own_slot, agg_slot = core, 1 - core
-
-    load_ids = pltpu.make_async_copy(ids_hbm.at[pl.ds(pl.multiple_of(rank * per, per), per)], ids_ref, load.at[0])
-    load_weights = [
-        pltpu.make_async_copy(source, weights.at[k], load.at[1 + k]) for k, source in enumerate((self_hbm, neigh_hbm))
-    ]
-    load_upstream = pltpu.make_async_copy(upstream_hbm, upstream_ref, load.at[3])
-    half = owned // 2
-    load_rows = []
-    for h in range(2):
-        columns = slice(h * half, (h + 1) * half)
-        for k, slot in enumerate((own_slot, agg_slot)):
-            load_rows.append(
-                pltpu.make_async_copy(
-                    moved_hbm.at[:, k * share : (k + 1) * share, columns],
-                    rows.at[slot, :, :, columns],
-                    load.at[4 + 2 * h + k],
-                )
-            )
-    for copy in [load_ids] + load_weights + load_rows[:2] + [load_upstream] + load_rows[2:]:
-        copy.start()
-
     limit = size_ref[:1, :] - rank * owned
-    load_ids.wait()
+
     lanes = lax.broadcasted_iota(jnp.int32, (8, BLOCK), 1).astype(jnp.bfloat16)
-    orders = [jnp.bitwise_and(ids_ref[b : b + 1, :], BLOCK - 1) for b in range(per)]
+    mine = ids_ref[pl.ds(pl.multiple_of(rank * per, per), per), :]
+    orders = [jnp.bitwise_and(mine[b : b + 1, :], BLOCK - 1) for b in range(per)]
     inverse = [dot(lanes, selector(order), NT).astype(jnp.int32) for order in orders]
-    offset = jnp.broadcast_to(bias_ref[...], (BLOCK, bias_ref.shape[1])).T
-    for k in range(2):
-        load_weights[k].wait()
-        turned[k] = weights[k].T
-
-    def rows_of(slot, columns):
-        return rows[slot, :, :, columns].reshape(features, BLOCK)
-
-    for h in range(2):
-        load_rows[2 * h].wait()
-        load_rows[2 * h + 1].wait()
-        if h == 0:
-            load_upstream.wait()
-        for b in range(h * per // 2, (h + 1) * per // 2):
-            columns = slice(b * BLOCK, (b + 1) * BLOCK)
-            own = move_lanes(dot(turned[0], rows_of(own_slot, columns)), orders[b])
-            pre = own + dot(turned[1], rows_of(agg_slot, columns)) + offset
-            active, back = gelu_and_slope(pre)
-            positions = b * BLOCK + lax.broadcasted_iota(jnp.int32, (1, BLOCK), 1)
-            valid = jnp.where(positions < limit, 1.0, 0.0)
-            hidden_ref[:, columns] = (active * valid).astype(jnp.bfloat16)
-            upstream = upstream_ref[columns, :].astype(jnp.float32).T
-            slope = (upstream * back * valid).astype(jnp.bfloat16)
-            slopes[agg_slot, :, columns] = slope
-            slopes[own_slot, :, columns] = move_lanes(slope.astype(jnp.float32), inverse[b]).astype(jnp.bfloat16)
-    leave_hidden = pltpu.make_async_copy(hidden_ref, hidden_hbm, leave.at[0])
-    leave_hidden.start()
+    offset = jnp.broadcast_to(bias_ref[...], (BLOCK, hidden)).T
+    turned[0] = self_ref[...].T
+    turned[1] = neigh_ref[...].T
+
+    for b in range(per):
+        columns = slice(b * BLOCK, (b + 1) * BLOCK)
+        own = dot(turned[0], moved_ref[:, :share, columns].reshape(features, BLOCK))
+        pre = move_lanes(own, orders[b]) + offset
+        pre = pre + dot(turned[1], moved_ref[:, share:, columns].reshape(features, BLOCK))
+        active, back = gelu_and_slope(pre)
+        positions = b * BLOCK + lax.broadcasted_iota(jnp.int32, (1, BLOCK), 1)
+        valid = jnp.where(positions < limit, 1.0, 0.0)
+        hidden_ref[:, columns] = (active * valid).astype(jnp.bfloat16)
+        upstream = upstream_ref[columns, :].astype(jnp.float32).T
+        slope = (upstream * back * valid).astype(jnp.bfloat16)
+        slopes[1, :, columns] = slope
+        slopes[0, :, columns] = move_lanes(slope.astype(jnp.float32), inverse[b]).astype(jnp.bfloat16)
 
     group = 4
 
-    def grads(slot, out_ref):
+    def grads(k, out_ref):
+        start = pl.multiple_of(k * share, share)
         for i in range(0, owners, group):
-            left = rows[slot, i : i + group].reshape(group * share, owned)
-            total = dot(left, slopes[slot], NT)
-            out_ref[i : i + group] = total.reshape(group, share, -1).astype(out_ref.dtype)
-
-    grads(1, send_ref)
-    leave_send = pltpu.make_async_copy(send_ref, send_hbm, leave.at[1])
-    leave_send.start()
-    grads(0, keep_ref)
-    leave_keep = pltpu.make_async_copy(keep_ref, keep_hbm, leave.at[2])
-    leave_keep.start()
-    leave_hidden.wait()
-    leave_send.wait()
-    leave_keep.wait()
+            left = moved_ref[i : i + group, pl.ds(start, share), :].reshape(group * share, owned)
+            out_ref[i : i + group] = dot(left, slopes[k], NT).reshape(group, share, hidden).astype(out_ref.dtype)
+
+    grads(1 - core, send_ref)
+    grads(core, keep_ref)
 
 
 def finish(size, bias, ids, moved, w_self, w_neigh, upstream):
     owners, share, owned = moved.shape[0], moved.shape[1] // 2, moved.shape[2]
     features, hidden = w_self.shape
     part = (owners, share, hidden)
-    vmem, anywhere = pl.BlockSpec(memory_space=pltpu.VMEM), pl.BlockSpec(memory_space=pl.ANY)
-    outs = [
-        jax.ShapeDtypeStruct((hidden, owned), jnp.bfloat16),
-        jax.ShapeDtypeStruct(part, jnp.float32),
-        jax.ShapeDtypeStruct(part, jnp.bfloat16),
-    ]
+    vmem = pl.BlockSpec(memory_space=pltpu.VMEM)
     return pl.pallas_call(
         finish_kernel,
-        in_specs=[vmem, vmem] + [anywhere] * 5,
-        out_specs=[anywhere] * 3,
-        out_shape=outs,
+        in_specs=[vmem] * 7,
+        out_specs=[vmem] * 3,
+        out_shape=[
+            jax.ShapeDtypeStruct((hidden, owned), jnp.bfloat16),
+            jax.ShapeDtypeStruct(part, jnp.float32),
+            jax.ShapeDtypeStruct(part, jnp.bfloat16),
+        ],
         scratch_shapes=[
-            pltpu.VMEM((owned // BLOCK, BLOCK), jnp.int32),
-            pltpu.VMEM((2, owners, share, owned), jnp.bfloat16),
-            pltpu.VMEM((2, features, hidden), jnp.bfloat16),
             pltpu.VMEM((2, hidden, features), jnp.bfloat16),
-            pltpu.VMEM(upstream.shape, jnp.bfloat16),
             pltpu.VMEM((2, hidden, owned), jnp.bfloat16),
-        ]
-        + [pltpu.VMEM(a.shape, a.dtype) for a in outs]
-        + [pltpu.SemaphoreType.DMA((8,)), pltpu.SemaphoreType.DMA((3,))],
-        compiler_params=pltpu.CompilerParams(vmem_limit_bytes=WHOLE),
+        ],
+        compiler_params=pltpu.CompilerParams(vmem_limit_bytes=24 * MIB),
         cost_estimate=pl.CostEstimate(flops=2_000_000_000, bytes_accessed=9 * MIB, transcendentals=262144),
         name="finish",
     )(size, bias, ids, moved, w_self, w_neigh, upstream)

time: 112 us -> 106 us (0.946)
  Pallas kernels: 20.8 us -> 16.5 us
  other arithmetic: 2.12 us -> 0.89 us
    pallas_call x1, Pallas kernels: 8.67 us -> 4.4 us  [finish(): pl.pallas_call(finish_kernel, in_specs=[vmem] * 7, out_specs=[vmem] * 3,...]
    convert_element_type x1, other arithmetic: 1.36 us -> 0.14 us  [on_device(): (keep + got).astype(jnp.bfloat16)]
where the time goes in v10:
time: 106 us
  blocking collectives  71.9 us (68%)
  Pallas kernels  16.5 us (16%)
  starting transfers between devices  9.62 us (9%)
  waiting for transfers between devices  4.83 us (5%)
  between operations  1.39 us (1%)
    all_to_all x1, blocking collectives, on_device(): moved = lax.all_to_all(rows, FEAT, split_axis=0, concat_axis=0, tiled=True)  58.6 us
    all_to_all x1, blocking collectives, on_device(): lax.all_to_all((keep + got).astype(jnp.bfloat16), FEAT, split_axis=0, con...  13.4 us
    pallas_call x1, Pallas kernels, outgoing(): pl.pallas_call(outgoing_kernel, in_specs=[smem, smem, smem, vmem, anywher...  12.1 us
    pallas_call x1, Pallas kernels, finish(): pl.pallas_call(finish_kernel, in_specs=[vmem] * 7, out_specs=[vmem] * 3,...  4.4 us
    ppermute x3, starting transfers between devices, on_device(): lax.ppermute(total, 'x', [(i, (i + k) % 4) for i in range(4)])  4.29 us
    ppermute x3, waiting for transfers between devices, on_device(): lax.ppermute(total, 'x', [(i, (i + k) % 4) for i in range(4)])  3.29 us
    ppermute x1, starting transfers between devices, on_device(): other = lax.ppermute(total, 'core', [(0, 1), (1, 0)])  3.28 us
  transfers between devices with their start and end apart: 5, of which 2 were waited for; matrix products, arithmetic and copies ran while one was open for 1% of the time, Pallas kernels for 0%

profile of v10, /device:TPU:1, one launch (start us, length us, event | category | flops | bytes accessed | tf_op | source)
XLA Modules:
  0.0 106.2 jit_solution(1460315937305617459)
XLA Ops:
  1.3 12.1 %pick_and_aggregate.1 = (bf16[16,128,1024]{2,1,0:T(8,128)(2,1)}, s32[8,128]{1,0:T(8,128)}) custom-call(s32[1]{0:T(128)S(6)} %copy.14.batch_ref, s32[3,1,128]{2,1,0:T(1,128)} %bitcast.18, s32[1,128]{1,0:T(1,128)} %counts_ref.1, s32[256,128]{1,0:T(8,128)} %bitcast.12, bf16[64,32768]{1,0:T(8,128)(2,1)} %bitcast.17, bf16[128,3,128,128]{3,2,1,0:T(8,128)(2,1)} %bitcast.16), custom_call_target="tpu_custom_call" | custom-call | flops 4000000000 | bytes 20971520 | tf_op jit(solution)/shard_map/pick_and_aggregate/pallas_call | solution.py:113
  13.4 0.0 copy-start
  13.4 0.0 copy-start.1
  13.4 0.0 copy-start.2
  13.4 0.0 copy-start.3
  13.4 0.0 copy-start.4
  13.4 0.0 copy-start.5
  13.4 58.6 %all_to_all.10.moved_ref = bf16[16,128,1024]{2,1,0:T(8,128)(2,1)S(1)} all-to-all(bf16[16,128,1024]{2,1,0:T(8,128)(2,1)} %get-tuple-element.9), channel_id=1, replica_groups=mesh['z'=4,'y'=4,'x'=4,'core'=2] {'z','y'}, dimensions={0} | all-to-all | bytes 8388608 | tf_op jit(solution)/shard_map/all_to_all | solution.py:227
  72.0 4.4 %finish.1 = (bf16[256,1024]{1,0:T(8,128)(2,1)S(1)}, f32[16,64,256]{2,1,0:T(8,128)S(1)}, bf16[16,64,256]{2,1,0:T(8,128)(2,1)S(1)}) custom-call(s32[8,128]{1,0:T(8,128)S(1)} %copy-done.4, f32[1,256]{1,0:T(1,128)S(1)} %bitcast.15, s32[256,128]{1,0:T(8,128)S(1)} %bitcast.13, bf16[16,128,1024]{2,1,0:T(8,128)(2,1)S(1)} %all_to_all.10.moved_ref, ...), custom_call_target="tpu_custom_call" | custom-call | flops 2000000000 | bytes 9437184 | tf_op jit(solution)/shard_map/finish/pallas_call | solution.py:198
  76.5 2.0 %collective-permute-start = (bf16[16,64,256]{2,1,0:T(8,128)(2,1)S(1)}, bf16[16,64,256]{2,1,0:T(8,128)(2,1)S(1)}, u32[]{:S(2)}, u32[]{:S(2)}) collective-permute-start(bf16[16,64,256]{2,1,0:T(8,128)(2,1)S(1)} %get-tuple-element.12), channel_id=1, source_target_pairs={{0,1},{1,0},{2,3},{3,2},{4,5},{5,4},{6,7},{7,6},{8,9},{9,8},{10,11... | collective-permute-start | bytes 1572872 | tf_op jit(solution)/shard_map/ppermute | solution.py:230
  78.5 1.5 %collective-permute-done = bf16[16,64,256]{2,1,0:T(8,128)(2,1)S(1)} collective-permute-done((bf16[16,64,256]{2,1,0:T(8,128)(2,1)S(1)}, bf16[16,64,256]{2,1,0:T(8,128)(2,1)S(1)}, u32[]{:S(2)}, u32[]{:S(2)}) %collective-permute-start) | collective-permute-done | bytes 524320 | tf_op jit(solution)/shard_map/ppermute | solution.py:230
  80.0 0.1 add_convert_fusion
  80.2 13.4 %all_to_all.11 = bf16[16,64,256]{2,1,0:T(8,128)(2,1)S(1)} all-to-all(bf16[16,64,256]{2,1,0:T(8,128)(2,1)S(1)} %add_convert_fusion), channel_id=1, replica_groups=mesh['z'=4,'y'=4,'x'=4,'core'=2] {'z','y'}, dimensions={0} | all-to-all | bytes 1048576 | tf_op jit(solution)/shard_map/all_to_all | solution.py:231
  93.6 0.1 convert_reduce_fusion
  93.6 2.6 %collective-permute-start.2 = (f32[64,256]{1,0:T(8,128)S(1)}, f32[64,256]{1,0:T(8,128)S(1)}, u32[]{:S(2)}, u32[]{:S(2)}) collective-permute-start(f32[64,256]{1,0:T(8,128)S(1)} %convert_reduce_fusion), channel_id=1, source_target_pairs={{0,6},{2,0},{4,2},{6,4},{1,7},{3,1},{5,3},{7,5},{8,14},{10,8},{12,... | collective-permute-start | bytes 196616 | tf_op jit(solution)/shard_map/ppermute | solution.py:233
  96.2 0.0 collective-permute-start.3
  96.2 1.7 %collective-permute-start.1 = (f32[64,256]{1,0:T(8,128)S(1)}, f32[64,256]{1,0:T(8,128)S(1)}, u32[]{:S(2)}, u32[]{:S(2)}) collective-permute-start(f32[64,256]{1,0:T(8,128)S(1)} %convert_reduce_fusion), channel_id=1, source_target_pairs={{0,4},{2,6},{4,0},{6,2},{1,5},{3,7},{5,1},{7,3},{8,12},{10,14},{12... | collective-permute-start | bytes 196616 | tf_op jit(solution)/shard_map/ppermute | solution.py:233
  97.9 0.0 collective-permute-done.2
  97.9 3.3 %collective-permute-done.3 = f32[64,256]{1,0:T(8,128)S(1)} collective-permute-done((f32[64,256]{1,0:T(8,128)S(1)}, f32[64,256]{1,0:T(8,128)S(1)}, u32[]{:S(2)}, u32[]{:S(2)}) %collective-permute-start.3) | collective-permute-done | bytes 65568 | tf_op jit(solution)/shard_map/ppermute | solution.py:233
  101.2 0.0 collective-permute-done.1
  101.2 3.3 %collective-permute-start.4 = (f32[64,256]{1,0:T(8,128)S(1)}, f32[64,256]{1,0:T(8,128)S(1)}, u32[]{:S(2)}, u32[]{:S(2)}) collective-permute-start(f32[64,256]{1,0:T(8,128)S(1)} %add_add_fusion), channel_id=1, source_target_pairs={{0,1},{1,0},{2,3},{3,2},{4,5},{5,4},{6,7},{7,6},{8,9},{9,8},{10,11... | collective-permute-start | bytes 196616 | tf_op jit(solution)/shard_map/ppermute | solution.py:235
  104.5 1.0 copy.13
  105.5 0.0 collective-permute-done.4
  105.5 0.7 broadcast_select_fusion
  (7 shorter events, 0.0 us)
Async XLA Ops:
  13.4 58.6 %copy-start = (s32[1,32768]{1,0:T(1,128)S(1)}, s32[1,32768]{1,0:T(1,128)}, u32[]{:S(2)}) copy-start(s32[1,32768]{1,0:T(1,128)} %param.11) | copy-start | bytes 393220
  13.4 58.6 %copy-start.1 = (bf16[1024,256]{1,0:T(8,128)(2,1)S(1)}, bf16[1024,256]{1,0:T(8,128)(2,1)}, u32[]{:S(2)}) copy-start(bf16[1024,256]{1,0:T(8,128)(2,1)} %self_ref.1) | copy-start | bytes 1572868
  13.4 58.6 %copy-start.2 = (bf16[1024,256]{1,0:T(8,128)(2,1)S(1)}, bf16[1024,256]{1,0:T(8,128)(2,1)}, u32[]{:S(2)}) copy-start(bf16[1024,256]{1,0:T(8,128)(2,1)} %neigh_ref.1) | copy-start | bytes 1572868
  13.4 58.6 %copy-start.3 = (bf16[1,1024,256]{2,1,0:T(8,128)(2,1)S(1)}, bf16[1,1024,256]{2,1,0:T(8,128)(2,1)}, u32[]{:S(2)}) copy-start(bf16[1,1024,256]{2,1,0:T(8,128)(2,1)} %param.19) | copy-start | bytes 1572868
  13.4 58.6 %copy-start.4 = (s32[8,128]{1,0:T(8,128)S(1)}, s32[8,128]{1,0:T(8,128)}, u32[]{:S(2)}) copy-start(s32[8,128]{1,0:T(8,128)} %get-tuple-element.8.size_ref) | copy-start | bytes 12292
  13.4 58.6 %copy-start.5 = (f32[256]{0:T(256)S(1)}, f32[256]{0:T(256)}, u32[]{:S(2)}) copy-start(f32[256]{0:T(256)} %param.18) | copy-start | bytes 3076
  76.5 3.6 %collective-permute-start = (bf16[16,64,256]{2,1,0:T(8,128)(2,1)S(1)}, bf16[16,64,256]{2,1,0:T(8,128)(2,1)S(1)}, u32[]{:S(2)}, u32[]{:S(2)}) collective-permute-start(bf16[16,64,256]{2,1,0:T(8,128)(2,1)S(1)} %get-tuple-element.12), channel_id=1, source_target_pairs={{0,1},{1,0},{2,3},{3,2},{4,5},{5,4},{6,7},{7,6},{8,9},{9,8},{10,11... | collective-permute-start | bytes 1572872 | tf_op jit(solution)/shard_map/ppermute | solution.py:230
  93.6 4.3 %collective-permute-start.2 = (f32[64,256]{1,0:T(8,128)S(1)}, f32[64,256]{1,0:T(8,128)S(1)}, u32[]{:S(2)}, u32[]{:S(2)}) collective-permute-start(f32[64,256]{1,0:T(8,128)S(1)} %convert_reduce_fusion), channel_id=1, source_target_pairs={{0,6},{2,0},{4,2},{6,4},{1,7},{3,1},{5,3},{7,5},{8,14},{10,8},{12,... | collective-permute-start | bytes 196616 | tf_op jit(solution)/shard_map/ppermute | solution.py:233
  96.2 5.0 %collective-permute-start.3 = (f32[64,256]{1,0:T(8,128)S(1)}, f32[64,256]{1,0:T(8,128)S(1)}, u32[]{:S(2)}, u32[]{:S(2)}) collective-permute-start(f32[64,256]{1,0:T(8,128)S(1)} %convert_reduce_fusion), channel_id=1, source_target_pairs={{0,2},{2,4},{4,6},{6,0},{1,3},{3,5},{5,7},{7,1},{8,10},{10,12},{12... | collective-permute-start | bytes 196616 | tf_op jit(solution)/shard_map/ppermute | solution.py:233
  96.2 5.0 %collective-permute-start.1 = (f32[64,256]{1,0:T(8,128)S(1)}, f32[64,256]{1,0:T(8,128)S(1)}, u32[]{:S(2)}, u32[]{:S(2)}) collective-permute-start(f32[64,256]{1,0:T(8,128)S(1)} %convert_reduce_fusion), channel_id=1, source_target_pairs={{0,4},{2,6},{4,0},{6,2},{1,5},{3,7},{5,1},{7,3},{8,12},{10,14},{12... | collective-permute-start | bytes 196616 | tf_op jit(solution)/shard_map/ppermute | solution.py:233
  101.2 4.3 %collective-permute-start.4 = (f32[64,256]{1,0:T(8,128)S(1)}, f32[64,256]{1,0:T(8,128)S(1)}, u32[]{:S(2)}, u32[]{:S(2)}) collective-permute-start(f32[64,256]{1,0:T(8,128)S(1)} %add_add_fusion), channel_id=1, source_target_pairs={{0,1},{1,0},{2,3},{3,2},{4,5},{5,4},{6,7},{7,6},{8,9},{9,8},{10,11... | collective-permute-start | bytes 196616 | tf_op jit(solution)/shard_map/ppermute | solution.py:235

commit v11 on v10

--- a/solution.py
+++ b/solution.py
@@ -81,7 +81,7 @@
             ones = jnp.full((16, BLOCK), jnp.where(used, 1.0, 0.0), jnp.float32).astype(jnp.bfloat16)
             left.append(jnp.concatenate([source, ones], axis=0))
         right = jnp.concatenate([tiles[d, s] for s in range(slots)], axis=1)
-        total = dot(jnp.concatenate(left, axis=1), right, NT)
+        total = dot(right, jnp.concatenate(left, axis=1), NT).T
         return (total[:width] * (1.0 / total[width : width + 1])).astype(jnp.bfloat16)
 
     def some(i, carry):
@@ -145,11 +145,20 @@
     return jnp.concatenate(moved, axis=0)
 
 
+def grads(k, moved_ref, slope, out_ref):
+    owners, share, hidden = out_ref.shape
+    start = pl.multiple_of(k * share, share)
+    group = 4
+    for i in range(0, owners, group):
+        left = moved_ref[i : i + group, pl.ds(start, share), :].reshape(group * share, -1)
+        out_ref[i : i + group] = dot(left, slope, NT).reshape(group, share, hidden).astype(out_ref.dtype)
+
+
 def finish_kernel(
-    size_ref, bias_ref, ids_ref, moved_ref, self_ref, neigh_ref, upstream_ref, hidden_ref, keep_ref, send_ref,
+    size_ref, bias_ref, ids_ref, moved_ref, self_ref, neigh_ref, upstream_ref, hidden_ref, slope_ref, send_ref,
     turned, slopes,
 ):
-    owners, share, hidden = keep_ref.shape
+    owners, share, hidden = send_ref.shape
     owned = moved_ref.shape[2]
     features = owners * share
     per = owned // BLOCK
@@ -178,16 +187,12 @@
         slopes[1, :, columns] = slope
         slopes[0, :, columns] = move_lanes(slope.astype(jnp.float32), inverse[b]).astype(jnp.bfloat16)
 
-    group = 4
-
-    def grads(k, out_ref):
-        start = pl.multiple_of(k * share, share)
-        for i in range(0, owners, group):
-            left = moved_ref[i : i + group, pl.ds(start, share), :].reshape(group * share, owned)
-            out_ref[i : i + group] = dot(left, slopes[k], NT).reshape(group, share, hidden).astype(out_ref.dtype)
-
-    grads(1 - core, send_ref)
-    grads(core, keep_ref)
+    grads(1 - core, moved_ref, slopes[1 - core], send_ref)
+    slope_ref[...] = slopes[core]
+
+
+def keep_kernel(moved_ref, slope_ref, keep_ref):
+    grads(lax.axis_index("core"), moved_ref, slope_ref[...], keep_ref)
 
 
 def finish(size, bias, ids, moved, w_self, w_neigh, upstream):
@@ -201,7 +206,7 @@
         out_specs=[vmem] * 3,
         out_shape=[
             jax.ShapeDtypeStruct((hidden, owned), jnp.bfloat16),
-            jax.ShapeDtypeStruct(part, jnp.float32),
+            jax.ShapeDtypeStruct((hidden, owned), jnp.bfloat16),
             jax.ShapeDtypeStruct(part, jnp.bfloat16),
         ],
         scratch_shapes=[
@@ -214,6 +219,20 @@
     )(size, bias, ids, moved, w_self, w_neigh, upstream)
 
 
+def keep_part(moved, slope):
+    vmem = pl.BlockSpec(memory_space=pltpu.VMEM)
+    part = (moved.shape[0], moved.shape[1] // 2, slope.shape[0])
+    return pl.pallas_call(
+        keep_kernel,
+        in_specs=[vmem] * 2,
+        out_specs=vmem,
+        out_shape=jax.ShapeDtypeStruct(part, jnp.float32),
+        compiler_params=pltpu.CompilerParams(vmem_limit_bytes=24 * MIB),
+        cost_estimate=pl.CostEstimate(flops=1_000_000_000, bytes_accessed=4 * MIB, transcendentals=0),
+        name="kept_gradient",
+    )(moved, slope)
+
+
 def on_device(
     node_table, node_ids, block_lists, block_counts, tiles, batch_sizes, w_self, w_neigh, bias, cotangent
 ):
@@ -225,9 +244,10 @@
     lists = jnp.transpose(block_lists, (2, 0, 1))
     rows, size = outgoing(batch_sizes, lists, block_counts, ids, table, tiles[0], owners)
     moved = lax.all_to_all(rows, FEAT, split_axis=0, concat_axis=0, tiled=True)
-    hidden, keep, send = finish(size, bias[None], ids, moved, w_self, w_neigh, cotangent[0])
+    hidden, slope, send = finish(size, bias[None], ids, moved, w_self, w_neigh, cotangent[0])
 
     got = lax.ppermute(send, "core", [(0, 1), (1, 0)])
+    keep = keep_part(moved, slope)
     parts = lax.all_to_all((keep + got).astype(jnp.bfloat16), FEAT, split_axis=0, concat_axis=0, tiled=True)
     total = jnp.sum(parts, axis=0, dtype=jnp.float32)
     others = [lax.ppermute(total, "x", [(i, (i + k) % 4) for i in range(4)]) for k in (3, 1, 2)]

time: 106 us -> 106 us (level)
  transfers between devices with their start and end apart: 5 -> 5, of which waited for: 2 -> 2; matrix products, arithmetic and copies ran while one was open for 1% -> 1% of each run, Pallas kernels for 0% -> 1%
where the time goes in v11:
time: 106 us; the launch traced here: 105 us
  blocking collectives  72 us (68%)
  Pallas kernels  16.3 us (15%)
  starting transfers between devices  9.64 us (9%)
  waiting for transfers between devices  4.11 us (4%)
  between operations  1.4 us (1%)
    all_to_all x1, blocking collectives, on_device(): moved = lax.all_to_all(rows, FEAT, split_axis=0, concat_axis=0, tiled=True)  58.6 us
    all_to_all x1, blocking collectives, on_device(): lax.all_to_all((keep + got).astype(jnp.bfloat16), FEAT, split_axis=0, con...  13.4 us
    pallas_call x1, Pallas kernels, outgoing(): pl.pallas_call(outgoing_kernel, in_specs=[smem, smem, smem, vmem, anywher...  11.6 us
    ppermute x3, starting transfers between devices, on_device(): lax.ppermute(total, 'x', [(i, (i + k) % 4) for i in range(4)])  4.27 us
    pallas_call x1, Pallas kernels, finish(): pl.pallas_call(finish_kernel, in_specs=[vmem] * 7, out_specs=[vmem] * 3,...  3.97 us
    ppermute x3, waiting for transfers between devices, on_device(): lax.ppermute(total, 'x', [(i, (i + k) % 4) for i in range(4)])  3.31 us
    ppermute x1, starting transfers between devices, on_device(): other = lax.ppermute(total, 'core', [(0, 1), (1, 0)])  3.28 us
  transfers between devices with their start and end apart: 5, of which 2 were waited for; matrix products, arithmetic and copies ran while one was open for 1% of the time, Pallas kernels for 1%

profile of v11, /device:TPU:1, one launch (start us, length us, event | category | flops | bytes accessed | tf_op | source)
XLA Modules:
  0.0 105.3 jit_solution(311487442629906764)
XLA Ops:
  1.3 11.6 %pick_and_aggregate.1 = (bf16[16,128,1024]{2,1,0:T(8,128)(2,1)}, s32[8,128]{1,0:T(8,128)}) custom-call(s32[1]{0:T(128)S(6)} %copy.14.batch_ref, s32[3,1,128]{2,1,0:T(1,128)} %bitcast.18, s32[1,128]{1,0:T(1,128)} %counts_ref.1, s32[256,128]{1,0:T(8,128)} %bitcast.12, bf16[64,32768]{1,0:T(8,128)(2,1)} %bitcast.17, bf16[128,3,128,128]{3,2,1,0:T(8,128)(2,1)} %bitcast.16), custom_call_target="tpu_custom_call" | custom-call | flops 4000000000 | bytes 20971520 | tf_op jit(solution)/shard_map/pick_and_aggregate/pallas_call | solution.py:113
  12.8 0.0 copy-start
  12.9 0.0 copy-start.1
  12.9 0.0 copy-start.2
  12.9 0.0 copy-start.3
  12.9 0.0 copy-start.4
  12.9 0.0 copy-start.5
  12.9 58.6 %all_to_all.10.moved_ref = bf16[16,128,1024]{2,1,0:T(8,128)(2,1)S(1)} all-to-all(bf16[16,128,1024]{2,1,0:T(8,128)(2,1)} %get-tuple-element.9), channel_id=1, replica_groups=mesh['z'=4,'y'=4,'x'=4,'core'=2] {'z','y'}, dimensions={0} | all-to-all | bytes 8388608 | tf_op jit(solution)/shard_map/all_to_all | solution.py:246
  71.5 4.0 %finish.1 = (bf16[256,1024]{1,0:T(8,128)(2,1)S(1)}, bf16[256,1024]{1,0:T(8,128)(2,1)S(1)}, bf16[16,64,256]{2,1,0:T(8,128)(2,1)S(1)}) custom-call(s32[8,128]{1,0:T(8,128)S(1)} %copy-done.4, f32[1,256]{1,0:T(1,128)S(1)} %bitcast.15, s32[256,128]{1,0:T(8,128)S(1)} %bitcast.13, bf16[16,128,1024]{2,1,0:T(8,128)(2,1)S(1)} %all_to_all.10.moved_ref, ...), custom_call_target="tpu_custom_call" | custom-call | flops 2000000000 | bytes 9437184 | tf_op jit(solution)/shard_map/finish/pallas_call | solution.py:203
  75.5 2.1 %collective-permute-start = (bf16[16,64,256]{2,1,0:T(8,128)(2,1)S(1)}, bf16[16,64,256]{2,1,0:T(8,128)(2,1)S(1)}, u32[]{:S(2)}, u32[]{:S(2)}) collective-permute-start(bf16[16,64,256]{2,1,0:T(8,128)(2,1)S(1)} %get-tuple-element.12), channel_id=1, source_target_pairs={{0,1},{1,0},{2,3},{3,2},{4,5},{5,4},{6,7},{7,6},{8,9},{9,8},{10,11... | collective-permute-start | bytes 1572872 | tf_op jit(solution)/shard_map/ppermute | solution.py:249
  77.6 0.7 kept_gradient.1
  78.4 0.8 collective-permute-done
  79.1 0.1 add_convert_fusion
  79.3 13.4 %all_to_all.11 = bf16[16,64,256]{2,1,0:T(8,128)(2,1)S(1)} all-to-all(bf16[16,64,256]{2,1,0:T(8,128)(2,1)S(1)} %add_convert_fusion), channel_id=1, replica_groups=mesh['z'=4,'y'=4,'x'=4,'core'=2] {'z','y'}, dimensions={0} | all-to-all | bytes 1048576 | tf_op jit(solution)/shard_map/all_to_all | solution.py:251
  92.7 0.1 convert_reduce_fusion
  92.8 2.5 %collective-permute-start.2 = (f32[64,256]{1,0:T(8,128)S(1)}, f32[64,256]{1,0:T(8,128)S(1)}, u32[]{:S(2)}, u32[]{:S(2)}) collective-permute-start(f32[64,256]{1,0:T(8,128)S(1)} %convert_reduce_fusion), channel_id=1, source_target_pairs={{0,6},{2,0},{4,2},{6,4},{1,7},{3,1},{5,3},{7,5},{8,14},{10,8},{12,... | collective-permute-start | bytes 196616 | tf_op jit(solution)/shard_map/ppermute | solution.py:253
  95.3 0.0 collective-permute-start.3
  95.3 1.7 %collective-permute-start.1 = (f32[64,256]{1,0:T(8,128)S(1)}, f32[64,256]{1,0:T(8,128)S(1)}, u32[]{:S(2)}, u32[]{:S(2)}) collective-permute-start(f32[64,256]{1,0:T(8,128)S(1)} %convert_reduce_fusion), channel_id=1, source_target_pairs={{0,4},{2,6},{4,0},{6,2},{1,5},{3,7},{5,1},{7,3},{8,12},{10,14},{12... | collective-permute-start | bytes 196616 | tf_op jit(solution)/shard_map/ppermute | solution.py:253
  97.0 0.0 collective-permute-done.2
  97.0 3.3 %collective-permute-done.3 = f32[64,256]{1,0:T(8,128)S(1)} collective-permute-done((f32[64,256]{1,0:T(8,128)S(1)}, f32[64,256]{1,0:T(8,128)S(1)}, u32[]{:S(2)}, u32[]{:S(2)}) %collective-permute-start.3) | collective-permute-done | bytes 65568 | tf_op jit(solution)/shard_map/ppermute | solution.py:253
  100.3 0.0 collective-permute-done.1
  100.4 3.3 %collective-permute-start.4 = (f32[64,256]{1,0:T(8,128)S(1)}, f32[64,256]{1,0:T(8,128)S(1)}, u32[]{:S(2)}, u32[]{:S(2)}) collective-permute-start(f32[64,256]{1,0:T(8,128)S(1)} %add_add_fusion), channel_id=1, source_target_pairs={{0,1},{1,0},{2,3},{3,2},{4,5},{5,4},{6,7},{7,6},{8,9},{9,8},{10,11... | collective-permute-start | bytes 196616 | tf_op jit(solution)/shard_map/ppermute | solution.py:255
  103.6 1.0 copy.13
  104.6 0.7 broadcast_select_fusion
  (8 shorter events, 0.0 us)
Async XLA Ops:
  12.8 58.7 %copy-start = (s32[1,32768]{1,0:T(1,128)S(1)}, s32[1,32768]{1,0:T(1,128)}, u32[]{:S(2)}) copy-start(s32[1,32768]{1,0:T(1,128)} %param.11) | copy-start | bytes 393220
  12.9 58.6 %copy-start.1 = (bf16[1024,256]{1,0:T(8,128)(2,1)S(1)}, bf16[1024,256]{1,0:T(8,128)(2,1)}, u32[]{:S(2)}) copy-start(bf16[1024,256]{1,0:T(8,128)(2,1)} %self_ref.1) | copy-start | bytes 1572868
  12.9 58.6 %copy-start.2 = (bf16[1024,256]{1,0:T(8,128)(2,1)S(1)}, bf16[1024,256]{1,0:T(8,128)(2,1)}, u32[]{:S(2)}) copy-start(bf16[1024,256]{1,0:T(8,128)(2,1)} %neigh_ref.1) | copy-start | bytes 1572868
  12.9 58.6 %copy-start.3 = (bf16[1,1024,256]{2,1,0:T(8,128)(2,1)S(1)}, bf16[1,1024,256]{2,1,0:T(8,128)(2,1)}, u32[]{:S(2)}) copy-start(bf16[1,1024,256]{2,1,0:T(8,128)(2,1)} %param.19) | copy-start | bytes 1572868
  12.9 58.6 %copy-start.4 = (s32[8,128]{1,0:T(8,128)S(1)}, s32[8,128]{1,0:T(8,128)}, u32[]{:S(2)}) copy-start(s32[8,128]{1,0:T(8,128)} %get-tuple-element.8.size_ref) | copy-start | bytes 12292
  12.9 58.6 %copy-start.5 = (f32[256]{0:T(256)S(1)}, f32[256]{0:T(256)}, u32[]{:S(2)}) copy-start(f32[256]{0:T(256)} %param.18) | copy-start | bytes 3076
  75.5 3.6 %collective-permute-start = (bf16[16,64,256]{2,1,0:T(8,128)(2,1)S(1)}, bf16[16,64,256]{2,1,0:T(8,128)(2,1)S(1)}, u32[]{:S(2)}, u32[]{:S(2)}) collective-permute-start(bf16[16,64,256]{2,1,0:T(8,128)(2,1)S(1)} %get-tuple-element.12), channel_id=1, source_target_pairs={{0,1},{1,0},{2,3},{3,2},{4,5},{5,4},{6,7},{7,6},{8,9},{9,8},{10,11... | collective-permute-start | bytes 1572872 | tf_op jit(solution)/shard_map/ppermute | solution.py:249
  92.8 4.3 %collective-permute-start.2 = (f32[64,256]{1,0:T(8,128)S(1)}, f32[64,256]{1,0:T(8,128)S(1)}, u32[]{:S(2)}, u32[]{:S(2)}) collective-permute-start(f32[64,256]{1,0:T(8,128)S(1)} %convert_reduce_fusion), channel_id=1, source_target_pairs={{0,6},{2,0},{4,2},{6,4},{1,7},{3,1},{5,3},{7,5},{8,14},{10,8},{12,... | collective-permute-start | bytes 196616 | tf_op jit(solution)/shard_map/ppermute | solution.py:253
  95.3 5.0 %collective-permute-start.3 = (f32[64,256]{1,0:T(8,128)S(1)}, f32[64,256]{1,0:T(8,128)S(1)}, u32[]{:S(2)}, u32[]{:S(2)}) collective-permute-start(f32[64,256]{1,0:T(8,128)S(1)} %convert_reduce_fusion), channel_id=1, source_target_pairs={{0,2},{2,4},{4,6},{6,0},{1,3},{3,5},{5,7},{7,1},{8,10},{10,12},{12... | collective-permute-start | bytes 196616 | tf_op jit(solution)/shard_map/ppermute | solution.py:253
  95.3 5.0 %collective-permute-start.1 = (f32[64,256]{1,0:T(8,128)S(1)}, f32[64,256]{1,0:T(8,128)S(1)}, u32[]{:S(2)}, u32[]{:S(2)}) collective-permute-start(f32[64,256]{1,0:T(8,128)S(1)} %convert_reduce_fusion), channel_id=1, source_target_pairs={{0,4},{2,6},{4,0},{6,2},{1,5},{3,7},{5,1},{7,3},{8,12},{10,14},{12... | collective-permute-start | bytes 196616 | tf_op jit(solution)/shard_map/ppermute | solution.py:253
  100.4 4.3 %collective-permute-start.4 = (f32[64,256]{1,0:T(8,128)S(1)}, f32[64,256]{1,0:T(8,128)S(1)}, u32[]{:S(2)}, u32[]{:S(2)}) collective-permute-start(f32[64,256]{1,0:T(8,128)S(1)} %add_add_fusion), channel_id=1, source_target_pairs={{0,1},{1,0},{2,3},{3,2},{4,5},{5,4},{6,7},{7,6},{8,9},{9,8},{10,11... | collective-permute-start | bytes 196616 | tf_op jit(solution)/shard_map/ppermute | solution.py:255

commit v12 on v11

--- a/solution.py
+++ b/solution.py
@@ -45,7 +45,7 @@
 
 
 def outgoing_kernel(
-    batch_ref, lists_ref, counts_ref, ids_ref, table_hbm, tiles_hbm, out_hbm, size_ref, rows, table, tiles, vector, which, load, leave
+    batch_ref, lists_ref, counts_ref, ids_ref, table_hbm, tiles_hbm, out_hbm, size_hbm, rows, size_ref, table, tiles, vector, which, load, leave
 ):
     blocks = ids_ref.shape[0]
     owners, width, owned = rows.shape
@@ -64,6 +64,8 @@
     for r in range(together):
         load_tiles(r).start()
     size_ref[...] = jnp.full(size_ref.shape, batch_ref[0], jnp.int32)
+    leave_size = pltpu.make_async_copy(size_ref, size_hbm, leave.at[owners])
+    leave_size.start()
     table[:, table_hbm.shape[1] :] = jnp.zeros((width, BLOCK), table.dtype)
     read_blocks(ids_ref, vector, which, load.at[owners])
     load_table.wait()
@@ -102,6 +104,7 @@
     lax.fori_loop(0, dst_blocks // per // together, some, 0)
     for r in range(owners):
         pltpu.make_async_copy(rows.at[r], out_hbm.at[r], leave.at[r]).wait()
+    leave_size.wait()
 
 
 def outgoing(batch, lists, counts, ids, table, tiles, owners):
@@ -113,16 +116,17 @@
     return pl.pallas_call(
         outgoing_kernel,
         in_specs=[smem, smem, smem, vmem, anywhere, anywhere],
-        out_specs=[anywhere, vmem],
+        out_specs=[anywhere, anywhere],
         out_shape=[jax.ShapeDtypeStruct(out, jnp.bfloat16), jax.ShapeDtypeStruct((8, BLOCK), jnp.int32)],
         scratch_shapes=[
             pltpu.VMEM(out, jnp.bfloat16),
+            pltpu.VMEM((8, BLOCK), jnp.int32),
             pltpu.VMEM((width, rows + BLOCK), jnp.bfloat16),
             pltpu.VMEM(tiles.shape, jnp.bfloat16),
             pltpu.VMEM((8, blocks), jnp.int32),
             pltpu.SMEM((8, blocks), jnp.int32),
             pltpu.SemaphoreType.DMA((owners + 2,)),
-            pltpu.SemaphoreType.DMA((owners,)),
+            pltpu.SemaphoreType.DMA((owners + 1,)),
         ],
         compiler_params=pltpu.CompilerParams(vmem_limit_bytes=WHOLE),
         cost_estimate=pl.CostEstimate(flops=4_000_000_000, bytes_accessed=20 * MIB, transcendentals=0),

time: 106 us -> 105 us (level)
  no operation moved by 1% of the time
where the time goes in v12:
time: 105 us
  blocking collectives  72 us (69%)
  Pallas kernels  15.8 us (15%)
  starting transfers between devices  9.61 us (9%)
  waiting for transfers between devices  4.06 us (4%)
  between operations  1.4 us (1%)
    all_to_all x1, blocking collectives, on_device(): moved = lax.all_to_all(rows, FEAT, split_axis=0, concat_axis=0, tiled=True)  58.6 us
    all_to_all x1, blocking collectives, on_device(): lax.all_to_all((keep + got).astype(jnp.bfloat16), FEAT, split_axis=0, con...  13.4 us
    pallas_call x1, Pallas kernels, outgoing(): pl.pallas_call(outgoing_kernel, in_specs=[smem, smem, smem, vmem, anywher...  11.1 us
    ppermute x3, starting transfers between devices, on_device(): lax.ppermute(total, 'x', [(i, (i + k) % 4) for i in range(4)])  4.29 us
    pallas_call x1, Pallas kernels, finish(): pl.pallas_call(finish_kernel, in_specs=[vmem] * 7, out_specs=[vmem] * 3,...  3.97 us
    ppermute x1, starting transfers between devices, on_device(): other = lax.ppermute(total, 'core', [(0, 1), (1, 0)])  3.28 us
    ppermute x3, waiting for transfers between devices, on_device(): lax.ppermute(total, 'x', [(i, (i + k) % 4) for i in range(4)])  3.26 us
  transfers between devices with their start and end apart: 5, of which 2 were waited for; matrix products, arithmetic and copies ran while one was open for 1% of the time, Pallas kernels for 1%

profile of v12, /device:TPU:1, one launch (start us, length us, event | category | flops | bytes accessed | tf_op | source)
XLA Modules:
  0.0 104.8 jit_solution(2019094639757012432)
XLA Ops:
  1.3 11.1 %pick_and_aggregate.1 = (bf16[16,128,1024]{2,1,0:T(8,128)(2,1)}, s32[8,128]{1,0:T(8,128)}) custom-call(s32[1]{0:T(128)S(6)} %copy.14.batch_ref, s32[3,1,128]{2,1,0:T(1,128)} %bitcast.18, s32[1,128]{1,0:T(1,128)} %counts_ref.1, s32[256,128]{1,0:T(8,128)} %bitcast.12, bf16[64,32768]{1,0:T(8,128)(2,1)} %bitcast.17, bf16[128,3,128,128]{3,2,1,0:T(8,128)(2,1)} %bitcast.16), custom_call_target="tpu_custom_call" | custom-call | flops 4000000000 | bytes 20971520 | tf_op jit(solution)/shard_map/pick_and_aggregate/pallas_call | solution.py:116
  12.4 0.0 copy-start
  12.4 0.0 copy-start.1
  12.4 0.0 copy-start.2
  12.4 0.0 copy-start.3
  12.4 0.0 copy-start.4
  12.5 0.0 copy-start.5
  12.5 58.6 %all_to_all.10.moved_ref = bf16[16,128,1024]{2,1,0:T(8,128)(2,1)S(1)} all-to-all(bf16[16,128,1024]{2,1,0:T(8,128)(2,1)} %get-tuple-element.9), channel_id=1, replica_groups=mesh['z'=4,'y'=4,'x'=4,'core'=2] {'z','y'}, dimensions={0} | all-to-all | bytes 8388608 | tf_op jit(solution)/shard_map/all_to_all | solution.py:250
  71.1 4.0 %finish.1 = (bf16[256,1024]{1,0:T(8,128)(2,1)S(1)}, bf16[256,1024]{1,0:T(8,128)(2,1)S(1)}, bf16[16,64,256]{2,1,0:T(8,128)(2,1)S(1)}) custom-call(s32[8,128]{1,0:T(8,128)S(1)} %copy-done.4, f32[1,256]{1,0:T(1,128)S(1)} %bitcast.15, s32[256,128]{1,0:T(8,128)S(1)} %bitcast.13, bf16[16,128,1024]{2,1,0:T(8,128)(2,1)S(1)} %all_to_all.10.moved_ref, ...), custom_call_target="tpu_custom_call" | custom-call | flops 2000000000 | bytes 9437184 | tf_op jit(solution)/shard_map/finish/pallas_call | solution.py:207
  75.1 2.0 %collective-permute-start = (bf16[16,64,256]{2,1,0:T(8,128)(2,1)S(1)}, bf16[16,64,256]{2,1,0:T(8,128)(2,1)S(1)}, u32[]{:S(2)}, u32[]{:S(2)}) collective-permute-start(bf16[16,64,256]{2,1,0:T(8,128)(2,1)S(1)} %get-tuple-element.12), channel_id=1, source_target_pairs={{0,1},{1,0},{2,3},{3,2},{4,5},{5,4},{6,7},{7,6},{8,9},{9,8},{10,11... | collective-permute-start | bytes 1572872 | tf_op jit(solution)/shard_map/ppermute | solution.py:253
  77.2 0.7 kept_gradient.1
  77.9 0.8 collective-permute-done
  78.7 0.1 add_convert_fusion
  78.8 13.4 %all_to_all.11 = bf16[16,64,256]{2,1,0:T(8,128)(2,1)S(1)} all-to-all(bf16[16,64,256]{2,1,0:T(8,128)(2,1)S(1)} %add_convert_fusion), channel_id=1, replica_groups=mesh['z'=4,'y'=4,'x'=4,'core'=2] {'z','y'}, dimensions={0} | all-to-all | bytes 1048576 | tf_op jit(solution)/shard_map/all_to_all | solution.py:255
  92.2 0.1 convert_reduce_fusion
  92.3 2.5 %collective-permute-start.2 = (f32[64,256]{1,0:T(8,128)S(1)}, f32[64,256]{1,0:T(8,128)S(1)}, u32[]{:S(2)}, u32[]{:S(2)}) collective-permute-start(f32[64,256]{1,0:T(8,128)S(1)} %convert_reduce_fusion), channel_id=1, source_target_pairs={{0,6},{2,0},{4,2},{6,4},{1,7},{3,1},{5,3},{7,5},{8,14},{10,8},{12,... | collective-permute-start | bytes 196616 | tf_op jit(solution)/shard_map/ppermute | solution.py:257
  94.8 0.0 collective-permute-start.3
  94.8 1.8 %collective-permute-start.1 = (f32[64,256]{1,0:T(8,128)S(1)}, f32[64,256]{1,0:T(8,128)S(1)}, u32[]{:S(2)}, u32[]{:S(2)}) collective-permute-start(f32[64,256]{1,0:T(8,128)S(1)} %convert_reduce_fusion), channel_id=1, source_target_pairs={{0,4},{2,6},{4,0},{6,2},{1,5},{3,7},{5,1},{7,3},{8,12},{10,14},{12... | collective-permute-start | bytes 196616 | tf_op jit(solution)/shard_map/ppermute | solution.py:257
  96.6 0.0 collective-permute-done.2
  96.6 3.3 %collective-permute-done.3 = f32[64,256]{1,0:T(8,128)S(1)} collective-permute-done((f32[64,256]{1,0:T(8,128)S(1)}, f32[64,256]{1,0:T(8,128)S(1)}, u32[]{:S(2)}, u32[]{:S(2)}) %collective-permute-start.3) | collective-permute-done | bytes 65568 | tf_op jit(solution)/shard_map/ppermute | solution.py:257
  99.9 0.0 collective-permute-done.1
  99.9 3.3 %collective-permute-start.4 = (f32[64,256]{1,0:T(8,128)S(1)}, f32[64,256]{1,0:T(8,128)S(1)}, u32[]{:S(2)}, u32[]{:S(2)}) collective-permute-start(f32[64,256]{1,0:T(8,128)S(1)} %add_add_fusion), channel_id=1, source_target_pairs={{0,1},{1,0},{2,3},{3,2},{4,5},{5,4},{6,7},{7,6},{8,9},{9,8},{10,11... | collective-permute-start | bytes 196616 | tf_op jit(solution)/shard_map/ppermute | solution.py:259
  103.2 1.0 copy.13
  104.2 0.7 broadcast_select_fusion
  (8 shorter events, 0.0 us)
Async XLA Ops:
  12.4 58.7 %copy-start = (s32[1,32768]{1,0:T(1,128)S(1)}, s32[1,32768]{1,0:T(1,128)}, u32[]{:S(2)}) copy-start(s32[1,32768]{1,0:T(1,128)} %param.11) | copy-start | bytes 393220
  12.4 58.7 %copy-start.1 = (bf16[1024,256]{1,0:T(8,128)(2,1)S(1)}, bf16[1024,256]{1,0:T(8,128)(2,1)}, u32[]{:S(2)}) copy-start(bf16[1024,256]{1,0:T(8,128)(2,1)} %self_ref.1) | copy-start | bytes 1572868
  12.4 58.7 %copy-start.2 = (bf16[1024,256]{1,0:T(8,128)(2,1)S(1)}, bf16[1024,256]{1,0:T(8,128)(2,1)}, u32[]{:S(2)}) copy-start(bf16[1024,256]{1,0:T(8,128)(2,1)} %neigh_ref.1) | copy-start | bytes 1572868
  12.4 58.7 %copy-start.3 = (bf16[1,1024,256]{2,1,0:T(8,128)(2,1)S(1)}, bf16[1,1024,256]{2,1,0:T(8,128)(2,1)}, u32[]{:S(2)}) copy-start(bf16[1,1024,256]{2,1,0:T(8,128)(2,1)} %param.19) | copy-start | bytes 1572868
  12.4 58.7 %copy-start.4 = (s32[8,128]{1,0:T(8,128)S(1)}, s32[8,128]{1,0:T(8,128)}, u32[]{:S(2)}) copy-start(s32[8,128]{1,0:T(8,128)} %get-tuple-element.8.size_ref) | copy-start | bytes 12292
  12.5 58.7 %copy-start.5 = (f32[256]{0:T(256)S(1)}, f32[256]{0:T(256)}, u32[]{:S(2)}) copy-start(f32[256]{0:T(256)} %param.18) | copy-start | bytes 3076
  75.1 3.6 %collective-permute-start = (bf16[16,64,256]{2,1,0:T(8,128)(2,1)S(1)}, bf16[16,64,256]{2,1,0:T(8,128)(2,1)S(1)}, u32[]{:S(2)}, u32[]{:S(2)}) collective-permute-start(bf16[16,64,256]{2,1,0:T(8,128)(2,1)S(1)} %get-tuple-element.12), channel_id=1, source_target_pairs={{0,1},{1,0},{2,3},{3,2},{4,5},{5,4},{6,7},{7,6},{8,9},{9,8},{10,11... | collective-permute-start | bytes 1572872 | tf_op jit(solution)/shard_map/ppermute | solution.py:253
  92.3 4.3 %collective-permute-start.2 = (f32[64,256]{1,0:T(8,128)S(1)}, f32[64,256]{1,0:T(8,128)S(1)}, u32[]{:S(2)}, u32[]{:S(2)}) collective-permute-start(f32[64,256]{1,0:T(8,128)S(1)} %convert_reduce_fusion), channel_id=1, source_target_pairs={{0,6},{2,0},{4,2},{6,4},{1,7},{3,1},{5,3},{7,5},{8,14},{10,8},{12,... | collective-permute-start | bytes 196616 | tf_op jit(solution)/shard_map/ppermute | solution.py:257
  94.8 5.0 %collective-permute-start.3 = (f32[64,256]{1,0:T(8,128)S(1)}, f32[64,256]{1,0:T(8,128)S(1)}, u32[]{:S(2)}, u32[]{:S(2)}) collective-permute-start(f32[64,256]{1,0:T(8,128)S(1)} %convert_reduce_fusion), channel_id=1, source_target_pairs={{0,2},{2,4},{4,6},{6,0},{1,3},{3,5},{5,7},{7,1},{8,10},{10,12},{12... | collective-permute-start | bytes 196616 | tf_op jit(solution)/shard_map/ppermute | solution.py:257
  94.8 5.0 %collective-permute-start.1 = (f32[64,256]{1,0:T(8,128)S(1)}, f32[64,256]{1,0:T(8,128)S(1)}, u32[]{:S(2)}, u32[]{:S(2)}) collective-permute-start(f32[64,256]{1,0:T(8,128)S(1)} %convert_reduce_fusion), channel_id=1, source_target_pairs={{0,4},{2,6},{4,0},{6,2},{1,5},{3,7},{5,1},{7,3},{8,12},{10,14},{12... | collective-permute-start | bytes 196616 | tf_op jit(solution)/shard_map/ppermute | solution.py:257
  99.9 4.3 %collective-permute-start.4 = (f32[64,256]{1,0:T(8,128)S(1)}, f32[64,256]{1,0:T(8,128)S(1)}, u32[]{:S(2)}, u32[]{:S(2)}) collective-permute-start(f32[64,256]{1,0:T(8,128)S(1)} %add_add_fusion), channel_id=1, source_target_pairs={{0,1},{1,0},{2,3},{3,2},{4,5},{5,4},{6,7},{7,6},{8,9},{9,8},{10,11... | collective-permute-start | bytes 196616 | tf_op jit(solution)/shard_map/ppermute | solution.py:259

commit v13 on v12

--- a/solution.py
+++ b/solution.py
@@ -195,7 +195,8 @@
     slope_ref[...] = slopes[core]
 
 
-def keep_kernel(moved_ref, slope_ref, keep_ref):
+def keep_kernel(moved_ref, slope_ref, hidden_ref, keep_ref, turned_ref):
+    turned_ref[...] = hidden_ref[...].T
     grads(lax.axis_index("core"), moved_ref, slope_ref[...], keep_ref)
 
 
@@ -223,18 +224,21 @@
     )(size, bias, ids, moved, w_self, w_neigh, upstream)
 
 
-def keep_part(moved, slope):
+def keep_part(moved, slope, hidden):
     vmem = pl.BlockSpec(memory_space=pltpu.VMEM)
     part = (moved.shape[0], moved.shape[1] // 2, slope.shape[0])
     return pl.pallas_call(
         keep_kernel,
-        in_specs=[vmem] * 2,
-        out_specs=vmem,
-        out_shape=jax.ShapeDtypeStruct(part, jnp.float32),
+        in_specs=[vmem] * 3,
+        out_specs=[vmem] * 2,
+        out_shape=[
+            jax.ShapeDtypeStruct(part, jnp.float32),
+            jax.ShapeDtypeStruct(hidden.shape[::-1], hidden.dtype),
+        ],
         compiler_params=pltpu.CompilerParams(vmem_limit_bytes=24 * MIB),
         cost_estimate=pl.CostEstimate(flops=1_000_000_000, bytes_accessed=4 * MIB, transcendentals=0),
         name="kept_gradient",
-    )(moved, slope)
+    )(moved, slope, hidden)
 
 
 def on_device(
@@ -251,7 +255,7 @@
     hidden, slope, send = finish(size, bias[None], ids, moved, w_self, w_neigh, cotangent[0])
 
     got = lax.ppermute(send, "core", [(0, 1), (1, 0)])
-    keep = keep_part(moved, slope)
+    keep, hidden = keep_part(moved, slope, hidden)
     parts = lax.all_to_all((keep + got).astype(jnp.bfloat16), FEAT, split_axis=0, concat_axis=0, tiled=True)
     total = jnp.sum(parts, axis=0, dtype=jnp.float32)
     others = [lax.ppermute(total, "x", [(i, (i + k) % 4) for i in range(4)]) for k in (3, 1, 2)]
@@ -259,7 +263,7 @@
     other = lax.ppermute(total, "core", [(0, 1), (1, 0)])
     first_core = core == 0
     return (
-        hidden.T[None],
+        hidden[None],
         jnp.where(first_core, total, other),
         jnp.where(first_core, other, total),
     )

time: 105 us -> 106 us (level)
  transfers between devices with their start and end apart: 5 -> 5, of which waited for: 2 -> 5; matrix products, arithmetic and copies ran while one was open for 1% -> 0% of each run, Pallas kernels for 1% -> 1%
where the time goes in v13:
time: 106 us
  blocking collectives  72 us (68%)
  Pallas kernels  16.7 us (16%)
  starting transfers between devices  9.92 us (9%)
  waiting for transfers between devices  4.68 us (4%)
  between operations  1.39 us (1%)
    all_to_all x1, blocking collectives, on_device(): moved = lax.all_to_all(rows, FEAT, split_axis=0, concat_axis=0, tiled=True)  58.6 us
    all_to_all x1, blocking collectives, on_device(): lax.all_to_all((keep + got).astype(jnp.bfloat16), FEAT, split_axis=0, con...  13.4 us
    pallas_call x1, Pallas kernels, outgoing(): pl.pallas_call(outgoing_kernel, in_specs=[smem, smem, smem, vmem, anywher...  11.1 us
    ppermute x3, starting transfers between devices, on_device(): lax.ppermute(total, 'x', [(i, (i + k) % 4) for i in range(4)])  4.31 us
    pallas_call x1, Pallas kernels, finish(): pl.pallas_call(finish_kernel, in_specs=[vmem] * 7, out_specs=[vmem] * 3,...  4.19 us
    ppermute x3, waiting for transfers between devices, on_device(): lax.ppermute(total, 'x', [(i, (i + k) % 4) for i in range(4)])  3.71 us
    ppermute x1, starting transfers between devices, on_device(): other = lax.ppermute(total, 'core', [(0, 1), (1, 0)])  3.56 us
  transfers between devices with their start and end apart: 5, of which 5 were waited for; matrix products, arithmetic and copies ran while one was open for 0% of the time, Pallas kernels for 1%

profile of v13, /device:TPU:1, one launch (start us, length us, event | category | flops | bytes accessed | tf_op | source)
XLA Modules:
  0.0 105.7 jit_solution(16264615843839187670)
XLA Ops:
  1.3 11.1 %pick_and_aggregate.1 = (bf16[16,128,1024]{2,1,0:T(8,128)(2,1)}, s32[8,128]{1,0:T(8,128)}) custom-call(s32[1]{0:T(128)S(6)} %copy.13.batch_ref, s32[3,1,128]{2,1,0:T(1,128)} %bitcast.15, s32[1,128]{1,0:T(1,128)} %counts_ref.1, s32[256,128]{1,0:T(8,128)} %bitcast.9, bf16[64,32768]{1,0:T(8,128)(2,1)} %bitcast.14, bf16[128,3,128,128]{3,2,1,0:T(8,128)(2,1)} %bitcast.13), custom_call_target="tpu_custom_call" | custom-call | flops 4000000000 | bytes 20971520 | tf_op jit(solution)/shard_map/pick_and_aggregate/pallas_call | solution.py:116
  12.4 0.0 copy-start
  12.4 0.0 copy-start.1
  12.4 0.0 copy-start.2
  12.4 0.0 copy-start.3
  12.4 0.0 copy-start.4
  12.4 0.0 copy-start.5
  12.4 58.6 %all_to_all.10.moved_ref = bf16[16,128,1024]{2,1,0:T(8,128)(2,1)S(1)} all-to-all(bf16[16,128,1024]{2,1,0:T(8,128)(2,1)} %get-tuple-element.10), channel_id=1, replica_groups=mesh['z'=4,'y'=4,'x'=4,'core'=2] {'z','y'}, dimensions={0} | all-to-all | bytes 8388608 | tf_op jit(solution)/shard_map/all_to_all | solution.py:254
  71.1 4.2 %finish.1 = (bf16[256,1024]{1,0:T(8,128)(2,1)S(1)}, bf16[256,1024]{1,0:T(8,128)(2,1)S(1)}, bf16[16,64,256]{2,1,0:T(8,128)(2,1)S(1)}) custom-call(s32[8,128]{1,0:T(8,128)S(1)} %copy-done.4, f32[1,256]{1,0:T(1,128)S(1)} %bitcast.12, s32[256,128]{1,0:T(8,128)S(1)} %bitcast.10, bf16[16,128,1024]{2,1,0:T(8,128)(2,1)S(1)} %all_to_all.10.moved_ref, ...), custom_call_target="tpu_custom_call" | custom-call | flops 2000000000 | bytes 9437184 | tf_op jit(solution)/shard_map/finish/pallas_call | solution.py:208
  75.3 2.0 %collective-permute-start = (bf16[16,64,256]{2,1,0:T(8,128)(2,1)S(1)}, bf16[16,64,256]{2,1,0:T(8,128)(2,1)S(1)}, u32[]{:S(2)}, u32[]{:S(2)}) collective-permute-start(bf16[16,64,256]{2,1,0:T(8,128)(2,1)S(1)} %get-tuple-element.16), channel_id=1, source_target_pairs={{0,1},{1,0},{2,3},{3,2},{4,5},{5,4},{6,7},{7,6},{8,9},{9,8},{10,11... | collective-permute-start | bytes 1572872 | tf_op jit(solution)/shard_map/ppermute | solution.py:257
  77.3 1.5 %kept_gradient.1 = (f32[16,64,256]{2,1,0:T(8,128)S(1)}, bf16[1024,256]{1,0:T(8,128)(2,1)}) custom-call(bf16[16,128,1024]{2,1,0:T(8,128)(2,1)S(1)} %all_to_all.10.moved_ref, bf16[256,1024]{1,0:T(8,128)(2,1)S(1)} %get-tuple-element.12.slope_ref, bf16[256,1024]{1,0:T(8,128)(2,1)S(1)} %get-tuple-element.13.hidden_ref), custom_call_target="tpu_custom_call" | custom-call | flops 1000000000 | bytes 4194304 | tf_op jit(solution)/shard_map/kept_gradient/pallas_call | solution.py:230
  78.8 0.1 collective-permute-done
  78.9 0.2 add_convert_fusion
  79.1 13.4 %all_to_all.11 = bf16[16,64,256]{2,1,0:T(8,128)(2,1)S(1)} all-to-all(bf16[16,64,256]{2,1,0:T(8,128)(2,1)S(1)} %add_convert_fusion), channel_id=1, replica_groups=mesh['z'=4,'y'=4,'x'=4,'core'=2] {'z','y'}, dimensions={0} | all-to-all | bytes 1048576 | tf_op jit(solution)/shard_map/all_to_all | solution.py:259
  92.5 0.1 convert_reduce_fusion
  92.5 2.8 %collective-permute-start.1 = (f32[64,256]{1,0:T(8,128)S(1)}, f32[64,256]{1,0:T(8,128)S(1)}, u32[]{:S(2)}, u32[]{:S(2)}) collective-permute-start(f32[64,256]{1,0:T(8,128)S(1)} %convert_reduce_fusion), channel_id=1, source_target_pairs={{0,4},{2,6},{4,0},{6,2},{1,5},{3,7},{5,1},{7,3},{8,12},{10,14},{12... | collective-permute-start | bytes 196616 | tf_op jit(solution)/shard_map/ppermute | solution.py:261
  95.4 0.9 collective-permute-start.2
  96.2 0.6 collective-permute-start.3
  96.8 0.4 collective-permute-done.1
  97.2 1.3 %collective-permute-done.2 = f32[64,256]{1,0:T(8,128)S(1)} collective-permute-done((f32[64,256]{1,0:T(8,128)S(1)}, f32[64,256]{1,0:T(8,128)S(1)}, u32[]{:S(2)}, u32[]{:S(2)}) %collective-permute-start.2) | collective-permute-done | bytes 65568 | tf_op jit(solution)/shard_map/ppermute | solution.py:261
  98.5 2.1 %collective-permute-done.3 = f32[64,256]{1,0:T(8,128)S(1)} collective-permute-done((f32[64,256]{1,0:T(8,128)S(1)}, f32[64,256]{1,0:T(8,128)S(1)}, u32[]{:S(2)}, u32[]{:S(2)}) %collective-permute-start.3) | collective-permute-done | bytes 65568 | tf_op jit(solution)/shard_map/ppermute | solution.py:261
  100.6 3.6 %collective-permute-start.4 = (f32[64,256]{1,0:T(8,128)S(1)}, f32[64,256]{1,0:T(8,128)S(1)}, u32[]{:S(2)}, u32[]{:S(2)}) collective-permute-start(f32[64,256]{1,0:T(8,128)S(1)} %add_add_fusion), channel_id=1, source_target_pairs={{0,1},{1,0},{2,3},{3,2},{4,5},{5,4},{6,7},{7,6},{8,9},{9,8},{10,11... | collective-permute-start | bytes 196616 | tf_op jit(solution)/shard_map/ppermute | solution.py:263
  104.1 0.9 collective-permute-done.4
  105.0 0.7 broadcast_select_fusion
  (7 shorter events, 0.0 us)
Async XLA Ops:
  12.4 58.7 %copy-start = (s32[1,32768]{1,0:T(1,128)S(1)}, s32[1,32768]{1,0:T(1,128)}, u32[]{:S(2)}) copy-start(s32[1,32768]{1,0:T(1,128)} %param.11) | copy-start | bytes 393220
  12.4 58.7 %copy-start.1 = (bf16[1024,256]{1,0:T(8,128)(2,1)S(1)}, bf16[1024,256]{1,0:T(8,128)(2,1)}, u32[]{:S(2)}) copy-start(bf16[1024,256]{1,0:T(8,128)(2,1)} %self_ref.1) | copy-start | bytes 1572868
  12.4 58.7 %copy-start.2 = (bf16[1024,256]{1,0:T(8,128)(2,1)S(1)}, bf16[1024,256]{1,0:T(8,128)(2,1)}, u32[]{:S(2)}) copy-start(bf16[1024,256]{1,0:T(8,128)(2,1)} %neigh_ref.1) | copy-start | bytes 1572868
  12.4 58.7 %copy-start.3 = (bf16[1,1024,256]{2,1,0:T(8,128)(2,1)S(1)}, bf16[1,1024,256]{2,1,0:T(8,128)(2,1)}, u32[]{:S(2)}) copy-start(bf16[1,1024,256]{2,1,0:T(8,128)(2,1)} %param.19) | copy-start | bytes 1572868
  12.4 58.7 %copy-start.4 = (s32[8,128]{1,0:T(8,128)S(1)}, s32[8,128]{1,0:T(8,128)}, u32[]{:S(2)}) copy-start(s32[8,128]{1,0:T(8,128)} %get-tuple-element.11.size_ref) | copy-start | bytes 12292
  12.4 58.6 %copy-start.5 = (f32[256]{0:T(256)S(1)}, f32[256]{0:T(256)}, u32[]{:S(2)}) copy-start(f32[256]{0:T(256)} %param.18) | copy-start | bytes 3076
  75.3 3.6 %collective-permute-start = (bf16[16,64,256]{2,1,0:T(8,128)(2,1)S(1)}, bf16[16,64,256]{2,1,0:T(8,128)(2,1)S(1)}, u32[]{:S(2)}, u32[]{:S(2)}) collective-permute-start(bf16[16,64,256]{2,1,0:T(8,128)(2,1)S(1)} %get-tuple-element.16), channel_id=1, source_target_pairs={{0,1},{1,0},{2,3},{3,2},{4,5},{5,4},{6,7},{7,6},{8,9},{9,8},{10,11... | collective-permute-start | bytes 1572872 | tf_op jit(solution)/shard_map/ppermute | solution.py:257
  92.5 4.7 %collective-permute-start.1 = (f32[64,256]{1,0:T(8,128)S(1)}, f32[64,256]{1,0:T(8,128)S(1)}, u32[]{:S(2)}, u32[]{:S(2)}) collective-permute-start(f32[64,256]{1,0:T(8,128)S(1)} %convert_reduce_fusion), channel_id=1, source_target_pairs={{0,4},{2,6},{4,0},{6,2},{1,5},{3,7},{5,1},{7,3},{8,12},{10,14},{12... | collective-permute-start | bytes 196616 | tf_op jit(solution)/shard_map/ppermute | solution.py:261
  95.4 3.1 %collective-permute-start.2 = (f32[64,256]{1,0:T(8,128)S(1)}, f32[64,256]{1,0:T(8,128)S(1)}, u32[]{:S(2)}, u32[]{:S(2)}) collective-permute-start(f32[64,256]{1,0:T(8,128)S(1)} %convert_reduce_fusion), channel_id=1, source_target_pairs={{0,6},{2,0},{4,2},{6,4},{1,7},{3,1},{5,3},{7,5},{8,14},{10,8},{12,... | collective-permute-start | bytes 196616 | tf_op jit(solution)/shard_map/ppermute | solution.py:261
  96.2 4.3 %collective-permute-start.3 = (f32[64,256]{1,0:T(8,128)S(1)}, f32[64,256]{1,0:T(8,128)S(1)}, u32[]{:S(2)}, u32[]{:S(2)}) collective-permute-start(f32[64,256]{1,0:T(8,128)S(1)} %convert_reduce_fusion), channel_id=1, source_target_pairs={{0,2},{2,4},{4,6},{6,0},{1,3},{3,5},{5,7},{7,1},{8,10},{10,12},{12... | collective-permute-start | bytes 196616 | tf_op jit(solution)/shard_map/ppermute | solution.py:261
  100.6 4.5 %collective-permute-start.4 = (f32[64,256]{1,0:T(8,128)S(1)}, f32[64,256]{1,0:T(8,128)S(1)}, u32[]{:S(2)}, u32[]{:S(2)}) collective-permute-start(f32[64,256]{1,0:T(8,128)S(1)} %add_add_fusion), channel_id=1, source_target_pairs={{0,1},{1,0},{2,3},{3,2},{4,5},{5,4},{6,7},{7,6},{8,9},{9,8},{10,11... | collective-permute-start | bytes 196616 | tf_op jit(solution)/shard_map/ppermute | solution.py:263
